TPU v7x, 32 devices: a whole 2x2x4 slice. The times are simulated.
32 devices in a mesh: seq: 8 (over z, x), wa: 4 (over y, core).
Axes of the slice: x: 2, y: 2, z: 4, core: 2. Of those that a mesh axis runs over, the one named last changes fastest.
Arguments:
- inputs: float32 [12288, 1024], P('seq'), may hold values from -6 to 6
- seq_starts: int32 [12288], P('seq'), may hold values from 0 to 1, as said below
- ln_gain: float32 [1024], replicated, may hold values from 0.5 to 1.5
- ln_bias: float32 [1024], replicated, may hold values from -1.8 to 1.8
- w_gate: float32 [1024, 3072], P(None, 'wa'), may hold values from -0.1875 to 0.1875
- b_gate: float32 [3072], P('wa'), may hold values from -1.8 to 1.8
- w_reduce: float32 [1024, 512], P(None, 'wa'), may hold values from -0.1875 to 0.1875
- b_reduce: float32 [512], P('wa'), may hold values from -1.8 to 1.8
- ssm_rate: float32 [512], P('wa'), may hold values from 2e-05 to 0.02
- ssm_step: float32 [512], P('wa'), may hold values from 0.5 to 2
- ssm_out: float32 [512], P('wa'), may hold values from 0.3 to 3
- w_expand: float32 [512, 3072], P(None, 'wa'), may hold values from -0.5 to 0.5
- b_expand: float32 [3072], P('wa'), may hold values from -1.8 to 1.8
- w_down: float32 [1024, 3072], P(None, 'wa'), may hold values from -0.4375 to 0.4375
- b_down: float32 [1024], replicated, may hold values from -1.8 to 1.8
- cotangent: float32 [12288, 1024], P('seq', 'wa'), may hold values from -6 to 6
Outputs:
- output: float32 [12288, 1024], P('seq', 'wa')
- grad_inputs: float32 [12288, 1024], P('seq')
- grad_ln_gain: float32 [1024], P('seq')
- grad_ln_bias: float32 [1024], P('seq')
- grad_w_gate: float32 [1024, 3072], P('seq', 'wa')
- grad_b_gate: float32 [3072], P(('wa', 'seq'))
- grad_w_reduce: float32 [1024, 512], P('seq', 'wa')
- grad_b_reduce: float32 [512], P(('wa', 'seq'))
- grad_ssm_rate: float32 [512], P(('wa', 'seq'))
- grad_ssm_step: float32 [512], P(('wa', 'seq'))
- grad_ssm_out: float32 [512], P(('wa', 'seq'))
- grad_w_expand: float32 [512, 3072], P('seq', 'wa')
- grad_b_expand: float32 [3072], P(('wa', 'seq'))
- grad_w_down: float32 [1024, 3072], P('seq', 'wa')
- grad_b_down: float32 [1024], P('seq')
Inputs may be any that keep to these rules, and one draw needn't show every extreme that they name: `seq_starts`: token 0 is a start; the sequences that the starts delimit hold 1024 to 4096 tokens, except the last, which may be shorter, and one holds exactly 4096.
All inputs are finite; a program needn't handle non-finite values.
Results may differ from a plain program's by a relative error of at most 0.0004.
Values sent between devices are 32-bit elements; how exact they have to be, the bound alone decides.
No kernel may reach another device: no remote copies, remote signals or barrier semaphores. Data moves between devices by JAX's collectives and lax.ppermute only.
A program may use at most 128 MiB of HBM per device.

v0:
```python
import math

import jax
import jax.numpy as jnp
from jax import lax
from jax.sharding import PartitionSpec as P

HIGHEST = lax.Precision.HIGHEST
EPSILON = 1e-05
ROOT_HALF = 0.7071067811865476
INV_ROOT_TAU = 0.3989422804014327


def prefix(part, axis, combine, identity, reverse):
    count = lax.axis_size(axis)
    place = lax.axis_index(axis)
    ahead = count - 1 - place if reverse else place
    gathered = jax.tree.map(lambda a: lax.all_gather(a, axis), part)
    state = jax.tree.map(lambda a, e: jnp.zeros_like(a) + jnp.asarray(e, a.dtype), part, identity)

    def one(hop, state):
        source = count - 1 - hop if reverse else hop
        return combine(
            state, jax.tree.map(lambda a: lax.dynamic_index_in_dim(a, source, 0, False), gathered)
        )

    return lax.fori_loop(0, ahead, one, state)


def gelu_parts(preact):
    normal_cdf = 0.5 * (1.0 + lax.erf(preact * ROOT_HALF))
    slope = normal_cdf + preact * INV_ROOT_TAU * jnp.exp(-0.5 * preact * preact)
    return (preact * normal_cdf, slope)


def combine(earlier, later):
    return (earlier[0] * later[0], later[1] + later[0] * earlier[1])


def contract_rows(left, right):
    return lax.dot_general(left, right, (((0,), (0,)), ((), ())), precision=HIGHEST)


def contract_cols(left, right):
    return lax.dot_general(left, right, (((1,), (1,)), ((), ())), precision=HIGHEST)


def local_scan(driven, counts, log_decay, count_in):
    row_count, channels = driven.shape
    block_len = math.gcd(row_count, 128)
    block_count = row_count // block_len
    offsets = jnp.arange(block_len, dtype=jnp.float32)
    distance = offsets[:, None] - offsets[None, :]
    causal = distance >= 0.0

    def advance(carry, blocks):
        carried, last_count = carry
        block_in, block_counts = blocks
        linked = causal & (block_counts[:, None] == block_counts[None, :])
        kernel = jnp.where(
            linked[:, :, None], jnp.exp(jnp.maximum(distance, 0.0)[:, :, None] * log_decay), 0.0
        )
        within = jnp.einsum("tsh,sh->th", kernel, block_in, precision=HIGHEST)
        lead_keep = jnp.where(
            (block_counts == last_count)[:, None],
            jnp.exp((offsets + 1.0)[:, None] * log_decay),
            0.0,
        )
        result = within + lead_keep * carried
        return ((result[-1], block_counts[-1]), result)

    start = (jnp.zeros((channels,), jnp.float32), count_in)
    (final, _), results = lax.scan(
        advance,
        start,
        (driven.reshape(block_count, block_len, channels), counts.reshape(block_count, block_len)),
    )
    return (results.reshape(row_count, channels), final)


def body(
    inputs,
    seq_starts,
    ln_gain,
    ln_bias,
    w_gate,
    b_gate,
    w_reduce,
    b_reduce,
    ssm_rate,
    ssm_step,
    ssm_out,
    w_expand,
    b_expand,
    w_down,
    b_down,
    cotangent,
):
    row_count = inputs.shape[0]
    part_width = cotangent.shape[1]
    wa_index = lax.axis_index("wa")
    row_mean = jnp.mean(inputs, axis=1, keepdims=True)
    centred = inputs - row_mean
    variance = jnp.mean(centred * centred, axis=1, keepdims=True)
    inv_std = lax.rsqrt(variance + EPSILON)
    standard = centred * inv_std
    normed = standard * ln_gain + ln_bias
    gate_act, gate_slope = gelu_parts(jnp.dot(normed, w_gate, precision=HIGHEST) + b_gate)
    reduced, reduce_slope = gelu_parts(jnp.dot(normed, w_reduce, precision=HIGHEST) + b_reduce)
    log_decay = -ssm_rate * ssm_step
    keep_rate = jnp.exp(log_decay)
    counts = jnp.cumsum(seq_starts)
    local_states, local_end = local_scan(
        reduced * (1.0 - keep_rate), counts, log_decay, jnp.zeros((), jnp.int32)
    )
    whole_keep = jnp.where(counts[-1] == 0, jnp.exp(float(row_count) * log_decay), 0.0)
    identity = (jnp.ones_like(keep_rate), jnp.zeros_like(keep_rate))
    _, entering = prefix((whole_keep, local_end), "seq", combine, identity, False)
    positions = jnp.arange(row_count, dtype=jnp.float32)[:, None]
    lead_keep = jnp.where((counts == 0)[:, None], jnp.exp((positions + 1.0) * log_decay), 0.0)
    states = local_states + lead_keep * entering
    mixed = states * ssm_out
    mixed_all = lax.all_gather(mixed, "wa", axis=1, tiled=True)
    expand = jnp.dot(mixed_all, w_expand, precision=HIGHEST) + b_expand
    product = gate_act * expand
    partial_out = contract_cols(product, w_down)
    own_inputs = lax.dynamic_slice_in_dim(inputs, wa_index * part_width, part_width, 1)
    own_bias = lax.dynamic_slice_in_dim(b_down, wa_index * part_width, part_width, 0)
    output = (
        lax.psum_scatter(partial_out, "wa", scatter_dimension=1, tiled=True) + own_inputs + own_bias
    )
    full_grad = lax.all_gather(cotangent, "wa", axis=1, tiled=True)
    grad_b_down = jnp.sum(full_grad, axis=0)
    grad_product = jnp.dot(full_grad, w_down, precision=HIGHEST)
    grad_w_down = contract_rows(full_grad, product)
    grad_gate = grad_product * expand
    grad_expand = grad_product * gate_act
    grad_b_expand = jnp.sum(grad_expand, axis=0)
    grad_w_expand = contract_rows(mixed_all, grad_expand)
    mixed_back = contract_cols(grad_expand, w_expand)
    grad_mixed = lax.psum_scatter(mixed_back, "wa", scatter_dimension=1, tiled=True)
    grad_ssm_out = jnp.sum(states * grad_mixed, axis=0)
    back_counts = counts[::-1]
    local_back, _ = local_scan((grad_mixed * ssm_out)[::-1], back_counts, log_decay, back_counts[0])
    local_adjoint = local_back[::-1]
    keep_first = keep_rate * (1.0 - seq_starts[0].astype(jnp.float32))
    leaving = keep_first * local_adjoint[0]
    _, arriving = prefix((whole_keep, leaving), "seq", combine, identity, True)
    tail_keep = jnp.where(
        (counts == counts[-1])[:, None],
        jnp.exp((float(row_count) - 1.0 - positions) * log_decay),
        0.0,
    )
    adjoint = local_adjoint + tail_keep * arriving
    previous = jnp.concatenate([entering[None], states[:-1]], axis=0)
    keep_rows = 1.0 - seq_starts.astype(jnp.float32)[:, None]
    grad_keep = jnp.sum(adjoint * (keep_rows * previous - reduced), axis=0)
    grad_ssm_rate = -grad_keep * keep_rate * ssm_step
    grad_ssm_step = -grad_keep * keep_rate * ssm_rate
    grad_pre_reduce = (1.0 - keep_rate) * adjoint * reduce_slope
    grad_b_reduce = jnp.sum(grad_pre_reduce, axis=0)
    grad_w_reduce = contract_rows(normed, grad_pre_reduce)
    grad_pre_gate = grad_gate * gate_slope
    grad_b_gate = jnp.sum(grad_pre_gate, axis=0)
    grad_w_gate = contract_rows(normed, grad_pre_gate)
    normed_back = contract_cols(grad_pre_gate, w_gate) + contract_cols(grad_pre_reduce, w_reduce)
    grad_normed = lax.psum(normed_back, "wa")
    grad_ln_gain = jnp.sum(grad_normed * standard, axis=0)
    grad_ln_bias = jnp.sum(grad_normed, axis=0)
    scaled = grad_normed * ln_gain
    grad_inputs = full_grad + inv_std * (
        scaled
        - jnp.mean(scaled, axis=1, keepdims=True)
        - standard * jnp.mean(scaled * standard, axis=1, keepdims=True)
    )
    summed = (
        lax.psum_scatter(grad_w_gate, "seq", scatter_dimension=0, tiled=True),
        lax.psum_scatter(grad_b_gate, "seq", scatter_dimension=0, tiled=True),
        lax.psum_scatter(grad_w_reduce, "seq", scatter_dimension=0, tiled=True),
        lax.psum_scatter(grad_b_reduce, "seq", scatter_dimension=0, tiled=True),
        lax.psum_scatter(grad_ssm_rate, "seq", scatter_dimension=0, tiled=True),
        lax.psum_scatter(grad_ssm_step, "seq", scatter_dimension=0, tiled=True),
        lax.psum_scatter(grad_ssm_out, "seq", scatter_dimension=0, tiled=True),
        lax.psum_scatter(grad_ln_gain, "seq", scatter_dimension=0, tiled=True),
        lax.psum_scatter(grad_ln_bias, "seq", scatter_dimension=0, tiled=True),
        lax.psum_scatter(grad_w_down, "seq", scatter_dimension=0, tiled=True),
        lax.psum_scatter(grad_b_down, "seq", scatter_dimension=0, tiled=True),
        lax.psum_scatter(grad_w_expand, "seq", scatter_dimension=0, tiled=True),
        lax.psum_scatter(grad_b_expand, "seq", scatter_dimension=0, tiled=True),
    )
    (
        total_w_gate,
        total_b_gate,
        total_w_reduce,
        total_b_reduce,
        total_rate,
        total_step,
        total_out,
        total_gain,
        total_bias,
        total_w_down,
        total_b_down,
        total_w_expand,
        total_b_expand,
    ) = summed
    return (
        output,
        grad_inputs,
        total_gain,
        total_bias,
        total_w_gate,
        total_b_gate,
        total_w_reduce,
        total_b_reduce,
        total_rate,
        total_step,
        total_out,
        total_w_expand,
        total_b_expand,
        total_w_down,
        total_b_down,
    )


def solution(mesh):
    in_specs = (
        P("seq", None),
        P("seq"),
        P(),
        P(),
        P(None, "wa"),
        P("wa"),
        P(None, "wa"),
        P("wa"),
        P("wa"),
        P("wa"),
        P("wa"),
        P(None, "wa"),
        P("wa"),
        P(None, "wa"),
        P(),
        P("seq", "wa"),
    )
    out_specs = (
        P("seq", "wa"),
        P("seq", None),
        P("seq"),
        P("seq"),
        P("seq", "wa"),
        P(("wa", "seq")),
        P("seq", "wa"),
        P(("wa", "seq")),
        P(("wa", "seq")),
        P(("wa", "seq")),
        P(("wa", "seq")),
        P("seq", "wa"),
        P(("wa", "seq")),
        P("seq", "wa"),
        P("seq"),
    )
    return jax.shard_map(body, mesh=mesh, in_specs=in_specs, out_specs=out_specs, check_vma=False)
```

profile of v0, /device:TPU:0, one launch (start us, length us, event | category | flops | bytes accessed | tf_op | source)
XLA Modules:
  0.0 898.7 jit_solution(10816871605943945724)
XLA Ops:
  18.6 8.4 broadcast_multiply_fusion.2
  27.0 17.8 %fusion.40 = f32[1536,768]{1,0:T(8,128)} fusion(f32[1024,768]{1,0:T(8,128)S(1)} %copy-done.15, f32[1536,1024]{1,0:T(8,128)S(1)} %copy-done.1, f32[1024]{0:T(1024)S(1)} %copy-done.17, f32[1024]{0:T(1024)S(1)} %copy-done.10, f32[1536]{0:T(1024)S(1)} %add_rsqrt_fusion, f32[1536]{0:T(1024)S(1)} %broadcast_multiply_fusion.5), kind=kOutput, calls=%fused_computation.94 | convolution fusion | flops 14501806080 | bytes 14176256 | tf_op jit(solution)/shard_map/dot_general | solution.py:108
  44.8 13.9 %all-gather.11.cloned.1.call-done = f32[1536,1024]{1,0:T(8,128)} async-done(((f32[1536,256]{1,0:T(8,128)}), f32[1536,1024]{1,0:T(8,128)}) %all-gather.11.cloned.1.call-update) | async-done | bytes 6291472 | tf_op jit(solution)/shard_map/all_gather | solution.py:132
  58.7 20.1 %fusion.41 = (f32[768]{0:T(1024)S(1)}, f32[1536,768]{1,0:T(8,128)S(1)}, f32[1536,768]{1,0:T(8,128)}) fusion(f32[1536,768]{1,0:T(8,128)} %fusion.40, f32[768]{0:T(1024)S(1)} %copy-done.8, f32[1536,1024]{1,0:T(8,128)} %all-gather.11.cloned.1.call-done, f32[1024,768]{1,0:T(8,128)S(1)} %copy-done), kind=kOutput, calls=%fused_computation.95 | convolution fusion | flops 14503771136 | bytes 23599104 | tf_op jit(solution)/shard_map/dot_general | solution.py:134
  81.0 9.4 %fusion.51 = f32[1536,512]{1,0:T(8,128)} fusion(f32[1536,768]{1,0:T(8,128)S(1)} %get-tuple-element.404, f32[512,768]{1,0:T(8,128)S(1)} %copy-done.4), kind=kOutput, calls=%fused_computation.101 | convolution fusion | flops 7247757312 | bytes 9437184 | tf_op jit(solution)/shard_map/dot_general | solution.py:45
  91.5 105.6 %while.58 = (s32[]{:T(128)}, f32[128]{0:T(128)S(1)}, s32[]{:T(128)}, f32[12,128,128]{2,1,0:T(8,128)}, f32[12,128,128]{2,1,0:T(8,128)}, /*index=5*/s32[12,128]{1,0:T(8,128)S(1)}, f32[128]{0:T(128)S(1)}, s32[]{:T(128)}) while((s32[]{:T(128)}, f32[128]{0:T(128)S(1)}, s32[]{:T(128)}, f32[12,128,128]{2,1,0:T(8,128)}, ...), condition=%wide.region_5.6_spmd.clone, body=%wide.region_4.5_spmd.clone.sunk | while | flops 8536322 | bytes 628085 | solution.py:73
  198.4 20.4 %all-gather.4 = f32[8,1,128]{2,1,0:T(1,128)S(1)} all-gather(f32[1,1,128]{2,1,0:T(1,128)S(1)} %get-tuple-element.413), channel_id=3, replica_groups=mesh['seq'=8,'wa'=4] {'seq'}, dimensions={0}, use_global_device_ids=true | all-gather | bytes 4608 | tf_op jit(solution)/shard_map/all_gather | solution.py:18
  218.8 16.1 %all-gather.3 = f32[8,1,128]{2,1,0:T(1,128)S(1)} all-gather(f32[1,1,128]{2,1,0:T(1,128)S(1)} %bitcast.144), channel_id=2, replica_groups=mesh['seq'=8,'wa'=4] {'seq'}, dimensions={0}, use_global_device_ids=true | all-gather | bytes 4608 | tf_op jit(solution)/shard_map/all_gather | solution.py:18
  248.7 105.2 %while.59 = (s32[]{:T(128)}, f32[128]{0:T(128)S(1)}, s32[]{:T(128)}, f32[12,128,128]{2,1,0:T(8,128)}, f32[12,128,128]{2,1,0:T(8,128)}, /*index=5*/s32[12,128]{1,0:T(8,128)S(1)}, f32[128]{0:T(128)S(1)}, s32[]{:T(128)}) while((s32[]{:T(128)}, f32[128]{0:T(128)S(1)}, s32[]{:T(128)}, f32[12,128,128]{2,1,0:T(8,128)}, ...), condition=%wide.region_11.12_spmd.clone, body=%wide.region_10.11_spmd.clone.sunk | while | flops 8536322 | bytes 628085 | solution.py:73
  361.3 18.4 %all-gather.5 = f32[8,1,128]{2,1,0:T(1,128)S(1)} all-gather(f32[1,1,128]{2,1,0:T(1,128)S(1)} %fusion.34), channel_id=4, replica_groups=mesh['seq'=8,'wa'=4] {'seq'}, dimensions={0}, use_global_device_ids=true | all-gather | bytes 4608 | tf_op jit(solution)/shard_map/all_gather | solution.py:18
  384.1 15.8 %fusion.45 = (f32[768]{0:T(1024)S(1)}, f32[1536,768]{1,0:T(8,128)S(1)}, f32[1536,768]{1,0:T(8,128)}) fusion(f32[1536,768]{1,0:T(8,128)} %fusion.40, f32[768]{0:T(1024)S(1)} %copy-done.8, f32[1536,768]{1,0:T(8,128)} %get-tuple-element.424, f32[768]{0:T(1024)S(1)} %copy-done.11, f32[1536,512]{1,0:T(8,128)} %all-gather.9.cloned.1.call-done, f32[512,768]{1,0:T(8,128)} %param.35), kind=kOutput, calls=%fused_computation.97 | convolution fusion | flops 7265451008 | bytes 23602176 | tf_op jit(solution)/shard_map/dot_general | solution.py:124
  400.0 16.9 %fusion.50 = f32[1536,1024]{1,0:T(8,128)S(1)} fusion(f32[1536,768]{1,0:T(8,128)S(1)} %get-tuple-element.410, f32[1024,768]{1,0:T(8,128)S(1)} %copy-done.16), kind=kOutput, calls=%fused_computation.100 | convolution fusion | flops 14495514624 | bytes 14155776 | tf_op jit(solution)/shard_map/dot_general | solution.py:45
  424.3 21.0 %convolution_bitcast_fusion = f32[1024,768]{0,1:T(8,128)} fusion(f32[1536,768]{1,0:T(8,128)} %get-tuple-element.417, f32[1536,1024]{1,0:T(8,128)} %all-gather.11.cloned.1.call-done), kind=kOutput, calls=%fused_computation.51 | convolution fusion | flops 14495514624 | bytes 14155776 | tf_op jit(solution)/shard_map/dot_general | solution.py:41
  445.4 19.1 %fusion.49 = f32[1536,1024]{1,0:T(8,128)} fusion(f32[1536,768]{1,0:T(8,128)} %get-tuple-element.417, f32[1024,768]{1,0:T(8,128)S(1)} %copy-done), kind=kOutput, calls=%fused_computation.99 | convolution fusion | flops 14495514624 | bytes 14155776 | tf_op jit(solution)/shard_map/dot_general | solution.py:45
  464.6 14.0 %fusion.38 = f32[1024,128]{1,0:T(8,128)} fusion(f32[1536,128]{1,0:T(8,128)} %get-tuple-element.408, f32[1536,1024]{1,0:T(8,128)} %param.24, f32[1024]{0:T(1024)S(1)} %copy-done.17, f32[1024]{0:T(1024)S(1)} %copy-done.10, f32[1536]{0:T(1024)S(1)} %add_rsqrt_fusion, f32[1536]{0:T(1024)S(1)} %broadcast_multiply_fusion.5), kind=kOutput, calls=%fused_computation.92 | convolution fusion | flops 2422210560 | bytes 7622656 | tf_op jit(solution)/shard_map/dot_general | solution.py:41
  478.7 11.5 %fusion.52 = f32[512,768]{1,0:T(8,128)} fusion(f32[1536,512]{1,0:T(8,128)} %all-gather.9.cloned.1.call-done, f32[1536,768]{1,0:T(8,128)} %copy-done.2), kind=kOutput, calls=%fused_computation.102 | convolution fusion | flops 7247757312 | bytes 9437184 | tf_op jit(solution)/shard_map/dot_general | solution.py:41
  490.3 21.3 %fusion.39 = f32[1024,768]{1,0:T(8,128)} fusion(f32[1536,768]{1,0:T(8,128)} %copy-done.5, f32[1536,1024]{1,0:T(8,128)} %param.24, f32[1024]{0:T(1024)S(1)} %copy-done.17, f32[1024]{0:T(1024)S(1)} %copy-done.10, f32[1536]{0:T(1024)S(1)} %add_rsqrt_fusion, f32[1536]{0:T(1024)S(1)} %broadcast_multiply_fusion.5), kind=kOutput, calls=%fused_computation.93 | convolution fusion | flops 14501806080 | bytes 14176256 | tf_op jit(solution)/shard_map/dot_general | solution.py:41
  515.0 25.4 %all-reduce.12.cloned.1.call-done = f32[1536,1024]{1,0:T(8,128)} async-done(((f32[1536,1024]{1,0:T(8,128)}), f32[1536,1024]{1,0:T(8,128)}) %all-reduce.12.cloned.1.call-update) | async-done | bytes 6291472 | tf_op jit(solution)/shard_map/psum | solution.py:167
  554.3 38.0 %all-reduce.9 = (f32[1024]{0:T(1024)S(1)}, f32[1024]{0:T(1024)S(1)}, f32[768]{0:T(1024)S(1)}, f32[128]{0:T(128)S(1)}, f32[128]{0:T(128)S(1)}, /*index=5*/f32[128...) all-reduce(f32[1024]{0:T(1024)S(1)} %get-tuple-element.334, ...), channel_id=7, replica_groups=mesh['seq'=8,'wa'=4] {'seq'}, use_global_device_ids=true, to_apply=%region_18.19.clone | all-reduce | flops 5120 | bytes 40960
  597.5 22.6 %reduce-scatter.17.cloned.1.call-done = f32[128,768]{0,1:T(8,128)} async-done(((f32[1024,768]{0,1:T(8,128)}), f32[128,768]{0,1:T(8,128)}) %reduce-scatter.17.cloned.1.call-update) | async-done | bytes 393232 | tf_op jit(solution)/shard_map/reduce_scatter | solution.py:186
  622.0 58.2 %reduce-scatter.7.cloned.1.call-done = f32[1536,256]{1,0:T(8,128)} async-done(((f32[1536,1024]{1,0:T(8,128)}), f32[1536,256]{1,0:T(8,128)}) %reduce-scatter.7.cloned.1.call-update) | async-done | bytes 1572880 | tf_op jit(solution)/shard_map/reduce_scatter | solution.py:130
  683.4 62.6 %reduce-scatter.13.cloned.1.call-done = f32[128,128]{1,0:T(8,128)} async-done(((f32[1024,128]{1,0:T(8,128)}), f32[128,128]{1,0:T(8,128)}) %reduce-scatter.13.cloned.1.call-update) | async-done | bytes 65552 | tf_op jit(solution)/shard_map/reduce_scatter | solution.py:179
  746.0 68.3 %reduce-scatter.15.cloned.1.call-done = f32[64,768]{1,0:T(8,128)} async-done(((f32[512,768]{1,0:T(8,128)}), f32[64,768]{1,0:T(8,128)}) %reduce-scatter.15.cloned.1.call-update) | async-done | bytes 196624 | tf_op jit(solution)/shard_map/reduce_scatter | solution.py:188
  814.3 77.6 %reduce-scatter.11.cloned.1.call-done = f32[128,768]{1,0:T(8,128)} async-done(((f32[1024,768]{1,0:T(8,128)}), f32[128,768]{1,0:T(8,128)}) %reduce-scatter.11.cloned.1.call-update) | async-done | bytes 393232 | tf_op jit(solution)/shard_map/reduce_scatter | solution.py:177
  (333 shorter events, 275.5 us)
Async XLA Ops:
  7.2 51.6 %copy-start = (f32[1024,768]{1,0:T(8,128)S(1)}, f32[1024,768]{1,0:T(8,128)}, u32[]{:S(2)}) copy-start(f32[1024,768]{1,0:T(8,128)} %param.37) | copy-start | bytes 9437188
  7.2 51.5 %all-gather.11.cloned.1.call-start = ((), (), s32[]{:S(2)}) async-start(), calls=%async_computation.8 | async-start | bytes 7864320 | tf_op jit(solution)/shard_map/all_gather | solution.py:132
  7.9 227.8 %reduce-scatter.9.cloned.1.call-start = ((), (), s32[]{:S(2)}) async-start(), calls=%async_computation.9 | async-start | bytes 3932160 | tf_op jit(solution)/shard_map/reduce_scatter | solution.py:141
  10.7 7.0 copy-start.10
  10.7 7.0 copy-start.17
  10.7 7.0 copy-start.18
  13.9 13.1 %copy-start.15 = (f32[1024,768]{1,0:T(8,128)S(1)}, f32[1024,768]{1,0:T(8,128)}, u32[]{:S(2)}) copy-start(f32[1024,768]{1,0:T(8,128)} %param.28) | copy-start | bytes 9437188
  27.0 31.7 %copy-start.8 = (f32[768]{0:T(1024)S(1)}, f32[768]{0:T(1024)}, u32[]{:S(2)}) copy-start(f32[768]{0:T(1024)} %param.29) | copy-start | bytes 9220
  58.7 22.3 %copy-start.4 = (f32[512,768]{1,0:T(8,128)S(1)}, f32[512,768]{1,0:T(8,128)}, u32[]{:S(2)}) copy-start(f32[512,768]{1,0:T(8,128)} %param.35) | copy-start | bytes 4718596
  90.5 293.6 %all-gather.9.cloned.1.call-start = ((), (), s32[]{:S(2)}) async-start(), calls=%async_computation.6 | async-start | bytes 3932160 | tf_op jit(solution)/shard_map/all_gather | solution.py:123
  91.5 105.7 %copy-start.9 = (s32[1536]{0:T(1024)S(1)}, s32[1536]{0:T(1024)}, u32[]{:S(2)}) copy-start(s32[1536]{0:T(1024)} %param.25) | copy-start | bytes 18436
  91.5 144.2 %copy-start.12 = (f32[128]{0:T(128)S(1)}, f32[128]{0:T(128)}, u32[]{:S(2)}) copy-start(f32[128]{0:T(128)} %param.34) | copy-start | bytes 1540
  247.6 292.7 %all-reduce.12.cloned.1.call-start = ((), (), s32[]{:S(2)}) async-start(), calls=%async_computation.10 | async-start | bytes 12582912 | tf_op jit(solution)/shard_map/psum | solution.py:167
  248.7 135.4 %copy-start.11 = (f32[768]{0:T(1024)S(1)}, f32[768]{0:T(1024)}, u32[]{:S(2)}) copy-start(f32[768]{0:T(1024)} %param.36) | copy-start | bytes 9220
  384.1 15.9 %copy-start.16 = (f32[1024,768]{1,0:T(8,128)S(1)}, f32[1024,768]{1,0:T(8,128)}, u32[]{:S(2)}) copy-start(f32[1024,768]{1,0:T(8,128)} %param.28) | copy-start | bytes 9437188
  400.0 17.0 %copy-start.5 = (f32[1536,768]{1,0:T(8,128)}, f32[1536,768]{1,0:T(8,128)S(1)}, u32[]{:S(2)}) copy-start(f32[1536,768]{1,0:T(8,128)S(1)} %get-tuple-element.410) | copy-start | bytes 14155780
  400.0 16.9 %copy-start.6 = (f32[1536,128]{1,0:T(8,128)S(1)}, f32[1536,128]{1,0:T(8,128)}, u32[]{:S(2)}) copy-start(f32[1536,128]{1,0:T(8,128)} %get-tuple-element.408) | copy-start | bytes 2359300
  400.0 16.9 %copy-start.7 = (f32[1024,128]{1,0:T(8,128)S(1)}, f32[1024,128]{1,0:T(8,128)}, u32[]{:S(2)}) copy-start(f32[1024,128]{1,0:T(8,128)} %param.30) | copy-start | bytes 1572868
  424.3 195.8 %reduce-scatter.17.cloned.1.call-start = ((), (), s32[]{:S(2)}) async-start(), calls=%async_computation.14 | async-start | bytes 3538944 | tf_op jit(solution)/shard_map/reduce_scatter | solution.py:186
  445.3 234.8 %reduce-scatter.7.cloned.1.call-start = ((), (), s32[]{:S(2)}) async-start(), calls=%async_computation.7 | async-start | bytes 7864320 | tf_op jit(solution)/shard_map/reduce_scatter | solution.py:130
  464.5 281.4 %reduce-scatter.13.cloned.1.call-start = ((), (), s32[]{:S(2)}) async-start(), calls=%async_computation.12 | async-start | bytes 589824 | tf_op jit(solution)/shard_map/reduce_scatter | solution.py:179
  478.7 335.7 %reduce-scatter.15.cloned.1.call-start = ((), (), s32[]{:S(2)}) async-start(), calls=%async_computation.13 | async-start | bytes 1769472 | tf_op jit(solution)/shard_map/reduce_scatter | solution.py:188
  490.2 21.4 %copy-start.19 = (u32[32]{0:T(128)S(1)}, u32[32]{0:T(128)}, u32[]{:S(2)}) copy-start(u32[32]{0:T(128)} %constant.134) | copy-start | bytes 388
  490.3 401.7 %reduce-scatter.11.cloned.1.call-start = ((), (), s32[]{:S(2)}) async-start(), calls=%async_computation.11 | async-start | bytes 3538944 | tf_op jit(solution)/shard_map/reduce_scatter | solution.py:177
  (5 other events, 26.7 us)
Sparse Core Ops, SparseCore 0:
  9.6 49.0 all-gather.10
  90.6 37.9 reduce-scatter.8
  247.7 26.9 all-gather.8
  424.4 115.9 all-reduce.11
  544.2 75.8 reduce-scatter.16
  622.7 57.4 reduce-scatter.6
  684.1 61.8 reduce-scatter.12
  750.4 63.9 reduce-scatter.14
  818.5 73.3 reduce-scatter.10
where the time goes:
time: 907 us; the launch traced here: 899 us
  waiting for transfers between devices  329 us (36%)
  other arithmetic  204 us (22%)
  matrix products  183 us (20%)
  blocking collectives  92.9 us (10%)
  local copies, waits for them, and re-layouts  63.2 us (7%)
  between operations  17.7 us (2%)
    dot_general x24, other arithmetic, advance(): within = jnp.einsum('tsh,sh->th', kernel, block_in, precision=HIGHEST)  139 us
    reduce_scatter x1, waiting for transfers between devices, body(): lax.psum_scatter(grad_w_gate, 'seq', scatter_dimension=0, tiled=True)  77.6 us
    reduce_scatter x1, waiting for transfers between devices, body(): lax.psum_scatter(grad_w_expand, 'seq', scatter_dimension=0, tiled=True)  68.3 us
    dot_general x4, matrix products, contract_rows(): lax.dot_general(left, right, (((0,), (0,)), ((), ())), precision=HIGHEST)  67.9 us
    reduce_scatter x1, waiting for transfers between devices, body(): lax.psum_scatter(grad_w_reduce, 'seq', scatter_dimension=0, tiled=True)  62.6 us
    reduce_scatter x1, waiting for transfers between devices, body(): lax.psum_scatter(partial_out, 'wa', scatter_dimension=1, tiled=True)  58.2 us
    all_gather x3, blocking collectives, prefix(): gathered = jax.tree.map(lambda a: lax.all_gather(a, axis), part)  55 us
    dot_general x4, matrix products, contract_cols(): lax.dot_general(left, right, (((1,), (1,)), ((), ())), precision=HIGHEST)  52.8 us
  transfers between devices with their start and end apart: 9, of which 7 were waited for; matrix products, arithmetic and copies ran while one was open for 41% of the time, Pallas kernels for 0%

commit v1 on v0

v1 whole, which is shorter than its diff:
```python
import functools

import jax
import jax.numpy as jnp
from jax import lax
from jax.experimental import pallas as pl
from jax.experimental.pallas import tpu as pltpu
from jax.sharding import PartitionSpec as P

EPSILON = 1e-05
INV_ROOT_TAU = 0.3989422804014327
SEQ_MAX = 4096
F32 = jnp.float32
BF16 = jnp.bfloat16
VMEM_LIMIT = 26 * 2**20
TILE = 256
COST = 10**5
RATE = 5 * 10**7
FILL = 400
NN = ((1,), (0,))
NT = ((1,), (1,))
TN = ((0,), (0,))


def split(value):
    high = value.astype(BF16)
    return high, (value - high.astype(F32)).astype(BF16)


def dot(left, right, dims):
    return lax.dot_general(left, right, (dims, ((), ())), preferred_element_type=F32)


def dot3(left, right, dims):
    (left_high, left_low), (right_high, right_low) = left, right
    return dot(left_high, right_high, dims) + (
        dot(left_high, right_low, dims) + dot(left_low, right_high, dims)
    )


def gelu_parts(v):
    bell = jnp.exp(-0.5 * v * v)
    span = 1.0 + 0.23164189 * jnp.abs(v)
    t = pl.reciprocal(span, approx=True)
    t = t * (2.0 - span * t)
    tail = 0.5 * (1.061405429 * t - 1.453152027)
    tail = tail * t + 0.5 * 1.421413741
    tail = tail * t - 0.5 * 0.284496736
    tail = tail * t + 0.5 * 0.254829592
    tail = tail * t * bell
    cdf = jnp.where(v < 0.0, tail, 1.0 - tail)
    return v * cdf, cdf + (INV_ROOT_TAU * v) * bell


def standardise(values):
    scale = 1.0 / values.shape[1]
    centred = values - jnp.sum(values, axis=1, keepdims=True) * scale
    variance = jnp.sum(centred * centred, axis=1, keepdims=True) * scale
    inv_std = lax.rsqrt(variance + EPSILON)
    return centred * inv_std, inv_std


def row_sums(value):
    return jnp.sum(value.reshape(value.shape[0] // 8, 8, value.shape[1]), axis=0)


def sublane(shape=(8, 128)):
    return lax.broadcasted_iota(jnp.int32, shape, 0)


def wide(row):
    return jnp.broadcast_to(row, (8, row.shape[1]))


def entering(gots):
    total = gots[0][0:1, :]
    keep = gots[0][1:2, :]
    for got in gots[1:]:
        total = total + keep * got[0:1, :]
        keep = keep * got[1:2, :]
    return total


def first_step():
    return pl.program_id(0) == 0


def last_step():
    return pl.program_id(0) == pl.num_programs(0) - 1


def apart():
    return pl.when(pl.program_id(0) >= 0)


def add_to(ref, value):
    @pl.when(first_step())
    def _():
        ref[...] = jnp.zeros_like(ref)

    ref[...] += value


def split_rows(ids_ref, order, source_ref, high, low):
    width = high.shape[0] // len(order)
    for place, r in enumerate(order):
        at = pl.multiple_of((ids_ref[0] ^ r) * width, width)
        to = slice(place * width, (place + 1) * width)
        high[to, :], low[to, :] = split(source_ref[pl.ds(at, width), :])


def reduce_kernel(
    x_ref, gain_ref, shift_ref, w_ref, b_ref, rate_ref, step_ref, mask_ref,
    high_ref, low_ref, red_ref, slope_ref, local_ref, lead_ref, end_ref,
    w_high, w_low, drive_ref, carry_ref,
):
    log_keep = -rate_ref[...] * step_ref[...]
    keep = wide(jnp.exp(log_keep))
    fresh = 1.0 - jnp.exp(log_keep)

    @pl.when(first_step())
    def _():
        w_high[...], w_low[...] = split(w_ref[...])
        carry_ref[0:8, :] = jnp.zeros((8, 128), F32)
        carry_ref[8:16, :] = jnp.ones((8, 128), F32)

    standard, _ = standardise(x_ref[...])
    parts = split(standard * gain_ref[...] + shift_ref[...])
    high_ref[...], low_ref[...] = parts
    pre = dot3(parts, (w_high[...], w_low[...]), NN) + b_ref[...]
    reduced, slope_ref[...] = gelu_parts(pre)
    red_ref[...] = reduced
    drive_ref[...] = fresh * reduced
    at = sublane()
    powers = [keep, keep * keep]
    powers.append(powers[1] * powers[1])
    ramp = jnp.exp((at + 1).astype(F32) * log_keep)

    def step(j, carry):
        state, decay = carry
        here = pl.ds(pl.multiple_of(j * 8, 8), 8)
        value = drive_ref[here, :]
        mask = mask_ref[here, :]
        for power, hop in zip(powers, (1, 2, 4)):
            inside = at >= hop
            value = value + jnp.where(inside, power * mask, 0.0) * pltpu.roll(value, hop, 0)
            mask = jnp.where(inside, mask * pltpu.roll(mask, hop, 0), mask)
        factor = ramp * mask
        value = value + factor * state
        factor = factor * decay
        local_ref[here, :] = value
        lead_ref[here, :] = factor
        return (wide(value[7:8, :]), wide(factor[7:8, :]))

    start = (carry_ref[0:8, :], carry_ref[8:16, :])
    state, decay = lax.fori_loop(0, x_ref.shape[0] // 8, step, start, unroll=8)
    carry_ref[0:8, :] = state
    carry_ref[8:16, :] = decay
    end_ref[...] = jnp.where(at == 0, state, decay)


def gate_kernel(high_ref, low_ref, w_ref, b_ref, act_ref, slope_ref, w_high, w_low):
    @pl.when(first_step())
    def _():
        w_high[...], w_low[...] = split(w_ref[...])

    pre = dot3((high_ref[...], low_ref[...]), (w_high[...], w_low[...]), NN) + b_ref[...]
    act_ref[...], slope_ref[...] = gelu_parts(pre)


def states_kernel(hops, local_ref, lead_ref, red_ref, mask_ref, out_ref, *rest):
    gots, (mixed_ref, states_ref, turn_ref, last_ref) = rest[:hops], rest[hops:]
    enter = entering(gots)

    @pl.when(first_step())
    def _():
        last_ref[...] = wide(enter)

    states = local_ref[...] + lead_ref[...] * enter
    states_ref[...] = states
    mixed_ref[...] = states * out_ref[...]
    first = sublane(states.shape) == 0
    before = jnp.where(first, last_ref[0:1, :], pltpu.roll(states, 1, 0))
    turn_ref[...] = mask_ref[...] * before - red_ref[...]
    last_ref[...] = wide(states[states.shape[0] - 1 :, :])


def cotangent_kernel(
    ids_ref, c0, c1, c2, c3, wd_ref, act_ref, we_ref,
    high_ref, low_ref, gp_ref, ge_high, ge_low, send_ref, c_sum,
    wd_high, wd_low, we_high, we_low,
):
    width = c0.shape[1]

    @pl.when(first_step())
    def _():
        split_rows(ids_ref, range(4), wd_ref, wd_high, wd_low)
        split_rows(ids_ref, (3, 1), we_ref, we_high, we_low)

    for r, c in enumerate((c0, c1, c2, c3)):
        at = slice(r * width, (r + 1) * width)
        high_ref[:, at], low_ref[:, at] = split(c[...])
        add_to(c_sum.at[:, at], row_sums(c[...]))
    grad_product = dot3((high_ref[...], low_ref[...]), (wd_high[...], wd_low[...]), NN)
    gp_ref[...] = grad_product
    ge_high[...], ge_low[...] = split(grad_product * act_ref[...])

    @apart()
    def _():
        send_ref[...] = dot3((ge_high[...], ge_low[...]), (we_high[...], we_low[...]), NT)


def back_kernel(ids_ref, ge_high, ge_low, we_ref, keep_ref, ge_sum, we_high, we_low):
    @pl.when(first_step())
    def _():
        split_rows(ids_ref, (2, 0), we_ref, we_high, we_low)

    keep_ref[...] = dot3((ge_high[...], ge_low[...]), (we_high[...], we_low[...]), NT)
    add_to(ge_sum, row_sums(ge_high[...].astype(F32) + ge_low[...].astype(F32)))


def expand_kernel(
    ids_ref, m0, m1, m2, m3, we_ref, be_ref, wd_ref, act_ref, slope_ref, gp_ref,
    mix_high, mix_low, prod_high, prod_low, gate_high, gate_low, send_ref, keep_ref, gate_sum,
    we_high, we_low, wd_high, wd_low,
):
    here = ids_ref[0]
    own = m0.shape[1]
    width = send_ref.shape[1]

    @pl.when(first_step())
    def _():
        for r in range(4):
            at = pl.multiple_of((here ^ r) * own, own)
            to = slice(r * own, (r + 1) * own)
            we_high[to, :], we_low[to, :] = split(we_ref[pl.ds(at, own), :])
        for place, r in enumerate((3, 2)):
            at = pl.multiple_of((here ^ r) * width, width)
            to = slice(place * width, (place + 1) * width)
            wd_high[to, :], wd_low[to, :] = split(wd_ref[pl.ds(at, width), :])

    for r, m in enumerate((m0, m1, m2, m3)):
        at = slice(r * own, (r + 1) * own)
        mix_high[:, at], mix_low[:, at] = split(m[...])
    expand = dot3((mix_high[...], mix_low[...]), (we_high[...], we_low[...]), NN) + be_ref[...]
    prod_high[...], prod_low[...] = split(act_ref[...] * expand)
    grad_gate = gp_ref[...] * expand * slope_ref[...]
    gate_high[...], gate_low[...] = split(grad_gate)
    add_to(gate_sum, row_sums(grad_gate))

    @apart()
    def _():
        out = dot3((prod_high[...], prod_low[...]), (wd_high[...], wd_low[...]), NT)
        send_ref[...] = out[:, :width]
        keep_ref[...] = out[:, width:]


def output_kernel(
    ids_ref, high_ref, low_ref, wd_ref, x_ref, b_ref, send_ref, keep_ref, wd_high, wd_low
):
    here = ids_ref[0]
    width = send_ref.shape[1]

    @pl.when(first_step())
    def _():
        for place, r in enumerate((1, 0)):
            at = pl.multiple_of((here ^ r) * width, width)
            to = slice(place * width, (place + 1) * width)
            wd_high[to, :], wd_low[to, :] = split(wd_ref[pl.ds(at, width), :])

    out = dot3((high_ref[...], low_ref[...]), (wd_high[...], wd_low[...]), NT)
    send_ref[...] = out[:, :width]
    keep_ref[...] = out[:, width:] + x_ref[...] + b_ref[...]


def adjoint_kernel(
    keep_ref, recv_ref, far_ref, states_ref, mask_ref, out_ref, rate_ref, step_ref,
    local_ref, tail_ref, end_ref, sum_ref, carry_ref,
):
    own = far_ref.shape[1]
    log_keep = -rate_ref[...] * step_ref[...]
    keep = wide(jnp.exp(log_keep))

    @pl.when(first_step())
    def _():
        carry_ref[0:8, :] = jnp.zeros((8, 128), F32)
        carry_ref[8:16, :] = jnp.ones((8, 128), F32)

    at = sublane()
    powers = [keep, keep * keep]
    powers.append(powers[1] * powers[1])
    ramp = jnp.exp((8 - at).astype(F32) * log_keep)
    out_rate = wide(out_ref[...])
    count = far_ref.shape[0] // 8

    def step(n, carry):
        state, decay, total = carry
        here = pl.ds(pl.multiple_of((count - 1 - n) * 8, 8), 8)
        grad = keep_ref[here, own:] + recv_ref[here, own:] + far_ref[here, :]
        total = total + grad * states_ref[here, :]
        drive = grad * out_rate
        mask = mask_ref[here, :]
        value = keep * mask * drive
        for power, hop in zip(powers, (1, 2, 4)):
            inside = at < 8 - hop
            value = value + jnp.where(inside, power * mask, 0.0) * pltpu.roll(value, 8 - hop, 0)
            mask = jnp.where(inside, mask * pltpu.roll(mask, 8 - hop, 0), mask)
        factor = ramp * mask
        value = value + factor * state
        factor = factor * decay
        local_ref[here, :] = drive + jnp.where(at == 7, state, pltpu.roll(value, 7, 0))
        tail_ref[here, :] = jnp.where(at == 7, decay, pltpu.roll(factor, 7, 0))
        return (wide(value[0:1, :]), wide(factor[0:1, :]), total)

    start = (carry_ref[0:8, :], carry_ref[8:16, :], jnp.zeros((8, 128), F32))
    state, decay, total = lax.fori_loop(0, count, step, start, unroll=8)
    carry_ref[0:8, :] = state
    carry_ref[8:16, :] = decay
    end_ref[...] = jnp.where(at == 0, state, decay)
    add_to(sum_ref, total)


def add_norm_sums(ids_ref, x_ref, parts, standard_ref, sums_ref):
    width = parts[0][1].shape[1]
    standard_ref[...], _ = standardise(x_ref[...])
    for r, part in parts:
        at = pl.ds(pl.multiple_of((ids_ref[0] ^ r) * width, width), width)
        sums_ref[0:8, at] += row_sums(part * standard_ref[:, at])
        sums_ref[8:16, at] += row_sums(part)


def normed_far_kernel(
    hops, ids_ref, local_ref, tail_ref, turn_ref, slope_ref, gate_high, gate_low, x_ref,
    wg_ref, wr_ref, rate_ref, step_ref, *rest,
):
    gots = rest[:hops]
    (red_high, red_low, send_ref, keep_ref, turn_sum, red_sum, norm_sum,
     wg_high, wg_low, wr_high, wr_low, standard_ref) = rest[hops:]
    width = send_ref.shape[1]

    @pl.when(first_step())
    def _():
        split_rows(ids_ref, (3, 2), wg_ref, wg_high, wg_low)
        split_rows(ids_ref, (3, 2), wr_ref, wr_high, wr_low)
        norm_sum[...] = jnp.zeros_like(norm_sum)

    adjoint = local_ref[...] + tail_ref[...] * entering(gots)
    fresh = 1.0 - jnp.exp(-rate_ref[...] * step_ref[...])
    grad = fresh * adjoint * slope_ref[...]
    parts = split(grad)
    red_high[...], red_low[...] = parts
    add_to(turn_sum, row_sums(adjoint * turn_ref[...]))
    add_to(red_sum, row_sums(grad))
    back = dot3((gate_high[...], gate_low[...]), (wg_high[...], wg_low[...]), NT)
    back = back + dot3(parts, (wr_high[...], wr_low[...]), NT)
    send_ref[...] = back[:, :width]
    keep_ref[...] = back[:, width:]
    add_norm_sums(ids_ref, x_ref, [(3, back[:, :width]), (2, back[:, width:])], standard_ref, norm_sum)


def normed_near_kernel(
    ids_ref, red_high, red_low, gate_high, gate_low, x_ref, wg_ref, wr_ref, far_sum,
    send_ref, keep_ref, norm_ref, wg_high, wg_low, wr_high, wr_low, standard_ref, norm_sum,
):
    width = send_ref.shape[1]

    @pl.when(first_step())
    def _():
        split_rows(ids_ref, (1, 0), wg_ref, wg_high, wg_low)
        split_rows(ids_ref, (1, 0), wr_ref, wr_high, wr_low)
        norm_sum[...] = far_sum[...]

    back = dot3((gate_high[...], gate_low[...]), (wg_high[...], wg_low[...]), NT)
    back = back + dot3((red_high[...], red_low[...]), (wr_high[...], wr_low[...]), NT)
    send_ref[...] = back[:, :width]
    keep_ref[...] = back[:, width:]
    add_norm_sums(ids_ref, x_ref, [(1, back[:, :width]), (0, back[:, width:])], standard_ref, norm_sum)

    @pl.when(last_step())
    def _():
        gain = jnp.sum(norm_sum[0:8, :], axis=0, keepdims=True)
        shift = jnp.sum(norm_sum[8:16, :], axis=0, keepdims=True)
        norm_ref[...] = jnp.where(sublane(norm_ref.shape) == 0, gain, shift)


def weight_kernel(relative, ids_ref, left_high, left_low, right_high, right_low, keep_ref, send_ref, acc_ref):
    @pl.when(first_step())
    def _():
        acc_ref[...] = jnp.zeros_like(acc_ref)

    for at in range(0, acc_ref.shape[1], 256):
        to = slice(at, at + 256)
        acc_ref[:, to] += dot3((left_high[...], left_low[...]), (right_high[:, to], right_low[:, to]), TN)
    half, rows, _ = keep_ref.shape
    block = acc_ref.shape[0] // 4

    @pl.when(last_step())
    def _():
        for place in range(2 * half):
            at = ids_ref[2 + place] * rows
            if relative:
                at = ((at // block) ^ ids_ref[0]) * block + at % block
            value = acc_ref[pl.ds(pl.multiple_of(at, 8), rows), :]
            if place < half:
                keep_ref[place] = value
            else:
                send_ref[place - half] = value


def reduce_weight_kernel(
    ids_ref, left_high, left_low, right_high, right_low, vector_ref, keep_ref, send_ref, acc_ref
):
    add_to(acc_ref, dot3((left_high[...], left_low[...]), (right_high[...], right_low[...]), TN))
    half, rows, _ = keep_ref.shape
    rows = rows - 8

    @pl.when(last_step())
    def _():
        for place in range(2 * half):
            block = ids_ref[2 + place]
            to, slot = (keep_ref, place) if place < half else (send_ref, place - half)
            to[slot, :rows] = acc_ref[pl.ds(pl.multiple_of(block * rows, 8), rows), :]
            to[slot, rows:] = vector_ref[pl.ds(pl.multiple_of(block * 8, 8), 8), :]


def pack_kernel(own_ref, core_ref, far_ref, far_core_ref, down_ref, gate_ref, expand_ref, red_ref, turn_ref, out_ref,
                vector_ref, whole_ref, here_ref):
    count = vector_ref.shape[0] // 8
    vector_ref[...] = jnp.zeros_like(vector_ref)
    width = down_ref.shape[1] // 4
    here = lax.axis_index("wa")
    for r in range(4):
        at = pl.multiple_of((here ^ r) * width, width)
        here_ref[2:3, pl.ds(at, width)] = jnp.sum(down_ref[:, r * width : (r + 1) * width], axis=0, keepdims=True)
    norm = (own_ref[...] + core_ref[...]) + (far_ref[...] + far_core_ref[...])
    here_ref[0:2, :] = norm[0:2, :]
    rows = [here_ref[0:1, :], here_ref[1:2, :], here_ref[2:3, :]]
    rows += [jnp.sum(ref[...], axis=0, keepdims=True) for ref in (gate_ref, expand_ref, red_ref, turn_ref, out_ref)]
    for k, row in enumerate(rows):
        whole_ref[k : k + 1, : row.shape[1]] = row
    for k, row in enumerate(rows):
        size = row.shape[1] // count
        for d in range(count):
            vector_ref[d * 8 + k : d * 8 + k + 1, :size] = whole_ref[k : k + 1, d * size : (d + 1) * size]


def final_kernel(ids_ref, x_ref, gain_ref, g0, g1, g2, g3, c0, c1, c2, c3, out_ref, grad_ref, cot_ref):
    width = g0.shape[1]
    for r, (g, c) in enumerate(((g0, c0), (g1, c1), (g2, c2), (g3, c3))):
        at = pl.ds(pl.multiple_of((ids_ref[0] ^ r) * width, width), width)
        grad_ref[:, at] = g[...]
        cot_ref[:, at] = c[...]
    scale = 1.0 / x_ref.shape[1]
    standard, inv_std = standardise(x_ref[...])
    scaled = grad_ref[...] * gain_ref[...]
    first = jnp.sum(scaled, axis=1, keepdims=True) * scale
    second = jnp.sum(scaled * standard, axis=1, keepdims=True) * scale
    out_ref[...] = cot_ref[...] + inv_std * (scaled - first - standard * second)


def shape(*dims, dtype=F32):
    return jax.ShapeDtypeStruct(dims, dtype)


def tiles(array, reverse=False, column=None, tile=TILE):
    width = array.shape[1] if column is None else column

    def index(i, *ids):
        row = array.shape[0] // tile - 1 - i if reverse else i
        return (row, 0 if column is None else ids[0][0])

    return pl.BlockSpec((tile, width), index)


def fixed(array):
    return pl.BlockSpec(array.shape, lambda i, *ids: (0,) * len(array.shape))


ANYWHERE = pl.BlockSpec(memory_space=pl.ANY)


def call(us, kernel, steps, ids, ins, outs, scratch, deps=(), vmem=VMEM_LIMIT):
    in_specs = [fixed(a) if spec is None else spec for a, spec in ins] + [ANYWHERE] * len(deps)
    skip = len(ins) + (ids is not None)

    def bare(*refs):
        kernel(*refs[:skip], *refs[skip + len(deps) :])

    out_specs = [fixed(a) if spec is None else spec for a, spec in outs]
    spec = pltpu.PrefetchScalarGridSpec(
        num_scalar_prefetch=0 if ids is None else 1,
        grid=(steps,),
        in_specs=in_specs,
        out_specs=out_specs,
        scratch_shapes=[pltpu.VMEM(s, d) for s, d in scratch],
    )
    run = pl.pallas_call(
        bare,
        grid_spec=spec,
        out_shape=[a for a, _ in outs],
        compiler_params=pltpu.CompilerParams(vmem_limit_bytes=vmem),
        cost_estimate=pl.CostEstimate(flops=int(us * RATE), bytes_accessed=int(us * COST), transcendentals=0),
    )
    arrays = [a for a, _ in ins] + list(deps)
    return run(*arrays) if ids is None else run(ids, *arrays)


def after(value, *others):
    return lax.optimization_barrier((value,) + others)[0]


def wa_swap(value, distance):
    count = lax.axis_size("wa")
    return lax.ppermute(value, "wa", [(i, i ^ distance) for i in range(count)])


def seq_swap(value, distance):
    count = lax.axis_size("seq")
    return lax.ppermute(value, "seq", [(i, i ^ distance) for i in range(count)])


def seq_shift(value, hop):
    count = lax.axis_size("seq")
    pairs = [(i, i + hop) for i in range(count) if 0 <= i + hop < count]
    return lax.ppermute(value, "seq", pairs)


def block_order(bits):
    count = lax.axis_size("seq")
    if count != 8:
        return jnp.arange(count, dtype=jnp.int32)
    order = [
        sum(bit for k, bit in enumerate(bits) if place >> (2 - k) & 1) for place in range(8)
    ]
    return jnp.array(order, jnp.int32) ^ lax.axis_index("seq")


class ScatterSum:
    def __init__(self, keep, send, bits):
        self.bits = bits
        if lax.axis_size("seq") != 8:
            whole = jnp.concatenate([keep, send], axis=0)
            whole = whole.reshape(-1, whole.shape[2])
            self.total = lax.psum_scatter(whole, "seq", scatter_dimension=0, tiled=True)
            self.keep = None
            return
        self.keep = keep
        self.recv = seq_swap(send, bits[0])

    def step(self, bit, token):
        if self.keep is None:
            return token
        recv = after(self.recv, token)
        half = self.keep.shape[0] // 2
        send = self.keep[half:] + recv[half:]
        self.keep = self.keep[:half] + recv[:half]
        self.recv = seq_swap(send, bit)
        return send

    def finish(self):
        if self.keep is None:
            return self.total
        return (self.keep + self.recv)[0]


def body(
    inputs,
    seq_starts,
    ln_gain,
    ln_bias,
    w_gate,
    b_gate,
    w_reduce,
    b_reduce,
    ssm_rate,
    ssm_step,
    ssm_out,
    w_expand,
    b_expand,
    w_down,
    b_down,
    cotangent,
):
    rows, width = inputs.shape
    part = cotangent.shape[1]
    units = w_gate.shape[1]
    own = w_reduce.shape[1]
    channels = w_expand.shape[0]
    seqs = lax.axis_size("seq")
    steps = rows // TILE
    hops = min(seqs - 1, (SEQ_MAX - 2 + rows) // rows)
    here = lax.axis_index("wa").astype(jnp.int32)
    place = lax.axis_index("seq").astype(jnp.int32)

    def ids_of(bits):
        return jnp.concatenate([jnp.stack([here, place]), block_order(bits)])

    ids = ids_of((1, 2, 4))
    ids_z = ids_of((2, 1, 4))
    gain, shift, b_gate, b_red, rate, step, out_rate, b_exp, b_down_row = (
        v[None] for v in (ln_gain, ln_bias, b_gate, b_reduce, ssm_rate, ssm_step, ssm_out, b_expand, b_down)
    )
    mask = jnp.broadcast_to(1.0 - seq_starts.astype(F32)[:, None], (rows, 128))

    def t(*dims, dtype=F32):
        return shape(rows, *dims, dtype=dtype)

    def tiled(*arrays):
        return [(a, tiles(a)) for a in arrays]

    def whole(*arrays):
        return [(a, None) for a in arrays]

    cot_y = wa_swap(cotangent, 2)
    cot_c = wa_swap(cotangent, 1)

    n_high, n_low, reduced, red_slope, local, lead, end = call(
        7,
        reduce_kernel,
        steps,
        None,
        tiled(inputs) + whole(gain, shift, w_reduce, b_red, rate, step) + tiled(mask),
        tiled(t(width, dtype=BF16), t(width, dtype=BF16), t(own), t(own), t(own), t(own)) + whole(shape(8, own)),
        [((width, own), BF16)] * 2 + [((TILE, own), F32), ((16, own), F32)],
    )
    gots = [seq_shift(end, hop) for hop in range(1, hops + 1)]
    act, slope = call(
        12,
        gate_kernel,
        steps,
        None,
        tiled(n_high, n_low) + whole(w_gate, b_gate),
        tiled(t(units), t(units)),
        [((width, units), BF16)] * 2,
    )
    mixed, states, turn = call(
        2,
        functools.partial(states_kernel, hops),
        steps,
        None,
        tiled(local, lead, reduced, mask) + whole(out_rate, *gots),
        tiled(t(own), t(own), t(own)),
        [((8, own), F32)],
        [act],
    )
    mixed_y = wa_swap(after(mixed, cot_y), 2)
    mixed_c = wa_swap(mixed, 1)
    cot_yc = wa_swap(after(cot_y, mixed), 1)
    cots = [cotangent, cot_c, cot_y, cot_yc]

    c_high, c_low, grad_product, ge_high, ge_low, back_send, c_sum = call(
        17,
        cotangent_kernel,
        steps,
        ids,
        tiled(*cots) + whole(w_down) + tiled(act) + whole(w_expand),
        tiled(
            t(width, dtype=BF16), t(width, dtype=BF16), t(units), t(units, dtype=BF16), t(units, dtype=BF16),
            t(2 * own),
        )
        + whole(shape(8, width)),
        [((width, units), BF16)] * 2 + [((2 * own, units), BF16)] * 2,
        [mixed],
    )
    back_recv = wa_swap(back_send, 1)
    back_keep, ge_sum = call(
        FILL,
        back_kernel,
        steps,
        ids,
        tiled(ge_high, ge_low) + whole(w_expand),
        tiled(t(2 * own)) + whole(shape(8, units)),
        [((2 * own, units), BF16)] * 2,
        [back_send],
    )
    back_far = back_keep[:, :own] + back_recv[:, :own]
    back_y = wa_swap(back_far, 2)

    mixed_yc = wa_swap(after(mixed_y, back_keep), 1)
    m_high, m_low, p_high, p_low, gg_high, gg_low, out_send, out_keep, gg_sum = call(
        14,
        expand_kernel,
        steps,
        ids,
        tiled(mixed, mixed_c, mixed_y, mixed_yc)
        + whole(w_expand, b_exp, w_down)
        + tiled(act, slope, grad_product),
        tiled(
            t(channels, dtype=BF16), t(channels, dtype=BF16), t(units, dtype=BF16), t(units, dtype=BF16),
            t(units, dtype=BF16), t(units, dtype=BF16), t(part), t(part),
        )
        + whole(shape(8, units)),
        [((channels, units), BF16)] * 2 + [((2 * part, units), BF16)] * 2,
        [back_far],
    )
    out_recv = wa_swap(out_send, 1)
    near_send, near_keep = call(
        6.5,
        output_kernel,
        steps,
        ids,
        tiled(p_high, p_low)
        + whole(w_down)
        + [(inputs, tiles(inputs, column=part)), (b_down_row, pl.BlockSpec((1, part), lambda i, ids: (0, ids[0])))],
        tiled(t(part), t(part)),
        [((2 * part, units), BF16)] * 2,
        [out_send],
    )
    out_far = after(out_keep, near_keep) + out_recv
    out_y = wa_swap(out_far, 2)
    near_recv = wa_swap(near_send, 1)

    def backwards(*arrays):
        return [(a, tiles(a, True)) for a in arrays]

    local_back, tail, back_end, out_sum = call(
        1.5,
        adjoint_kernel,
        steps,
        None,
        backwards(back_keep, back_recv, back_y, states, mask) + whole(out_rate, rate, step),
        backwards(t(own), t(own)) + whole(shape(8, own), shape(8, own)),
        [((16, own), F32)],
        [near_keep],
    )
    back_gots = [seq_shift(back_end, -hop) for hop in range(1, hops + 1)]

    def weight(left, right, ids, relative, deps):
        blocks = left[0].shape[1] // seqs
        half = shape(seqs // 2, blocks, right[0].shape[1])
        tile = 2 * TILE
        return call(
            10,
            functools.partial(weight_kernel, relative),
            rows // tile,
            ids,
            [(a, tiles(a, tile=tile)) for a in (*left, *right)],
            whole(half, half),
            [((left[0].shape[1], right[0].shape[1]), F32)],
            deps,
        )

    w_down_keep, w_down_send = weight((c_high, c_low), (p_high, p_low), ids, True, [back_end, out_far])
    down_sum = ScatterSum(w_down_keep, after(w_down_send, *back_gots), (1, 2, 4))
    r_high, r_low, far_send, far_keep, turn_sum, red_sum, far_norm = call(
        8,
        functools.partial(normed_far_kernel, hops),
        steps,
        ids,
        tiled(local_back, tail, turn, red_slope, gg_high, gg_low, inputs)
        + whole(w_gate, w_reduce, rate, step)
        + whole(*back_gots),
        tiled(t(own, dtype=BF16), t(own, dtype=BF16), t(part), t(part))
        + whole(shape(8, own), shape(8, own), shape(16, width)),
        [((2 * part, units), BF16)] * 2 + [((2 * part, own), BF16)] * 2 + [((TILE, width), F32)],
        [w_down_keep],
    )
    far_recv = wa_swap(far_send, 1)
    next_send, next_keep, norm = call(
        7,
        normed_near_kernel,
        steps,
        ids,
        tiled(r_high, r_low, gg_high, gg_low, inputs) + whole(w_gate, w_reduce, far_norm),
        tiled(t(part), t(part)) + whole(shape(8, width)),
        [((2 * part, units), BF16)] * 2
        + [((2 * part, own), BF16)] * 2
        + [((TILE, width), F32), ((16, width), F32)],
        [far_keep],
    )
    far_sum = after(far_keep, next_keep) + far_recv
    far_y = wa_swap(far_sum, 2)
    next_recv = wa_swap(next_send, 1)
    near_sum = after(next_keep, far_sum) + next_recv
    norm_c = wa_swap(norm, 1)
    norm_y = wa_swap(norm, 2)
    norm_yc = wa_swap(norm, 3)

    w_gate_keep, w_gate_send = weight((n_high, n_low), (gg_high, gg_low), ids_z, False, [near_sum])
    gate_total = ScatterSum(w_gate_keep, w_gate_send, (2, 1, 4))
    output = after(near_keep, w_gate_keep) + near_recv + out_y
    w_expand_keep, w_expand_send = weight((m_high, m_low), (ge_high, ge_low), ids, True, [output])
    expand_total = ScatterSum(w_expand_keep, w_expand_send, (1, 2, 4))

    [vector] = call(
        1.5,
        pack_kernel,
        1,
        None,
        whole(norm, norm_c, norm_y, norm_yc, c_sum, gg_sum, ge_sum, red_sum, turn_sum, out_sum),
        whole(shape(8 * seqs, 128)),
        [((8, max(width, units)), F32), ((8, width), F32)],
        [w_expand_keep],
    )
    half = shape(seqs // 2, width // seqs + 8, own)
    w_red_keep, w_red_send = call(
        5,
        reduce_weight_kernel,
        steps,
        ids,
        tiled(n_high, n_low, r_high, r_low) + whole(vector),
        whole(half, half),
        [((width, own), F32)],
        [w_expand_keep],
    )
    reduce_total = ScatterSum(w_red_keep, w_red_send, (1, 2, 4))

    token = down_sum.step(2, w_red_keep)
    grad_own = after(near_sum, token) + far_y
    all_y = wa_swap(grad_own, 2)
    all_c = wa_swap(grad_own, 1)
    all_yc = wa_swap(all_y, 1)
    token = gate_total.step(1, grad_own)
    token = expand_total.step(2, token)
    token = reduce_total.step(2, token)
    token = down_sum.step(4, token)
    token = gate_total.step(4, token)
    token = expand_total.step(4, token)
    token = reduce_total.step(4, token)

    total_w_down = down_sum.finish()
    total_w_gate = gate_total.finish()
    total_w_expand = expand_total.finish()
    total = reduce_total.finish()
    matrix_rows = width // seqs

    def vector_of(k, length):
        return total[matrix_rows + k, : length // seqs]

    count = own // seqs
    rate_here = lax.dynamic_slice_in_dim(ssm_rate, place * count, count, 0)
    step_here = lax.dynamic_slice_in_dim(ssm_step, place * count, count, 0)
    keep_sum = vector_of(6, own)
    grad_log = -keep_sum * jnp.exp(-rate_here * step_here)
    [grad_inputs] = call(
        9,
        final_kernel,
        steps,
        ids,
        tiled(inputs) + whole(gain) + tiled(grad_own, all_c, all_y, all_yc, *cots),
        tiled(t(width)),
        [((TILE, width), F32)] * 2,
    )
    return (
        output,
        grad_inputs,
        vector_of(0, width),
        vector_of(1, width),
        total_w_gate,
        vector_of(3, units),
        total[:matrix_rows],
        vector_of(5, own),
        grad_log * step_here,
        grad_log * rate_here,
        vector_of(7, own),
        total_w_expand,
        vector_of(4, units),
        total_w_down,
        vector_of(2, width),
    )


def solution(mesh):
    in_specs = (
        P("seq", None),
        P("seq"),
        P(),
        P(),
        P(None, "wa"),
        P("wa"),
        P(None, "wa"),
        P("wa"),
        P("wa"),
        P("wa"),
        P("wa"),
        P(None, "wa"),
        P("wa"),
        P(None, "wa"),
        P(),
        P("seq", "wa"),
    )
    out_specs = (
        P("seq", "wa"),
        P("seq", None),
        P("seq"),
        P("seq"),
        P("seq", "wa"),
        P(("wa", "seq")),
        P("seq", "wa"),
        P(("wa", "seq")),
        P(("wa", "seq")),
        P(("wa", "seq")),
        P(("wa", "seq")),
        P("seq", "wa"),
        P(("wa", "seq")),
        P("seq", "wa"),
        P("seq"),
    )
    return jax.shard_map(body, mesh=mesh, in_specs=in_specs, out_specs=out_specs, check_vma=False)
```

time: 907 us -> 339 us (0.37)
  waiting for transfers between devices: 329 us -> 109 us
  other arithmetic: 204 us -> 18.9 us
  matrix products: 183 us -> 0 us
  Pallas kernels: 0 us -> 114 us
  blocking collectives: 92.9 us -> 0 us
  starting transfers between devices: 0.37 us -> 48.4 us
  local copies, waits for them, and re-layouts: 63.2 us -> 44.8 us
  between operations: 17.7 us -> 1.52 us
    reduce_scatter x6 -> x0, waiting for transfers between devices: 289 us -> none  [the longest x1 77.6 us: body(): lax.psum_scatter(grad_w_gate, 'seq', scatter_dimension=0, tiled=True)]
    dot_general x12 -> x0, matrix products: 183 us -> none  [the longest x4 67.9 us: contract_rows(): lax.dot_general(left, right, (((0,), (0,)), ((), ())), precision=HIGHEST)]
    dot_general x24 -> x0, other arithmetic: 139 us -> none  [advance(): within = jnp.einsum('tsh,sh->th', kernel, block_in, precision=HIGHEST)]
    pallas_call x0 -> x16, Pallas kernels: none -> 114 us  [call(): return run(*arrays) if ids is None else run(ids, *arrays)]
    ppermute x0 -> x38, waiting for transfers between devices: none -> 109 us  [the longest x20 56.6 us: wa_swap(): return lax.ppermute(value, 'wa', [(i, i ^ distance) for i in range(count)])]
    all_gather x3 -> x0, blocking collectives: 55 us -> none  [prefix(): gathered = jax.tree.map(lambda a: lax.all_gather(a, axis), part)]
    ppermute x0 -> x38, starting transfers between devices: none -> 48.4 us  [the longest x12 23.9 us: seq_swap(): return lax.ppermute(value, 'seq', [(i, i ^ distance) for i in range(count)])]
    unnamed x1 -> x0, blocking collectives: 38 us -> none
  transfers between devices with their start and end apart: 9 -> 38, of which waited for: 7 -> 13; matrix products, arithmetic and copies ran while one was open for 41% -> 6% of each run, Pallas kernels for 0% -> 25%
where the time goes in v1:
time: 339 us; the launch traced here: 336 us
  Pallas kernels  114 us (34%)
  waiting for transfers between devices  109 us (32%)
  starting transfers between devices  48.4 us (14%)
  local copies, waits for them, and re-layouts  44.8 us (13%)
  other arithmetic  18.9 us (6%)
    pallas_call x16, Pallas kernels, call(): return run(*arrays) if ids is None else run(ids, *arrays)  114 us
    ppermute x20, waiting for transfers between devices, wa_swap(): return lax.ppermute(value, 'wa', [(i, i ^ distance) for i in range(count)])  56.6 us
    ppermute x12, waiting for transfers between devices, seq_swap(): return lax.ppermute(value, 'seq', [(i, i ^ distance) for i in range(count)])  52.1 us
    unnamed x150, local copies, waits for them, and re-layouts  42.3 us
    ppermute x12, starting transfers between devices, seq_swap(): return lax.ppermute(value, 'seq', [(i, i ^ distance) for i in range(count)])  23.9 us
    ppermute x6, starting transfers between devices, seq_shift(): return lax.ppermute(value, 'seq', pairs)  15.7 us
    ppermute x20, starting transfers between devices, wa_swap(): return lax.ppermute(value, 'wa', [(i, i ^ distance) for i in range(count)])  8.82 us
  transfers between devices with their start and end apart: 38, of which 13 were waited for; matrix products, arithmetic and copies ran while one was open for 6% of the time, Pallas kernels for 25%

profile of v1, /device:TPU:0, one launch (start us, length us, event | category | flops | bytes accessed | tf_op | source)
XLA Modules:
  0.0 336.0 jit_solution(17986954090667652614)
XLA Ops:
  12.1 7.0 %shard_map.289 = (bf16[1536,1024]{1,0:T(8,128)(2,1)S(1)}, bf16[1536,1024]{1,0:T(8,128)(2,1)S(1)}, f32[1536,128]{1,0:T(8,128)S(1)}, f32[1536,128]{1,0:T(8,128)S(1...) custom-call(f32[1536,1024]{1,0:T(8,128)S(1)} %copy-done, f32[1,1024]{1,0:T(1,128)S(1)} %bitcast.41, ...), custom_call_target="tpu_custom_call" | custom-call | flops 350000000 | bytes 700000 | tf_op jit(solution)/shard_map/pallas_call | solution.py:505
  27.0 4.5 %collective-permute-start.2 = (f32[8,128]{1,0:T(8,128)S(1)}, f32[8,128]{1,0:T(8,128)S(1)}, u32[]{:S(2)}, u32[]{:S(2)}) collective-permute-start(f32[8,128]{1,0:T(8,128)S(1)} %get-tuple-element.89), channel_id=1, source_target_pairs={{0,12},{4,16},{8,20},{12,24},{16,28},{1,13},{5,17},{9,21},{13,25},... | collective-permute-start | bytes 12296 | tf_op jit(solution)/shard_map/ppermute | solution.py:525
  31.6 11.7 %shard_map.290 = (f32[1536,768]{1,0:T(8,128)S(1)}, f32[1536,768]{1,0:T(8,128)S(1)}) custom-call(bf16[1536,1024]{1,0:T(8,128)(2,1)S(1)} %get-tuple-element.90.refs_0_.refs_1_, bf16[1536,1024]{1,0:T(8,128)(2,1)S(1)} %get-tuple-element.91.refs_1_.refs_2_, f32[1024,768]{1,0:T(8,128)S(1)} %copy-done.3, f32[1,768]{1,0:T(1,128)S(1)} %broadcast_in_dim.40.refs_3_), custom_call_target="tpu_custom_call" | custom-call | flops 600000000 | bytes 1200000 | tf_op jit(solution)/shard_map/pallas_call | solution.py:505
  51.5 3.8 %collective-permute-done.7.refs_4_.refs_10_ = f32[1536,256]{1,0:T(8,128)} collective-permute-done((f32[1536,256]{1,0:T(8,128)}, f32[1536,256]{1,0:T(8,128)}, u32[]{:S(2)}, u32[]{:S(2)}) %collective-permute-start.7) | collective-permute-done | bytes 1572896 | tf_op jit(solution)/shard_map/ppermute | solution.py:514
  59.7 16.2 %shard_map.292 = (bf16[1536,1024]{1,0:T(8,128)(2,1)S(1)}, bf16[1536,1024]{1,0:T(8,128)(2,1)S(1)}, f32[1536,768]{1,0:T(8,128)S(1)}, bf16[1536,768]{1,0:T(8,128)(2...) custom-call(s32[10]{0:T(128)S(1)} %pad_add_fusion.refs_0_, ...), custom_call_target="tpu_custom_call" | custom-call | flops 850000000 | bytes 1700000 | tf_op jit(solution)/shard_map/pallas_call | solution.py:505
  81.8 4.3 %shard_map.293 = (f32[1536,256]{1,0:T(8,128)S(1)}, f32[8,768]{1,0:T(8,128)S(1)}) custom-call(s32[10]{0:T(128)S(1)} %pad_add_fusion.refs_0_, bf16[1536,768]{1,0:T(8,128)(2,1)S(1)} %get-tuple-element.96.refs_1_.refs_3_, bf16[1536,768]{1,0:T(8,128)(2,1)S(1)} %get-tuple-element.97.refs_2_.refs_4_, f32[512,768]{1,0:T(8,128)S(1)} %copy-done.22, ...), custom_call_target="tpu_custom_call" | custom-call | flops 20000000000 | bytes 40000000 | tf_op jit(solution)/shard_map/pallas_call | solution.py:505
  93.2 13.3 %shard_map.294 = (bf16[1536,512]{1,0:T(8,128)(2,1)S(1)}, bf16[1536,512]{1,0:T(8,128)(2,1)S(1)}, bf16[1536,768]{1,0:T(8,128)(2,1)S(1)}, bf16[1536,768]{1,0:T(8,12...) custom-call(s32[10]{0:T(128)S(1)} %pad_add_fusion.refs_0_, ...), custom_call_target="tpu_custom_call" | custom-call | flops 700000000 | bytes 1400000 | tf_op jit(solution)/shard_map/pallas_call | solution.py:505
  115.6 5.9 %shard_map.295 = (f32[1536,256]{1,0:T(8,128)S(1)}, f32[1536,256]{1,0:T(8,128)S(1)}) custom-call(s32[10]{0:T(128)S(1)} %pad_add_fusion.refs_0_, bf16[1536,768]{1,0:T(8,128)(2,1)S(1)} %copy-done.18, bf16[1536,768]{1,0:T(8,128)(2,1)S(1)} %get-tuple-element.104.refs_2_.refs_4_, f32[1024,768]{1,0:T(8,128)S(1)} %copy-done.10, f32[1536,1024]{1,0:T(8,128)S(1)} %bitcast.38, ...), custom_call_target="tpu_custom_call" | custom-call | flops 325000000 | bytes 650000 | tf_op jit(solution)/shard_map/pallas_call | solution.py:505
  122.6 7.6 %collective-permute-done.10.refs_2_ = f32[1536,128]{1,0:T(8,128)S(1)} collective-permute-done((f32[1536,128]{1,0:T(8,128)S(1)}, f32[1536,128]{1,0:T(8,128)S(1)}, u32[]{:S(2)}, u32[]{:S(2)}) %collective-permute-start.10) | collective-permute-done | bytes 786464 | tf_op jit(solution)/shard_map/ppermute | solution.py:514
  138.0 9.1 %shard_map.297 = (f32[4,128,768]{2,1,0:T(8,128)S(1)}, f32[4,128,768]{2,1,0:T(8,128)S(1)}) custom-call(s32[10]{0:T(128)S(1)} %pad_add_fusion.refs_0_, bf16[1536,1024]{1,0:T(8,128)(2,1)S(1)} %copy-done.36, bf16[1536,1024]{1,0:T(8,128)(2,1)S(1)} %copy-done.38, bf16[1536,768]{1,0:T(8,128)(2,1)S(1)} %copy-done.19, ...), custom_call_target="tpu_custom_call" | custom-call | flops 500000000 | bytes 1000000 | tf_op jit(solution)/shard_map/pallas_call | solution.py:505
  147.1 7.9 %shard_map.298 = (bf16[1536,128]{1,0:T(8,128)(2,1)S(1)}, bf16[1536,128]{1,0:T(8,128)(2,1)S(1)}, f32[1536,256]{1,0:T(8,128)S(1)}, f32[1536,256]{1,0:T(8,128)S(1)}...) custom-call(s32[10]{0:T(128)S(1)} %pad_add_fusion.refs_0_, ...), custom_call_target="tpu_custom_call" | custom-call | flops 400000000 | bytes 800000 | tf_op jit(solution)/shard_map/pallas_call | solution.py:505
  155.2 7.2 %shard_map.299 = (f32[1536,256]{1,0:T(8,128)S(1)}, f32[1536,256]{1,0:T(8,128)S(1)}, f32[8,1024]{1,0:T(8,128)S(1)}) custom-call(s32[10]{0:T(128)S(1)} %pad_add_fusion.refs_0_, bf16[1536,128]{1,0:T(8,128)(2,1)S(1)} %get-tuple-element.120.refs_1_.refs_3_, bf16[1536,128]{1,0:T(8,128)(2,1)S(1)} %get-tuple-element.121.refs_2_.refs_4_, ...), custom_call_target="tpu_custom_call" | custom-call | flops 350000000 | bytes 700000 | tf_op jit(solution)/shard_map/pallas_call | solution.py:505
  169.1 9.1 %shard_map.300 = (f32[4,128,768]{2,1,0:T(8,128)S(1)}, f32[4,128,768]{2,1,0:T(8,128)S(1)}) custom-call(s32[10]{0:T(128)S(1)} %pad_add_fusion.2.refs_0_, bf16[1536,1024]{1,0:T(8,128)(2,1)S(1)} %copy-done.5, bf16[1536,1024]{1,0:T(8,128)(2,1)S(1)} %copy-done.7, bf16[1536,768]{1,0:T(8,128)(2,1)S(1)} %copy-done.12, bf16[1536,768]{1,0:T(8,128)(2,1)S(1)} %copy-done.14, ...), custom_call_target="tpu_custom_call" | custom-call | flops 500000000 | bytes 1000000 | tf_op jit(solution)/shard_map/pallas_call | solution.py:505
  181.5 18.9 %collective-permute-done.18 = f32[1536,256]{1,0:T(8,128)} collective-permute-done((f32[1536,256]{1,0:T(8,128)S(1)}, f32[1536,256]{1,0:T(8,128)}, u32[]{:S(2)}, u32[]{:S(2)}) %collective-permute-start.18) | collective-permute-done | bytes 1572896 | tf_op jit(solution)/shard_map/ppermute | solution.py:514
  203.2 6.0 %shard_map.301 = (f32[4,64,768]{2,1,0:T(8,128)S(1)}, f32[4,64,768]{2,1,0:T(8,128)}) custom-call(s32[10]{0:T(128)S(1)} %pad_add_fusion.refs_0_, bf16[1536,512]{1,0:T(8,128)(2,1)S(1)} %copy-done.44, bf16[1536,512]{1,0:T(8,128)(2,1)S(1)} %copy-done.46, bf16[1536,768]{1,0:T(8,128)(2,1)S(1)} %copy-done.40, bf16[1536,768]{1,0:T(8,128)(2,1)S(1)} %copy-done.42, ...), custom_call_target="tpu_custom_call" | custom-call | flops 500000000 | bytes 1000000 | tf_op jit(solution)/shard_map/pallas_call | solution.py:505
  213.5 20.7 %collective-permute-done.21.refs_2_ = f32[8,1024]{1,0:T(8,128)S(1)} collective-permute-done((f32[8,1024]{1,0:T(8,128)S(1)}, f32[8,1024]{1,0:T(8,128)S(1)}, u32[]{:S(2)}, u32[]{:S(2)}) %collective-permute-start.21) | collective-permute-done | bytes 32800 | tf_op jit(solution)/shard_map/ppermute | solution.py:514
  237.8 4.8 %shard_map.303 = (f32[4,136,128]{2,1,0:T(8,128)S(1)}, f32[4,136,128]{2,1,0:T(8,128)S(1)}) custom-call(s32[10]{0:T(128)S(1)} %pad_add_fusion.refs_0_, bf16[1536,1024]{1,0:T(8,128)(2,1)S(1)} %copy-done.5, bf16[1536,1024]{1,0:T(8,128)(2,1)S(1)} %copy-done.7, bf16[1536,128]{1,0:T(8,128)(2,1)S(1)} %get-tuple-element.120.refs_1_.refs_3_, ...), custom_call_target="tpu_custom_call" | custom-call | flops 250000000 | bytes 500000 | tf_op jit(solution)/shard_map/pallas_call | solution.py:505
  244.0 4.2 %collective-permute-start.33 = (f32[2,128,768]{2,1,0:T(8,128)}, f32[2,128,768]{2,1,0:T(8,128)}, u32[]{:S(2)}, u32[]{:S(2)}) collective-permute-start(f32[2,128,768]{2,1,0:T(8,128)} %get-tuple-element.160), channel_id=1, source_target_pairs={{0,8},{4,12},{8,0},{12,4},{16,24},{20,28},{24,16},{28,20},{1,9},{5... | collective-permute-start | bytes 2359304 | tf_op jit(solution)/shard_map/ppermute | solution.py:519
  254.6 21.7 %collective-permute-done.27 = f32[4,136,128]{2,1,0:T(8,128)} collective-permute-done((f32[4,136,128]{2,1,0:T(8,128)S(1)}, f32[4,136,128]{2,1,0:T(8,128)}, u32[]{:S(2)}, u32[]{:S(2)}) %collective-permute-start.27) | collective-permute-done | bytes 278560 | tf_op jit(solution)/shard_map/ppermute | solution.py:519
  280.5 4.1 %collective-permute-start.37 = (f32[1,128,768]{2,1,0:T(8,128)S(1)}, f32[1,128,768]{2,1,0:T(8,128)S(1)}, u32[]{:S(2)}, u32[]{:S(2)}) collective-permute-start(f32[1,128,768]{2,1,0:T(8,128)S(1)} %slice_add_fusion.7), channel_id=1, source_target_pairs={{0,16},{4,20},{8,24},{12,28},{16,0},{20,4},{24,8},{28,12},{1,17},{... | collective-permute-start | bytes 1179656 | tf_op jit(solution)/shard_map/ppermute | solution.py:519
  285.6 10.4 %collective-permute-done.31 = f32[2,64,768]{2,1,0:T(8,128)S(1)} collective-permute-done((f32[2,64,768]{2,1,0:T(8,128)S(1)}, f32[2,64,768]{2,1,0:T(8,128)S(1)}, u32[]{:S(2)}, u32[]{:S(2)}) %collective-permute-start.31) | collective-permute-done | bytes 393248 | tf_op jit(solution)/shard_map/ppermute | solution.py:519
  307.5 7.1 %collective-permute-done.36 = f32[1,64,768]{2,1,0:T(8,128)S(1)} collective-permute-done((f32[1,64,768]{2,1,0:T(8,128)S(1)}, f32[1,64,768]{2,1,0:T(8,128)S(1)}, u32[]{:S(2)}, u32[]{:S(2)}) %collective-permute-start.36) | collective-permute-done | bytes 196640 | tf_op jit(solution)/shard_map/ppermute | solution.py:519
  315.3 9.7 %collective-permute-done.35 = f32[1,128,768]{2,1,0:T(8,128)S(1)} collective-permute-done((f32[1,128,768]{2,1,0:T(8,128)S(1)}, f32[1,128,768]{2,1,0:T(8,128)S(1)}, u32[]{:S(2)}, u32[]{:S(2)}) %collective-permute-start.35) | collective-permute-done | bytes 393248 | tf_op jit(solution)/shard_map/ppermute | solution.py:519
  326.9 9.1 %shard_map.304 = f32[1536,1024]{1,0:T(8,128)} custom-call(s32[10]{0:T(128)S(1)} %pad_add_fusion.refs_0_, f32[1536,1024]{1,0:T(8,128)S(1)} %bitcast.40, f32[1,1024]{1,0:T(1,128)S(1)} %bitcast.42, f32[1536,256]{1,0:T(8,128)S(1)} %copy-done.21, f32[1536,256]{1,0:T(8,128)S(1)} %collective-permute-done.24.refs_4_, ...), custom_call_target="tpu_custom_call" | custom-call | flops 450000000 | bytes 900000 | tf_op jit(solution)/shard_map/pallas_call | solution.py:505
  (252 shorter events, 110.1 us)
Async XLA Ops:
  0.6 49.7 %collective-permute-start.4 = (f32[1536,256]{1,0:T(8,128)}, f32[1536,256]{1,0:T(8,128)}, u32[]{:S(2)}, u32[]{:S(2)}) collective-permute-start(f32[1536,256]{1,0:T(8,128)} %refs_7_.9), channel_id=1, source_target_pairs={{0,2},{1,3},{2,0},{3,1},{4,6},{5,7},{6,4},{7,5},{8,10},{9,11},{10,... | collective-permute-start | bytes 4718600 | tf_op jit(solution)/shard_map/ppermute | solution.py:514
  20.1 25.4 %collective-permute-start = (f32[8,128]{1,0:T(8,128)S(1)}, f32[8,128]{1,0:T(8,128)S(1)}, u32[]{:S(2)}, u32[]{:S(2)}) collective-permute-start(f32[8,128]{1,0:T(8,128)S(1)} %get-tuple-element.89), channel_id=1, source_target_pairs={{0,4},{4,8},{8,12},{12,16},{16,20},{20,24},{24,28},{1,5},{5,9},{9,... | collective-permute-start | bytes 12296 | tf_op jit(solution)/shard_map/ppermute | solution.py:525
  23.5 22.0 %collective-permute-start.1 = (f32[8,128]{1,0:T(8,128)S(1)}, f32[8,128]{1,0:T(8,128)S(1)}, u32[]{:S(2)}, u32[]{:S(2)}) collective-permute-start(f32[8,128]{1,0:T(8,128)S(1)} %get-tuple-element.89), channel_id=1, source_target_pairs={{0,8},{4,12},{8,16},{12,20},{16,24},{20,28},{1,9},{5,13},{9,17},{1... | collective-permute-start | bytes 12296 | tf_op jit(solution)/shard_map/ppermute | solution.py:525
  31.5 20.0 %collective-permute-start.6 = (f32[1536,256]{1,0:T(8,128)}, f32[1536,256]{1,0:T(8,128)}, u32[]{:S(2)}, u32[]{:S(2)}) collective-permute-start(f32[1536,256]{1,0:T(8,128)} %refs_7_.9), channel_id=1, source_target_pairs={{0,1},{1,0},{2,3},{3,2},{4,5},{5,4},{6,7},{7,6},{8,9},{9,8},{10,11... | collective-permute-start | bytes 4718600 | tf_op jit(solution)/shard_map/ppermute | solution.py:514
  50.9 36.7 %collective-permute-start.3 = (f32[1536,128]{1,0:T(8,128)}, f32[1536,128]{1,0:T(8,128)S(1)}, u32[]{:S(2)}, u32[]{:S(2)}) collective-permute-start(f32[1536,128]{1,0:T(8,128)} %copy-done.32), channel_id=1, source_target_pairs={{0,1},{1,0},{2,3},{3,2},{4,5},{5,4},{6,7},{7,6},{8,9},{9,8},{10,11... | collective-permute-start | bytes 2359304 | tf_op jit(solution)/shard_map/ppermute | solution.py:514
  50.9 35.2 %collective-permute-start.5 = (f32[1536,128]{1,0:T(8,128)}, f32[1536,128]{1,0:T(8,128)S(1)}, u32[]{:S(2)}, u32[]{:S(2)}) collective-permute-start(f32[1536,128]{1,0:T(8,128)} %copy-done.32), channel_id=1, source_target_pairs={{0,2},{1,3},{2,0},{3,1},{4,6},{5,7},{6,4},{7,5},{8,10},{9,11},{10,... | collective-permute-start | bytes 2359304 | tf_op jit(solution)/shard_map/ppermute | solution.py:514
  110.3 26.0 %collective-permute-start.14 = (f32[1536,256]{1,0:T(8,128)S(1)}, f32[1536,256]{1,0:T(8,128)}, u32[]{:S(2)}, u32[]{:S(2)}) collective-permute-start(f32[1536,256]{1,0:T(8,128)S(1)} %get-tuple-element.105.refs_6_), channel_id=1, source_target_pairs={{0,1},{1,0},{2,3},{3,2},{4,5},{5,4},{6,7},{7,6},{8,9},{9,8},{10,11... | collective-permute-start | bytes 4718600 | tf_op jit(solution)/shard_map/ppermute | solution.py:514
  110.3 20.0 %collective-permute-start.10 = (f32[1536,128]{1,0:T(8,128)S(1)}, f32[1536,128]{1,0:T(8,128)S(1)}, u32[]{:S(2)}, u32[]{:S(2)}) collective-permute-start(f32[1536,128]{1,0:T(8,128)S(1)} %slice_add_fusion.refs_11_), channel_id=1, source_target_pairs={{0,2},{1,3},{2,0},{3,1},{4,6},{5,7},{6,4},{7,5},{8,10},{9,11},{10,... | collective-permute-start | bytes 2359304 | tf_op jit(solution)/shard_map/ppermute | solution.py:514
  163.0 18.5 %collective-permute-start.17 = (f32[1536,256]{1,0:T(8,128)S(1)}, f32[1536,256]{1,0:T(8,128)S(1)}, u32[]{:S(2)}, u32[]{:S(2)}) collective-permute-start(f32[1536,256]{1,0:T(8,128)S(1)} %copy-done.64), channel_id=1, source_target_pairs={{0,1},{1,0},{2,3},{3,2},{4,5},{5,4},{6,7},{7,6},{8,9},{9,8},{10,11... | collective-permute-start | bytes 4718600 | tf_op jit(solution)/shard_map/ppermute | solution.py:514
  163.0 37.3 %collective-permute-start.18 = (f32[1536,256]{1,0:T(8,128)S(1)}, f32[1536,256]{1,0:T(8,128)}, u32[]{:S(2)}, u32[]{:S(2)}) collective-permute-start(f32[1536,256]{1,0:T(8,128)S(1)} %add.86.refs_6_), channel_id=1, source_target_pairs={{0,2},{1,3},{2,0},{3,1},{4,6},{5,7},{6,4},{7,5},{8,10},{9,11},{10,... | collective-permute-start | bytes 4718600 | tf_op jit(solution)/shard_map/ppermute | solution.py:514
  163.5 79.2 %collective-permute-start.19 = (f32[4,128,768]{2,1,0:T(8,128)S(1)}, f32[4,128,768]{2,1,0:T(8,128)S(1)}, u32[]{:S(2)}, u32[]{:S(2)}) collective-permute-start(f32[4,128,768]{2,1,0:T(8,128)S(1)} %get-tuple-element.133), channel_id=1, source_target_pairs={{0,4},{4,0},{8,12},{12,8},{16,20},{20,16},{24,28},{28,24},{1,5},{5... | collective-permute-start | bytes 4718600 | tf_op jit(solution)/shard_map/ppermute | solution.py:519
  166.4 81.8 %collective-permute-start.23 = (f32[1536,256]{1,0:T(8,128)S(1)}, f32[1536,256]{1,0:T(8,128)S(1)}, u32[]{:S(2)}, u32[]{:S(2)}) collective-permute-start(f32[1536,256]{1,0:T(8,128)S(1)} %add.87), channel_id=1, source_target_pairs={{0,2},{1,3},{2,0},{3,1},{4,6},{5,7},{6,4},{7,5},{8,10},{9,11},{10,... | collective-permute-start | bytes 4718600 | tf_op jit(solution)/shard_map/ppermute | solution.py:514
  178.2 71.4 %collective-permute-start.29 = (f32[4,128,768]{2,1,0:T(8,128)S(1)}, f32[4,128,768]{2,1,0:T(8,128)S(1)}, u32[]{:S(2)}, u32[]{:S(2)}) collective-permute-start(f32[4,128,768]{2,1,0:T(8,128)S(1)} %get-tuple-element.149), channel_id=1, source_target_pairs={{0,8},{4,12},{8,0},{12,4},{16,24},{20,28},{24,16},{28,20},{1,9},{5... | collective-permute-start | bytes 4718600 | tf_op jit(solution)/shard_map/ppermute | solution.py:519
  209.2 44.2 %collective-permute-start.28 = (f32[4,64,768]{2,1,0:T(8,128)}, f32[4,64,768]{2,1,0:T(8,128)}, u32[]{:S(2)}, u32[]{:S(2)}) collective-permute-start(f32[4,64,768]{2,1,0:T(8,128)} %get-tuple-element.148), channel_id=1, source_target_pairs={{0,4},{4,0},{8,12},{12,8},{16,20},{20,16},{24,28},{28,24},{1,5},{5... | collective-permute-start | bytes 2359304 | tf_op jit(solution)/shard_map/ppermute | solution.py:519
  213.1 21.1 %collective-permute-start.21 = (f32[8,1024]{1,0:T(8,128)S(1)}, f32[8,1024]{1,0:T(8,128)S(1)}, u32[]{:S(2)}, u32[]{:S(2)}) collective-permute-start(f32[8,1024]{1,0:T(8,128)S(1)} %get-tuple-element.134.refs_0_), channel_id=1, source_target_pairs={{0,2},{1,3},{2,0},{3,1},{4,6},{5,7},{6,4},{7,5},{8,10},{9,11},{10,... | collective-permute-start | bytes 98312 | tf_op jit(solution)/shard_map/ppermute | solution.py:514
  244.0 33.7 %collective-permute-start.33 = (f32[2,128,768]{2,1,0:T(8,128)}, f32[2,128,768]{2,1,0:T(8,128)}, u32[]{:S(2)}, u32[]{:S(2)}) collective-permute-start(f32[2,128,768]{2,1,0:T(8,128)} %get-tuple-element.160), channel_id=1, source_target_pairs={{0,8},{4,12},{8,0},{12,4},{16,24},{20,28},{24,16},{28,20},{1,9},{5... | collective-permute-start | bytes 2359304 | tf_op jit(solution)/shard_map/ppermute | solution.py:519
  250.9 29.6 %collective-permute-start.32 = (f32[2,128,768]{2,1,0:T(8,128)}, f32[2,128,768]{2,1,0:T(8,128)}, u32[]{:S(2)}, u32[]{:S(2)}) collective-permute-start(f32[2,128,768]{2,1,0:T(8,128)} %get-tuple-element.162), channel_id=1, source_target_pairs={{0,4},{4,0},{8,12},{12,8},{16,20},{20,16},{24,28},{28,24},{1,5},{5... | collective-permute-start | bytes 2359304 | tf_op jit(solution)/shard_map/ppermute | solution.py:519
  252.6 23.7 %collective-permute-start.27 = (f32[4,136,128]{2,1,0:T(8,128)S(1)}, f32[4,136,128]{2,1,0:T(8,128)}, u32[]{:S(2)}, u32[]{:S(2)}) collective-permute-start(f32[4,136,128]{2,1,0:T(8,128)S(1)} %get-tuple-element.147), channel_id=1, source_target_pairs={{0,4},{4,0},{8,12},{12,8},{16,20},{20,16},{24,28},{28,24},{1,5},{5... | collective-permute-start | bytes 835592 | tf_op jit(solution)/shard_map/ppermute | solution.py:519
  253.0 51.7 %collective-permute-start.25 = (f32[1536,256]{1,0:T(8,128)}, f32[1536,256]{1,0:T(8,128)S(1)}, u32[]{:S(2)}, u32[]{:S(2)}) collective-permute-start(f32[1536,256]{1,0:T(8,128)} %add.92.refs_3_), channel_id=1, source_target_pairs={{0,2},{1,3},{2,0},{3,1},{4,6},{5,7},{6,4},{7,5},{8,10},{9,11},{10,... | collective-permute-start | bytes 4718600 | tf_op jit(solution)/shard_map/ppermute | solution.py:514
  253.4 73.5 %collective-permute-start.24 = (f32[1536,256]{1,0:T(8,128)}, f32[1536,256]{1,0:T(8,128)S(1)}, u32[]{:S(2)}, u32[]{:S(2)}) collective-permute-start(f32[1536,256]{1,0:T(8,128)} %add.92.refs_3_), channel_id=1, source_target_pairs={{0,1},{1,0},{2,3},{3,2},{4,5},{5,4},{6,7},{7,6},{8,9},{9,8},{10,11... | collective-permute-start | bytes 4718600 | tf_op jit(solution)/shard_map/ppermute | solution.py:514
  276.3 19.7 %collective-permute-start.31 = (f32[2,64,768]{2,1,0:T(8,128)S(1)}, f32[2,64,768]{2,1,0:T(8,128)S(1)}, u32[]{:S(2)}, u32[]{:S(2)}) collective-permute-start(f32[2,64,768]{2,1,0:T(8,128)S(1)} %get-tuple-element.164), channel_id=1, source_target_pairs={{0,8},{4,12},{8,0},{12,4},{16,24},{20,28},{24,16},{28,20},{1,9},{5... | collective-permute-start | bytes 1179656 | tf_op jit(solution)/shard_map/ppermute | solution.py:519
  277.8 19.8 %collective-permute-start.30 = (f32[2,136,128]{2,1,0:T(8,128)S(1)}, f32[2,136,128]{2,1,0:T(8,128)S(1)}, u32[]{:S(2)}, u32[]{:S(2)}) collective-permute-start(f32[2,136,128]{2,1,0:T(8,128)S(1)} %get-tuple-element.165), channel_id=1, source_target_pairs={{0,8},{4,12},{8,0},{12,4},{16,24},{20,28},{24,16},{28,20},{1,9},{5... | collective-permute-start | bytes 417800 | tf_op jit(solution)/shard_map/ppermute | solution.py:519
  302.4 22.7 %collective-permute-start.35 = (f32[1,128,768]{2,1,0:T(8,128)S(1)}, f32[1,128,768]{2,1,0:T(8,128)S(1)}, u32[]{:S(2)}, u32[]{:S(2)}) collective-permute-start(f32[1,128,768]{2,1,0:T(8,128)S(1)} %slice_add_fusion.8), channel_id=1, source_target_pairs={{0,16},{4,20},{8,24},{12,28},{16,0},{20,4},{24,8},{28,12},{1,17},{... | collective-permute-start | bytes 1179656 | tf_op jit(solution)/shard_map/ppermute | solution.py:519
  304.6 22.2 %collective-permute-start.26 = (f32[1536,256]{1,0:T(8,128)S(1)}, f32[1536,256]{1,0:T(8,128)S(1)}, u32[]{:S(2)}, u32[]{:S(2)}) collective-permute-start(f32[1536,256]{1,0:T(8,128)S(1)} %collective-permute-done.25.refs_5_), channel_id=1, source_target_pairs={{0,1},{1,0},{2,3},{3,2},{4,5},{5,4},{6,7},{7,6},{8,9},{9,8},{10,11... | collective-permute-start | bytes 4718600 | tf_op jit(solution)/shard_map/ppermute | solution.py:514
  (89 other events, 902.9 us)

commit v2 on v1

--- a/solution.py
+++ b/solution.py
@@ -12,7 +12,7 @@
 SEQ_MAX = 4096
 F32 = jnp.float32
 BF16 = jnp.bfloat16
-VMEM_LIMIT = 26 * 2**20
+VMEM_LIMIT = 22 * 2**20
 TILE = 256
 COST = 10**5
 RATE = 5 * 10**7
@@ -220,24 +220,14 @@
 
 
 def expand_kernel(
-    ids_ref, m0, m1, m2, m3, we_ref, be_ref, wd_ref, act_ref, slope_ref, gp_ref,
-    mix_high, mix_low, prod_high, prod_low, gate_high, gate_low, send_ref, keep_ref, gate_sum,
-    we_high, we_low, wd_high, wd_low,
+    ids_ref, m0, m1, m2, m3, we_ref, be_ref, act_ref, slope_ref, gp_ref,
+    mix_high, mix_low, prod_high, prod_low, gate_high, gate_low, gate_sum, we_high, we_low,
 ):
-    here = ids_ref[0]
     own = m0.shape[1]
-    width = send_ref.shape[1]
-
-    @pl.when(first_step())
-    def _():
-        for r in range(4):
-            at = pl.multiple_of((here ^ r) * own, own)
-            to = slice(r * own, (r + 1) * own)
-            we_high[to, :], we_low[to, :] = split(we_ref[pl.ds(at, own), :])
-        for place, r in enumerate((3, 2)):
-            at = pl.multiple_of((here ^ r) * width, width)
-            to = slice(place * width, (place + 1) * width)
-            wd_high[to, :], wd_low[to, :] = split(wd_ref[pl.ds(at, width), :])
+
+    @pl.when(first_step())
+    def _():
+        split_rows(ids_ref, range(4), we_ref, we_high, we_low)
 
     for r, m in enumerate((m0, m1, m2, m3)):
         at = slice(r * own, (r + 1) * own)
@@ -248,29 +238,21 @@
     gate_high[...], gate_low[...] = split(grad_gate)
     add_to(gate_sum, row_sums(grad_gate))
 
-    @apart()
-    def _():
-        out = dot3((prod_high[...], prod_low[...]), (wd_high[...], wd_low[...]), NT)
-        send_ref[...] = out[:, :width]
-        keep_ref[...] = out[:, width:]
-
 
 def output_kernel(
-    ids_ref, high_ref, low_ref, wd_ref, x_ref, b_ref, send_ref, keep_ref, wd_high, wd_low
+    ids_ref, high_ref, low_ref, wd_ref, x_ref, b_ref, far_send, far_keep, near_send, near_keep, wd_high, wd_low
 ):
-    here = ids_ref[0]
-    width = send_ref.shape[1]
-
-    @pl.when(first_step())
-    def _():
-        for place, r in enumerate((1, 0)):
-            at = pl.multiple_of((here ^ r) * width, width)
-            to = slice(place * width, (place + 1) * width)
-            wd_high[to, :], wd_low[to, :] = split(wd_ref[pl.ds(at, width), :])
+    width = near_keep.shape[1]
+
+    @pl.when(first_step())
+    def _():
+        split_rows(ids_ref, (3, 2, 1, 0), wd_ref, wd_high, wd_low)
 
     out = dot3((high_ref[...], low_ref[...]), (wd_high[...], wd_low[...]), NT)
-    send_ref[...] = out[:, :width]
-    keep_ref[...] = out[:, width:] + x_ref[...] + b_ref[...]
+    far_send[...] = out[:, :width]
+    far_keep[...] = out[:, width : 2 * width]
+    near_send[...] = out[:, 2 * width : 3 * width]
+    near_keep[...] = out[:, 3 * width :] + x_ref[...] + b_ref[...]
 
 
 def adjoint_kernel(
@@ -423,7 +405,7 @@
             to[slot, rows:] = vector_ref[pl.ds(pl.multiple_of(block * 8, 8), 8), :]
 
 
-def pack_kernel(own_ref, core_ref, far_ref, far_core_ref, down_ref, gate_ref, expand_ref, red_ref, turn_ref, out_ref,
+def pack_kernel(norm_ref, down_ref, gate_ref, expand_ref, red_ref, turn_ref, out_ref,
                 vector_ref, whole_ref, here_ref):
     count = vector_ref.shape[0] // 8
     vector_ref[...] = jnp.zeros_like(vector_ref)
@@ -432,8 +414,7 @@
     for r in range(4):
         at = pl.multiple_of((here ^ r) * width, width)
         here_ref[2:3, pl.ds(at, width)] = jnp.sum(down_ref[:, r * width : (r + 1) * width], axis=0, keepdims=True)
-    norm = (own_ref[...] + core_ref[...]) + (far_ref[...] + far_core_ref[...])
-    here_ref[0:2, :] = norm[0:2, :]
+    here_ref[0:2, :] = norm_ref[0:2, :]
     rows = [here_ref[0:1, :], here_ref[1:2, :], here_ref[2:3, :]]
     rows += [jnp.sum(ref[...], axis=0, keepdims=True) for ref in (gate_ref, expand_ref, red_ref, turn_ref, out_ref)]
     for k, row in enumerate(rows):
@@ -624,6 +605,15 @@
         [((width, own), BF16)] * 2 + [((TILE, own), F32), ((16, own), F32)],
     )
     gots = [seq_shift(end, hop) for hop in range(1, hops + 1)]
+    mixed, states, turn = call(
+        2,
+        functools.partial(states_kernel, hops),
+        steps,
+        None,
+        tiled(local, lead, reduced, mask) + whole(out_rate, *gots),
+        tiled(t(own), t(own), t(own)),
+        [((8, own), F32)],
+    )
     act, slope = call(
         12,
         gate_kernel,
@@ -632,20 +622,11 @@
         tiled(n_high, n_low) + whole(w_gate, b_gate),
         tiled(t(units), t(units)),
         [((width, units), BF16)] * 2,
-    )
-    mixed, states, turn = call(
-        2,
-        functools.partial(states_kernel, hops),
-        steps,
-        None,
-        tiled(local, lead, reduced, mask) + whole(out_rate, *gots),
-        tiled(t(own), t(own), t(own)),
-        [((8, own), F32)],
-        [act],
-    )
-    mixed_y = wa_swap(after(mixed, cot_y), 2)
+        [mixed],
+    )
+    mixed_y = wa_swap(mixed, 2)
     mixed_c = wa_swap(mixed, 1)
-    cot_yc = wa_swap(after(cot_y, mixed), 1)
+    cot_yc = wa_swap(after(cot_y, act), 1)
     cots = [cotangent, cot_c, cot_y, cot_yc]
 
     c_high, c_low, grad_product, ge_high, ge_low, back_send, c_sum = call(
@@ -660,7 +641,7 @@
         )
         + whole(shape(8, width)),
         [((width, units), BF16)] * 2 + [((2 * own, units), BF16)] * 2,
-        [mixed],
+        [act],
     )
     back_recv = wa_swap(back_send, 1)
     back_keep, ge_sum = call(
@@ -677,53 +658,20 @@
     back_y = wa_swap(back_far, 2)
 
     mixed_yc = wa_swap(after(mixed_y, back_keep), 1)
-    m_high, m_low, p_high, p_low, gg_high, gg_low, out_send, out_keep, gg_sum = call(
-        14,
+    m_high, m_low, p_high, p_low, gg_high, gg_low, gg_sum = call(
+        9,
         expand_kernel,
         steps,
         ids,
-        tiled(mixed, mixed_c, mixed_y, mixed_yc)
-        + whole(w_expand, b_exp, w_down)
-        + tiled(act, slope, grad_product),
+        tiled(mixed, mixed_c, mixed_y, mixed_yc) + whole(w_expand, b_exp) + tiled(act, slope, grad_product),
         tiled(
             t(channels, dtype=BF16), t(channels, dtype=BF16), t(units, dtype=BF16), t(units, dtype=BF16),
-            t(units, dtype=BF16), t(units, dtype=BF16), t(part), t(part),
+            t(units, dtype=BF16), t(units, dtype=BF16),
         )
         + whole(shape(8, units)),
-        [((channels, units), BF16)] * 2 + [((2 * part, units), BF16)] * 2,
+        [((channels, units), BF16)] * 2,
         [back_far],
     )
-    out_recv = wa_swap(out_send, 1)
-    near_send, near_keep = call(
-        6.5,
-        output_kernel,
-        steps,
-        ids,
-        tiled(p_high, p_low)
-        + whole(w_down)
-        + [(inputs, tiles(inputs, column=part)), (b_down_row, pl.BlockSpec((1, part), lambda i, ids: (0, ids[0])))],
-        tiled(t(part), t(part)),
-        [((2 * part, units), BF16)] * 2,
-        [out_send],
-    )
-    out_far = after(out_keep, near_keep) + out_recv
-    out_y = wa_swap(out_far, 2)
-    near_recv = wa_swap(near_send, 1)
-
-    def backwards(*arrays):
-        return [(a, tiles(a, True)) for a in arrays]
-
-    local_back, tail, back_end, out_sum = call(
-        1.5,
-        adjoint_kernel,
-        steps,
-        None,
-        backwards(back_keep, back_recv, back_y, states, mask) + whole(out_rate, rate, step),
-        backwards(t(own), t(own)) + whole(shape(8, own), shape(8, own)),
-        [((16, own), F32)],
-        [near_keep],
-    )
-    back_gots = [seq_shift(back_end, -hop) for hop in range(1, hops + 1)]
 
     def weight(left, right, ids, relative, deps):
         blocks = left[0].shape[1] // seqs
@@ -740,7 +688,35 @@
             deps,
         )
 
-    w_down_keep, w_down_send = weight((c_high, c_low), (p_high, p_low), ids, True, [back_end, out_far])
+    w_down_keep, w_down_send = weight((c_high, c_low), (p_high, p_low), ids, True, [gg_sum])
+
+    def backwards(*arrays):
+        return [(a, tiles(a, True)) for a in arrays]
+
+    local_back, tail, back_end, out_sum = call(
+        1.5,
+        adjoint_kernel,
+        steps,
+        None,
+        backwards(back_keep, back_recv, back_y, states, mask) + whole(out_rate, rate, step),
+        backwards(t(own), t(own)) + whole(shape(8, own), shape(8, own)),
+        [((16, own), F32)],
+        [w_down_keep],
+    )
+    back_gots = [seq_shift(back_end, -hop) for hop in range(1, hops + 1)]
+
+    out_send, out_keep, near_send, near_keep = call(
+        9,
+        output_kernel,
+        steps,
+        ids,
+        tiled(p_high, p_low)
+        + whole(w_down)
+        + [(inputs, tiles(inputs, column=part)), (b_down_row, pl.BlockSpec((1, part), lambda i, ids: (0, ids[0])))],
+        tiled(t(part), t(part), t(part), t(part)),
+        [((width, units), BF16)] * 2,
+        [back_end],
+    )
     down_sum = ScatterSum(w_down_keep, after(w_down_send, *back_gots), (1, 2, 4))
     r_high, r_low, far_send, far_keep, turn_sum, red_sum, far_norm = call(
         8,
@@ -753,7 +729,7 @@
         tiled(t(own, dtype=BF16), t(own, dtype=BF16), t(part), t(part))
         + whole(shape(8, own), shape(8, own), shape(16, width)),
         [((2 * part, units), BF16)] * 2 + [((2 * part, own), BF16)] * 2 + [((TILE, width), F32)],
-        [w_down_keep],
+        [near_keep],
     )
     far_recv = wa_swap(far_send, 1)
     next_send, next_keep, norm = call(
@@ -772,25 +748,24 @@
     far_y = wa_swap(far_sum, 2)
     next_recv = wa_swap(next_send, 1)
     near_sum = after(next_keep, far_sum) + next_recv
-    norm_c = wa_swap(norm, 1)
-    norm_y = wa_swap(norm, 2)
-    norm_yc = wa_swap(norm, 3)
 
     w_gate_keep, w_gate_send = weight((n_high, n_low), (gg_high, gg_low), ids_z, False, [near_sum])
     gate_total = ScatterSum(w_gate_keep, w_gate_send, (2, 1, 4))
-    output = after(near_keep, w_gate_keep) + near_recv + out_y
-    w_expand_keep, w_expand_send = weight((m_high, m_low), (ge_high, ge_low), ids, True, [output])
+    w_expand_keep, w_expand_send = weight((m_high, m_low), (ge_high, ge_low), ids, True, [w_gate_keep])
     expand_total = ScatterSum(w_expand_keep, w_expand_send, (1, 2, 4))
+    token = down_sum.step(2, w_expand_keep)
+    grad_own = after(near_sum, token) + far_y
+    all_y = wa_swap(grad_own, 2)
 
     [vector] = call(
         1.5,
         pack_kernel,
         1,
         None,
-        whole(norm, norm_c, norm_y, norm_yc, c_sum, gg_sum, ge_sum, red_sum, turn_sum, out_sum),
+        whole(norm, c_sum, gg_sum, ge_sum, red_sum, turn_sum, out_sum),
         whole(shape(8 * seqs, 128)),
         [((8, max(width, units)), F32), ((8, width), F32)],
-        [w_expand_keep],
+        [grad_own],
     )
     half = shape(seqs // 2, width // seqs + 8, own)
     w_red_keep, w_red_send = call(
@@ -801,20 +776,33 @@
         tiled(n_high, n_low, r_high, r_low) + whole(vector),
         whole(half, half),
         [((width, own), F32)],
-        [w_expand_keep],
+        [grad_own],
     )
     reduce_total = ScatterSum(w_red_keep, w_red_send, (1, 2, 4))
 
-    token = down_sum.step(2, w_red_keep)
-    grad_own = after(near_sum, token) + far_y
-    all_y = wa_swap(grad_own, 2)
-    all_c = wa_swap(grad_own, 1)
-    all_yc = wa_swap(all_y, 1)
-    token = gate_total.step(1, grad_own)
+    out_recv = wa_swap(after(out_send, w_red_keep), 1)
+    near_recv = wa_swap(after(near_send, w_red_keep), 1)
+    token = gate_total.step(1, w_red_keep)
     token = expand_total.step(2, token)
+    out_far = after(out_keep, token) + out_recv
+    out_y = wa_swap(after(out_far, all_y), 2)
+    near_keep = near_keep + near_recv
+    token = down_sum.step(4, out_far)
     token = reduce_total.step(2, token)
-    token = down_sum.step(4, token)
-    token = gate_total.step(4, token)
+    all_c = wa_swap(after(grad_own, token), 1)
+    all_yc = wa_swap(after(all_y, token), 1)
+    [grad_inputs] = call(
+        9,
+        final_kernel,
+        steps,
+        ids,
+        tiled(inputs) + whole(gain) + tiled(grad_own, all_c, all_y, all_yc, *cots),
+        tiled(t(width)),
+        [((TILE, width), F32)] * 2,
+        [token],
+    )
+    output = after(near_keep, grad_inputs) + out_y
+    token = gate_total.step(4, grad_inputs)
     token = expand_total.step(4, token)
     token = reduce_total.step(4, token)
 
@@ -823,6 +811,9 @@
     total_w_expand = expand_total.finish()
     total = reduce_total.finish()
     matrix_rows = width // seqs
+    norm_sums = total[matrix_rows : matrix_rows + 8]
+    norm_sums = norm_sums + wa_swap(norm_sums, 1)
+    norm_sums = norm_sums + wa_swap(norm_sums, 2)
 
     def vector_of(k, length):
         return total[matrix_rows + k, : length // seqs]
@@ -832,20 +823,11 @@
     step_here = lax.dynamic_slice_in_dim(ssm_step, place * count, count, 0)
     keep_sum = vector_of(6, own)
     grad_log = -keep_sum * jnp.exp(-rate_here * step_here)
-    [grad_inputs] = call(
-        9,
-        final_kernel,
-        steps,
-        ids,
-        tiled(inputs) + whole(gain) + tiled(grad_own, all_c, all_y, all_yc, *cots),
-        tiled(t(width)),
-        [((TILE, width), F32)] * 2,
-    )
     return (
         output,
         grad_inputs,
-        vector_of(0, width),
-        vector_of(1, width),
+        norm_sums[0, : width // seqs],
+        norm_sums[1, : width // seqs],
         total_w_gate,
         vector_of(3, units),
         total[:matrix_rows],

time: 339 us -> 290 us (0.86)
  waiting for transfers between devices: 109 us -> 60.7 us
    ppermute x20 -> x19, waiting for transfers between devices: 56.6 us -> 19.2 us  [wa_swap(): return lax.ppermute(value, 'wa', [(i, i ^ distance) for i in range(count)])]
    ppermute x12, waiting for transfers between devices: 52.1 us -> 40.3 us  [seq_swap(): return lax.ppermute(value, 'seq', [(i, i ^ distance) for i in range(count)])]
    ppermute x12, starting transfers between devices: 23.9 us -> 28.2 us  [seq_swap(): return lax.ppermute(value, 'seq', [(i, i ^ distance) for i in range(count)])]
    unnamed x150 -> x146, local copies, waits for them, and re-layouts: 42.3 us -> 39.8 us
    ppermute x20 -> x19, starting transfers between devices: 8.82 us -> 7.9 us  [wa_swap(): return lax.ppermute(value, 'wa', [(i, i ^ distance) for i in range(count)])]
  transfers between devices with their start and end apart: 38 -> 37, of which waited for: 13 -> 14; matrix products, arithmetic and copies ran while one was open for 6% -> 8% of each run, Pallas kernels for 25% -> 35%
where the time goes in v2:
time: 290 us; the launch traced here: 289 us
  Pallas kernels  111 us (38%)
  waiting for transfers between devices  60.7 us (21%)
  starting transfers between devices  51.6 us (18%)
  local copies, waits for them, and re-layouts  42.8 us (15%)
  other arithmetic  21.3 us (7%)
    pallas_call x16, Pallas kernels, call(): return run(*arrays) if ids is None else run(ids, *arrays)  111 us
    ppermute x12, waiting for transfers between devices, seq_swap(): return lax.ppermute(value, 'seq', [(i, i ^ distance) for i in range(count)])  40.3 us
    unnamed x146, local copies, waits for them, and re-layouts  39.8 us
    ppermute x12, starting transfers between devices, seq_swap(): return lax.ppermute(value, 'seq', [(i, i ^ distance) for i in range(count)])  28.2 us
    ppermute x19, waiting for transfers between devices, wa_swap(): return lax.ppermute(value, 'wa', [(i, i ^ distance) for i in range(count)])  19.2 us
    ppermute x6, starting transfers between devices, seq_shift(): return lax.ppermute(value, 'seq', pairs)  15.5 us
    ppermute x19, starting transfers between devices, wa_swap(): return lax.ppermute(value, 'wa', [(i, i ^ distance) for i in range(count)])  7.9 us
  transfers between devices with their start and end apart: 37, of which 14 were waited for; matrix products, arithmetic and copies ran while one was open for 8% of the time, Pallas kernels for 35%

profile of v2, /device:TPU:0, one launch (start us, length us, event | category | flops | bytes accessed | tf_op | source)
XLA Modules:
  0.0 288.9 jit_solution(4044154121306634765)
XLA Ops:
  12.1 7.0 %shard_map.289 = (bf16[1536,1024]{1,0:T(8,128)(2,1)S(1)}, bf16[1536,1024]{1,0:T(8,128)(2,1)S(1)}, f32[1536,128]{1,0:T(8,128)S(1)}, f32[1536,128]{1,0:T(8,128)S(1...) custom-call(f32[1536,1024]{1,0:T(8,128)S(1)} %copy-done, f32[1,1024]{1,0:T(1,128)S(1)} %bitcast.45, ...), custom_call_target="tpu_custom_call" | custom-call | flops 350000000 | bytes 700000 | tf_op jit(solution)/shard_map/pallas_call | solution.py:486
  20.0 3.4 %collective-permute-start = (f32[8,128]{1,0:T(8,128)S(1)}, f32[8,128]{1,0:T(8,128)S(1)}, u32[]{:S(2)}, u32[]{:S(2)}) collective-permute-start(f32[8,128]{1,0:T(8,128)S(1)} %get-tuple-element.93), channel_id=1, source_target_pairs={{0,4},{4,8},{8,12},{12,16},{16,20},{20,24},{24,28},{1,5},{5,9},{9,... | collective-permute-start | bytes 12296 | tf_op jit(solution)/shard_map/ppermute | solution.py:506
  23.4 3.5 %collective-permute-start.1 = (f32[8,128]{1,0:T(8,128)S(1)}, f32[8,128]{1,0:T(8,128)S(1)}, u32[]{:S(2)}, u32[]{:S(2)}) collective-permute-start(f32[8,128]{1,0:T(8,128)S(1)} %get-tuple-element.93), channel_id=1, source_target_pairs={{0,8},{4,12},{8,16},{12,20},{16,24},{20,28},{1,9},{5,13},{9,17},{1... | collective-permute-start | bytes 12296 | tf_op jit(solution)/shard_map/ppermute | solution.py:506
  26.9 4.5 %collective-permute-start.2 = (f32[8,128]{1,0:T(8,128)S(1)}, f32[8,128]{1,0:T(8,128)S(1)}, u32[]{:S(2)}, u32[]{:S(2)}) collective-permute-start(f32[8,128]{1,0:T(8,128)S(1)} %get-tuple-element.93), channel_id=1, source_target_pairs={{0,12},{4,16},{8,20},{12,24},{16,28},{1,13},{5,17},{9,21},{13,25},... | collective-permute-start | bytes 12296 | tf_op jit(solution)/shard_map/ppermute | solution.py:506
  34.9 11.7 %shard_map.291 = (f32[1536,768]{1,0:T(8,128)S(1)}, f32[1536,768]{1,0:T(8,128)S(1)}) custom-call(bf16[1536,1024]{1,0:T(8,128)(2,1)S(1)} %get-tuple-element.95.refs_0_.refs_1_, bf16[1536,1024]{1,0:T(8,128)(2,1)S(1)} %get-tuple-element.96.refs_1_.refs_2_, f32[1024,768]{1,0:T(8,128)S(1)} %copy-done.4, f32[1,768]{1,0:T(1,128)S(1)} %broadcast_in_dim.40.refs_3_, ...), custom_call_target="tpu_custom_call" | custom-call | flops 600000000 | bytes 1200000 | tf_op jit(solution)/shard_map/pallas_call | solution.py:486
  60.1 15.9 %shard_map.292 = (bf16[1536,1024]{1,0:T(8,128)(2,1)S(1)}, bf16[1536,1024]{1,0:T(8,128)(2,1)S(1)}, f32[1536,768]{1,0:T(8,128)S(1)}, bf16[1536,768]{1,0:T(8,128)(2...) custom-call(s32[10]{0:T(128)S(1)} %pad_add_fusion.refs_0_, ...), custom_call_target="tpu_custom_call" | custom-call | flops 850000000 | bytes 1700000 | tf_op jit(solution)/shard_map/pallas_call | solution.py:486
  79.4 4.3 %shard_map.293 = (f32[1536,256]{1,0:T(8,128)S(1)}, f32[8,768]{1,0:T(8,128)S(1)}) custom-call(s32[10]{0:T(128)S(1)} %pad_add_fusion.refs_0_, bf16[1536,768]{1,0:T(8,128)(2,1)S(1)} %get-tuple-element.99.refs_1_.refs_3_, bf16[1536,768]{1,0:T(8,128)(2,1)S(1)} %get-tuple-element.100.refs_2_.refs_4_, f32[512,768]{1,0:T(8,128)S(1)} %copy-done.16, ...), custom_call_target="tpu_custom_call" | custom-call | flops 20000000000 | bytes 40000000 | tf_op jit(solution)/shard_map/pallas_call | solution.py:486
  91.7 6.8 %shard_map.294 = (bf16[1536,512]{1,0:T(8,128)(2,1)S(1)}, bf16[1536,512]{1,0:T(8,128)(2,1)S(1)}, bf16[1536,768]{1,0:T(8,128)(2,1)S(1)}, bf16[1536,768]{1,0:T(8,12...) custom-call(s32[10]{0:T(128)S(1)} %pad_add_fusion.refs_0_, ...), custom_call_target="tpu_custom_call" | custom-call | flops 450000000 | bytes 900000 | tf_op jit(solution)/shard_map/pallas_call | solution.py:486
  103.5 9.1 %shard_map.295 = (f32[4,128,768]{2,1,0:T(8,128)S(1)}, f32[4,128,768]{2,1,0:T(8,128)S(1)}) custom-call(s32[10]{0:T(128)S(1)} %pad_add_fusion.refs_0_, bf16[1536,1024]{1,0:T(8,128)(2,1)S(1)} %copy-done.31, bf16[1536,1024]{1,0:T(8,128)(2,1)S(1)} %copy-done.33, bf16[1536,768]{1,0:T(8,128)(2,1)S(1)} %get-tuple-element.106.refs_3_.refs_1_, ...), custom_call_target="tpu_custom_call" | custom-call | flops 500000000 | bytes 1000000 | tf_op jit(solution)/shard_map/pallas_call | solution.py:486
  118.6 9.8 %shard_map.297 = (f32[1536,256]{1,0:T(8,128)S(1)}, f32[1536,256]{1,0:T(8,128)S(1)}, f32[1536,256]{1,0:T(8,128)S(1)}, f32[1536,256]{1,0:T(8,128)S(1)}) custom-call(s32[10]{0:T(128)S(1)} %pad_add_fusion.refs_0_, bf16[1536,768]{1,0:T(8,128)(2,1)S(1)} %copy-done.15, bf16[1536,768]{1,0:T(8,128)(2,1)S(1)} %get-tuple-element.107.refs_4_.refs_2_, ...), custom_call_target="tpu_custom_call" | custom-call | flops 450000000 | bytes 900000 | tf_op jit(solution)/shard_map/pallas_call | solution.py:486
  128.5 7.9 %shard_map.298 = (bf16[1536,128]{1,0:T(8,128)(2,1)S(1)}, bf16[1536,128]{1,0:T(8,128)(2,1)S(1)}, f32[1536,256]{1,0:T(8,128)S(1)}, f32[1536,256]{1,0:T(8,128)S(1)}...) custom-call(s32[10]{0:T(128)S(1)} %pad_add_fusion.refs_0_, ...), custom_call_target="tpu_custom_call" | custom-call | flops 400000000 | bytes 800000 | tf_op jit(solution)/shard_map/pallas_call | solution.py:486
  136.6 7.3 %shard_map.299 = (f32[1536,256]{1,0:T(8,128)S(1)}, f32[1536,256]{1,0:T(8,128)S(1)}, f32[8,1024]{1,0:T(8,128)S(1)}) custom-call(s32[10]{0:T(128)S(1)} %pad_add_fusion.refs_0_, bf16[1536,128]{1,0:T(8,128)(2,1)S(1)} %get-tuple-element.122.refs_1_.refs_3_, bf16[1536,128]{1,0:T(8,128)(2,1)S(1)} %get-tuple-element.123.refs_2_.refs_4_, ...), custom_call_target="tpu_custom_call" | custom-call | flops 350000000 | bytes 700000 | tf_op jit(solution)/shard_map/pallas_call | solution.py:486
  150.1 9.1 %shard_map.300 = (f32[4,128,768]{2,1,0:T(8,128)S(1)}, f32[4,128,768]{2,1,0:T(8,128)S(1)}) custom-call(s32[10]{0:T(128)S(1)} %pad_add_fusion.2.refs_0_, bf16[1536,1024]{1,0:T(8,128)(2,1)S(1)} %copy-done.7, bf16[1536,1024]{1,0:T(8,128)(2,1)S(1)} %copy-done.9, bf16[1536,768]{1,0:T(8,128)(2,1)S(1)} %get-tuple-element.120.refs_5_.refs_3_, ...), custom_call_target="tpu_custom_call" | custom-call | flops 500000000 | bytes 1000000 | tf_op jit(solution)/shard_map/pallas_call | solution.py:486
  159.1 3.3 %collective-permute-start.22 = (f32[4,128,768]{2,1,0:T(8,128)S(1)}, f32[4,128,768]{2,1,0:T(8,128)S(1)}, u32[]{:S(2)}, u32[]{:S(2)}) collective-permute-start(f32[4,128,768]{2,1,0:T(8,128)S(1)} %get-tuple-element.150), channel_id=1, source_target_pairs={{0,8},{4,12},{8,0},{12,4},{16,24},{20,28},{24,16},{28,20},{1,9},{5... | collective-permute-start | bytes 4718600 | tf_op jit(solution)/shard_map/ppermute | solution.py:500
  162.5 5.2 %shard_map.301 = (f32[4,64,768]{2,1,0:T(8,128)S(1)}, f32[4,64,768]{2,1,0:T(8,128)S(1)}) custom-call(s32[10]{0:T(128)S(1)} %pad_add_fusion.refs_0_, bf16[1536,512]{1,0:T(8,128)(2,1)S(1)} %copy-done.39, bf16[1536,512]{1,0:T(8,128)(2,1)S(1)} %copy-done.41, bf16[1536,768]{1,0:T(8,128)(2,1)S(1)} %copy-done.35, bf16[1536,768]{1,0:T(8,128)(2,1)S(1)} %copy-done.37, ...), custom_call_target="tpu_custom_call" | custom-call | flops 500000000 | bytes 1000000 | tf_op jit(solution)/shard_map/pallas_call | solution.py:486
  167.7 14.0 %collective-permute-done.16 = f32[4,128,768]{2,1,0:T(8,128)} collective-permute-done((f32[4,128,768]{2,1,0:T(8,128)S(1)}, f32[4,128,768]{2,1,0:T(8,128)}, u32[]{:S(2)}, u32[]{:S(2)}) %collective-permute-start.16) | collective-permute-done | bytes 1572896 | tf_op jit(solution)/shard_map/ppermute | solution.py:500
  185.3 4.9 %shard_map.303 = (f32[4,136,128]{2,1,0:T(8,128)S(1)}, f32[4,136,128]{2,1,0:T(8,128)S(1)}) custom-call(s32[10]{0:T(128)S(1)} %pad_add_fusion.refs_0_, bf16[1536,1024]{1,0:T(8,128)(2,1)S(1)} %copy-done.7, bf16[1536,1024]{1,0:T(8,128)(2,1)S(1)} %copy-done.9, bf16[1536,128]{1,0:T(8,128)(2,1)S(1)} %get-tuple-element.122.refs_1_.refs_3_, ...), custom_call_target="tpu_custom_call" | custom-call | flops 250000000 | bytes 500000 | tf_op jit(solution)/shard_map/pallas_call | solution.py:486
  198.2 12.4 %collective-permute-done.21 = f32[4,64,768]{2,1,0:T(8,128)S(1)} collective-permute-done((f32[4,64,768]{2,1,0:T(8,128)S(1)}, f32[4,64,768]{2,1,0:T(8,128)S(1)}, u32[]{:S(2)}, u32[]{:S(2)}) %collective-permute-start.21) | collective-permute-done | bytes 786464 | tf_op jit(solution)/shard_map/ppermute | solution.py:500
  218.6 8.6 %collective-permute-done.25.refs_5_ = f32[1536,256]{1,0:T(8,128)} collective-permute-done((f32[1536,256]{1,0:T(8,128)S(1)}, f32[1536,256]{1,0:T(8,128)}, u32[]{:S(2)}, u32[]{:S(2)}) %collective-permute-start.25) | collective-permute-done | bytes 1572896 | tf_op jit(solution)/shard_map/ppermute | solution.py:495
  235.0 4.2 %collective-permute-start.36 = (f32[1,128,768]{2,1,0:T(8,128)S(1)}, f32[1,128,768]{2,1,0:T(8,128)S(1)}, u32[]{:S(2)}, u32[]{:S(2)}) collective-permute-start(f32[1,128,768]{2,1,0:T(8,128)S(1)} %copy-done.64), channel_id=1, source_target_pairs={{0,16},{4,20},{8,24},{12,28},{16,0},{20,4},{24,8},{28,12},{1,17},{... | collective-permute-start | bytes 1179656 | tf_op jit(solution)/shard_map/ppermute | solution.py:500
  243.3 10.3 %shard_map.304 = f32[1536,1024]{1,0:T(8,128)} custom-call(s32[10]{0:T(128)S(1)} %pad_add_fusion.refs_0_, f32[1536,1024]{1,0:T(8,128)S(1)} %copy-done.1, f32[1,1024]{1,0:T(1,128)S(1)} %bitcast.46, f32[1536,256]{1,0:T(8,128)S(1)} %add.95.refs_7_.refs_6_.refs_3_, f32[1536,256]{1,0:T(8,128)} %collective-permute-done.24.refs_4_, ...), custom_call_target="tpu_custom_call" | custom-call | flops 450000000 | bytes 900000 | tf_op jit(solution)/shard_map/pallas_call | solution.py:486
  261.6 4.2 %collective-permute-done.27 = f32[1536,256]{1,0:T(8,128)} collective-permute-done((f32[1536,256]{1,0:T(8,128)}, f32[1536,256]{1,0:T(8,128)}, u32[]{:S(2)}, u32[]{:S(2)}) %collective-permute-start.27) | collective-permute-done | bytes 1572896 | tf_op jit(solution)/shard_map/ppermute | solution.py:495
  268.5 6.4 %collective-permute-done.31 = f32[1,136,128]{2,1,0:T(8,128)S(1)} collective-permute-done((f32[1,136,128]{2,1,0:T(8,128)S(1)}, f32[1,136,128]{2,1,0:T(8,128)S(1)}, u32[]{:S(2)}, u32[]{:S(2)}) %collective-permute-start.31) | collective-permute-done | bytes 69664 | tf_op jit(solution)/shard_map/ppermute | solution.py:500
  283.6 3.5 %collective-permute-done.34 = f32[1,128,768]{2,1,0:T(8,128)S(1)} collective-permute-done((f32[1,128,768]{2,1,0:T(8,128)S(1)}, f32[1,128,768]{2,1,0:T(8,128)S(1)}, u32[]{:S(2)}, u32[]{:S(2)}) %collective-permute-start.34) | collective-permute-done | bytes 393248 | tf_op jit(solution)/shard_map/ppermute | solution.py:500
  (251 shorter events, 110.5 us)
Async XLA Ops:
  0.6 51.9 %collective-permute-start.6 = (f32[1536,256]{1,0:T(8,128)}, f32[1536,256]{1,0:T(8,128)}, u32[]{:S(2)}, u32[]{:S(2)}) collective-permute-start(f32[1536,256]{1,0:T(8,128)} %refs_7_.7), channel_id=1, source_target_pairs={{0,2},{1,3},{2,0},{3,1},{4,6},{5,7},{6,4},{7,5},{8,10},{9,11},{10,... | collective-permute-start | bytes 4718600 | tf_op jit(solution)/shard_map/ppermute | solution.py:495
  31.4 22.0 %collective-permute-start.5 = (f32[1536,256]{1,0:T(8,128)}, f32[1536,256]{1,0:T(8,128)}, u32[]{:S(2)}, u32[]{:S(2)}) collective-permute-start(f32[1536,256]{1,0:T(8,128)} %refs_7_.7), channel_id=1, source_target_pairs={{0,1},{1,0},{2,3},{3,2},{4,5},{5,4},{6,7},{7,6},{8,9},{9,8},{10,11... | collective-permute-start | bytes 4718600 | tf_op jit(solution)/shard_map/ppermute | solution.py:495
  52.7 31.2 %collective-permute-start.4 = (f32[1536,128]{1,0:T(8,128)}, f32[1536,128]{1,0:T(8,128)S(1)}, u32[]{:S(2)}, u32[]{:S(2)}) collective-permute-start(f32[1536,128]{1,0:T(8,128)} %copy-done.28), channel_id=1, source_target_pairs={{0,2},{1,3},{2,0},{3,1},{4,6},{5,7},{6,4},{7,5},{8,10},{9,11},{10,... | collective-permute-start | bytes 2359304 | tf_op jit(solution)/shard_map/ppermute | solution.py:495
  53.2 32.8 %collective-permute-start.3 = (f32[1536,128]{1,0:T(8,128)}, f32[1536,128]{1,0:T(8,128)S(1)}, u32[]{:S(2)}, u32[]{:S(2)}) collective-permute-start(f32[1536,128]{1,0:T(8,128)} %copy-done.28), channel_id=1, source_target_pairs={{0,1},{1,0},{2,3},{3,2},{4,5},{5,4},{6,7},{7,6},{8,9},{9,8},{10,11... | collective-permute-start | bytes 2359304 | tf_op jit(solution)/shard_map/ppermute | solution.py:495
  85.5 27.2 %collective-permute-start.10 = (f32[1536,128]{1,0:T(8,128)S(1)}, f32[1536,128]{1,0:T(8,128)S(1)}, u32[]{:S(2)}, u32[]{:S(2)}) collective-permute-start(f32[1536,128]{1,0:T(8,128)S(1)} %slice_add_fusion.refs_10_), channel_id=1, source_target_pairs={{0,2},{1,3},{2,0},{3,1},{4,6},{5,7},{6,4},{7,5},{8,10},{9,11},{10,... | collective-permute-start | bytes 2359304 | tf_op jit(solution)/shard_map/ppermute | solution.py:495
  114.3 14.1 %collective-permute-start.11 = (f32[8,128]{1,0:T(8,128)S(1)}, f32[8,128]{1,0:T(8,128)S(1)}, u32[]{:S(2)}, u32[]{:S(2)}) collective-permute-start(f32[8,128]{1,0:T(8,128)S(1)} %get-tuple-element.113.refs_6_), channel_id=1, source_target_pairs={{4,0},{8,4},{12,8},{16,12},{20,16},{24,20},{28,24},{5,1},{9,5},{13... | collective-permute-start | bytes 12296 | tf_op jit(solution)/shard_map/ppermute | solution.py:506
  115.7 12.7 %collective-permute-start.12 = (f32[8,128]{1,0:T(8,128)S(1)}, f32[8,128]{1,0:T(8,128)S(1)}, u32[]{:S(2)}, u32[]{:S(2)}) collective-permute-start(f32[8,128]{1,0:T(8,128)S(1)} %get-tuple-element.113.refs_6_), channel_id=1, source_target_pairs={{8,0},{12,4},{16,8},{20,12},{24,16},{28,20},{9,1},{13,5},{17,9},{2... | collective-permute-start | bytes 12296 | tf_op jit(solution)/shard_map/ppermute | solution.py:506
  144.3 37.4 %collective-permute-start.16 = (f32[4,128,768]{2,1,0:T(8,128)S(1)}, f32[4,128,768]{2,1,0:T(8,128)}, u32[]{:S(2)}, u32[]{:S(2)}) collective-permute-start(f32[4,128,768]{2,1,0:T(8,128)S(1)} %get-tuple-element.138), channel_id=1, source_target_pairs={{0,4},{4,0},{8,12},{12,8},{16,20},{20,16},{24,28},{28,24},{1,5},{5... | collective-permute-start | bytes 4718600 | tf_op jit(solution)/shard_map/ppermute | solution.py:500
  147.2 36.3 %collective-permute-start.17 = (f32[1536,256]{1,0:T(8,128)S(1)}, f32[1536,256]{1,0:T(8,128)}, u32[]{:S(2)}, u32[]{:S(2)}) collective-permute-start(f32[1536,256]{1,0:T(8,128)S(1)} %add.92), channel_id=1, source_target_pairs={{0,2},{1,3},{2,0},{3,1},{4,6},{5,7},{6,4},{7,5},{8,10},{9,11},{10,... | collective-permute-start | bytes 4718600 | tf_op jit(solution)/shard_map/ppermute | solution.py:495
  159.1 37.7 %collective-permute-start.22 = (f32[4,128,768]{2,1,0:T(8,128)S(1)}, f32[4,128,768]{2,1,0:T(8,128)S(1)}, u32[]{:S(2)}, u32[]{:S(2)}) collective-permute-start(f32[4,128,768]{2,1,0:T(8,128)S(1)} %get-tuple-element.150), channel_id=1, source_target_pairs={{0,8},{4,12},{8,0},{12,4},{16,24},{20,28},{24,16},{28,20},{1,9},{5... | collective-permute-start | bytes 4718600 | tf_op jit(solution)/shard_map/ppermute | solution.py:500
  190.2 23.1 %collective-permute-start.23 = (f32[1536,256]{1,0:T(8,128)S(1)}, f32[1536,256]{1,0:T(8,128)S(1)}, u32[]{:S(2)}, u32[]{:S(2)}) collective-permute-start(f32[1536,256]{1,0:T(8,128)S(1)} %get-tuple-element.155), channel_id=1, source_target_pairs={{0,1},{1,0},{2,3},{3,2},{4,5},{5,4},{6,7},{7,6},{8,9},{9,8},{10,11... | collective-permute-start | bytes 4718600 | tf_op jit(solution)/shard_map/ppermute | solution.py:495
  190.2 36.9 %collective-permute-start.25 = (f32[1536,256]{1,0:T(8,128)S(1)}, f32[1536,256]{1,0:T(8,128)}, u32[]{:S(2)}, u32[]{:S(2)}) collective-permute-start(f32[1536,256]{1,0:T(8,128)S(1)} %add.95.refs_7_.refs_6_.refs_3_), channel_id=1, source_target_pairs={{0,2},{1,3},{2,0},{3,1},{4,6},{5,7},{6,4},{7,5},{8,10},{9,11},{10,... | collective-permute-start | bytes 4718600 | tf_op jit(solution)/shard_map/ppermute | solution.py:495
  190.9 19.6 %collective-permute-start.21 = (f32[4,64,768]{2,1,0:T(8,128)S(1)}, f32[4,64,768]{2,1,0:T(8,128)S(1)}, u32[]{:S(2)}, u32[]{:S(2)}) collective-permute-start(f32[4,64,768]{2,1,0:T(8,128)S(1)} %get-tuple-element.149), channel_id=1, source_target_pairs={{0,4},{4,0},{8,12},{12,8},{16,20},{20,16},{24,28},{28,24},{1,5},{5... | collective-permute-start | bytes 2359304 | tf_op jit(solution)/shard_map/ppermute | solution.py:500
  192.6 21.9 %collective-permute-start.20 = (f32[2,128,768]{2,1,0:T(8,128)S(1)}, f32[2,128,768]{2,1,0:T(8,128)S(1)}, u32[]{:S(2)}, u32[]{:S(2)}) collective-permute-start(f32[2,128,768]{2,1,0:T(8,128)S(1)} %get-tuple-element.170), channel_id=1, source_target_pairs={{0,8},{4,12},{8,0},{12,4},{16,24},{20,28},{24,16},{28,20},{1,9},{5... | collective-permute-start | bytes 2359304 | tf_op jit(solution)/shard_map/ppermute | solution.py:500
  213.2 16.8 %collective-permute-start.18 = (f32[1536,256]{1,0:T(8,128)S(1)}, f32[1536,256]{1,0:T(8,128)}, u32[]{:S(2)}, u32[]{:S(2)}) collective-permute-start(f32[1536,256]{1,0:T(8,128)S(1)} %get-tuple-element.146), channel_id=1, source_target_pairs={{0,1},{1,0},{2,3},{3,2},{4,5},{5,4},{6,7},{7,6},{8,9},{9,8},{10,11... | collective-permute-start | bytes 4718600 | tf_op jit(solution)/shard_map/ppermute | solution.py:495
  227.2 12.0 %collective-permute-start.24 = (f32[1536,256]{1,0:T(8,128)S(1)}, f32[1536,256]{1,0:T(8,128)}, u32[]{:S(2)}, u32[]{:S(2)}) collective-permute-start(f32[1536,256]{1,0:T(8,128)S(1)} %add.95.refs_7_.refs_6_.refs_3_), channel_id=1, source_target_pairs={{0,1},{1,0},{2,3},{3,2},{4,5},{5,4},{6,7},{7,6},{8,9},{9,8},{10,11... | collective-permute-start | bytes 4718600 | tf_op jit(solution)/shard_map/ppermute | solution.py:495
  227.7 25.9 %collective-permute-start.30 = (f32[2,128,768]{2,1,0:T(8,128)}, f32[2,128,768]{2,1,0:T(8,128)}, u32[]{:S(2)}, u32[]{:S(2)}) collective-permute-start(f32[2,128,768]{2,1,0:T(8,128)} %get-tuple-element.168), channel_id=1, source_target_pairs={{0,4},{4,0},{8,12},{12,8},{16,20},{20,16},{24,28},{28,24},{1,5},{5... | collective-permute-start | bytes 2359304 | tf_op jit(solution)/shard_map/ppermute | solution.py:500
  229.4 36.3 %collective-permute-start.27 = (f32[1536,256]{1,0:T(8,128)}, f32[1536,256]{1,0:T(8,128)}, u32[]{:S(2)}, u32[]{:S(2)}) collective-permute-start(f32[1536,256]{1,0:T(8,128)} %add.100), channel_id=1, source_target_pairs={{0,2},{1,3},{2,0},{3,1},{4,6},{5,7},{6,4},{7,5},{8,10},{9,11},{10,... | collective-permute-start | bytes 4718600 | tf_op jit(solution)/shard_map/ppermute | solution.py:495
  230.0 24.8 %collective-permute-start.29 = (f32[2,64,768]{2,1,0:T(8,128)}, f32[2,64,768]{2,1,0:T(8,128)}, u32[]{:S(2)}, u32[]{:S(2)}) collective-permute-start(f32[2,64,768]{2,1,0:T(8,128)} %get-tuple-element.172), channel_id=1, source_target_pairs={{0,8},{4,12},{8,0},{12,4},{16,24},{20,28},{24,16},{28,20},{1,9},{5... | collective-permute-start | bytes 1179656 | tf_op jit(solution)/shard_map/ppermute | solution.py:500
  235.0 22.8 %collective-permute-start.36 = (f32[1,128,768]{2,1,0:T(8,128)S(1)}, f32[1,128,768]{2,1,0:T(8,128)S(1)}, u32[]{:S(2)}, u32[]{:S(2)}) collective-permute-start(f32[1,128,768]{2,1,0:T(8,128)S(1)} %copy-done.64), channel_id=1, source_target_pairs={{0,16},{4,20},{8,24},{12,28},{16,0},{20,4},{24,8},{28,12},{1,17},{... | collective-permute-start | bytes 1179656 | tf_op jit(solution)/shard_map/ppermute | solution.py:500
  239.2 16.6 %collective-permute-start.28 = (f32[2,136,128]{2,1,0:T(8,128)S(1)}, f32[2,136,128]{2,1,0:T(8,128)S(1)}, u32[]{:S(2)}, u32[]{:S(2)}) collective-permute-start(f32[2,136,128]{2,1,0:T(8,128)S(1)} %get-tuple-element.174.refs_11_), channel_id=1, source_target_pairs={{0,8},{4,12},{8,0},{12,4},{16,24},{20,28},{24,16},{28,20},{1,9},{5... | collective-permute-start | bytes 417800 | tf_op jit(solution)/shard_map/ppermute | solution.py:500
  255.8 19.1 %collective-permute-start.31 = (f32[1,136,128]{2,1,0:T(8,128)S(1)}, f32[1,136,128]{2,1,0:T(8,128)S(1)}, u32[]{:S(2)}, u32[]{:S(2)}) collective-permute-start(f32[1,136,128]{2,1,0:T(8,128)S(1)} %slice_add_fusion.15), channel_id=1, source_target_pairs={{0,16},{4,20},{8,24},{12,28},{16,0},{20,4},{24,8},{28,12},{1,17},{... | collective-permute-start | bytes 208904 | tf_op jit(solution)/shard_map/ppermute | solution.py:500
  258.7 23.3 %collective-permute-start.35 = (f32[1,64,768]{2,1,0:T(8,128)S(1)}, f32[1,64,768]{2,1,0:T(8,128)S(1)}, u32[]{:S(2)}, u32[]{:S(2)}) collective-permute-start(f32[1,64,768]{2,1,0:T(8,128)S(1)} %slice_add_fusion.12), channel_id=1, source_target_pairs={{0,16},{4,20},{8,24},{12,28},{16,0},{20,4},{24,8},{28,12},{1,17},{... | collective-permute-start | bytes 589832 | tf_op jit(solution)/shard_map/ppermute | solution.py:500
  259.6 27.5 %collective-permute-start.34 = (f32[1,128,768]{2,1,0:T(8,128)S(1)}, f32[1,128,768]{2,1,0:T(8,128)S(1)}, u32[]{:S(2)}, u32[]{:S(2)}) collective-permute-start(f32[1,128,768]{2,1,0:T(8,128)S(1)} %slice_add_fusion.7), channel_id=1, source_target_pairs={{0,16},{4,20},{8,24},{12,28},{16,0},{20,4},{24,8},{28,12},{1,17},{... | collective-permute-start | bytes 1179656 | tf_op jit(solution)/shard_map/ppermute | solution.py:500
  (86 other events, 655.6 us)

commit v3 on v2

--- a/solution.py
+++ b/solution.py
@@ -12,7 +12,7 @@
 SEQ_MAX = 4096
 F32 = jnp.float32
 BF16 = jnp.bfloat16
-VMEM_LIMIT = 22 * 2**20
+VMEM_LIMIT = 20 * 2**20
 TILE = 256
 COST = 10**5
 RATE = 5 * 10**7
@@ -753,10 +753,6 @@
     gate_total = ScatterSum(w_gate_keep, w_gate_send, (2, 1, 4))
     w_expand_keep, w_expand_send = weight((m_high, m_low), (ge_high, ge_low), ids, True, [w_gate_keep])
     expand_total = ScatterSum(w_expand_keep, w_expand_send, (1, 2, 4))
-    token = down_sum.step(2, w_expand_keep)
-    grad_own = after(near_sum, token) + far_y
-    all_y = wa_swap(grad_own, 2)
-
     [vector] = call(
         1.5,
         pack_kernel,
@@ -765,7 +761,7 @@
         whole(norm, c_sum, gg_sum, ge_sum, red_sum, turn_sum, out_sum),
         whole(shape(8 * seqs, 128)),
         [((8, max(width, units)), F32), ((8, width), F32)],
-        [grad_own],
+        [w_expand_keep],
     )
     half = shape(seqs // 2, width // seqs + 8, own)
     w_red_keep, w_red_send = call(
@@ -776,13 +772,17 @@
         tiled(n_high, n_low, r_high, r_low) + whole(vector),
         whole(half, half),
         [((width, own), F32)],
-        [grad_own],
-    )
+        [w_expand_keep],
+    )
+    token = down_sum.step(2, w_red_keep)
+    grad_own = after(near_sum, token) + far_y
+    all_y = wa_swap(grad_own, 2)
+
     reduce_total = ScatterSum(w_red_keep, w_red_send, (1, 2, 4))
 
-    out_recv = wa_swap(after(out_send, w_red_keep), 1)
-    near_recv = wa_swap(after(near_send, w_red_keep), 1)
-    token = gate_total.step(1, w_red_keep)
+    out_recv = wa_swap(after(out_send, grad_own), 1)
+    near_recv = wa_swap(after(near_send, grad_own), 1)
+    token = gate_total.step(1, grad_own)
     token = expand_total.step(2, token)
     out_far = after(out_keep, token) + out_recv
     out_y = wa_swap(after(out_far, all_y), 2)

time: 290 us -> 280 us (0.966)
  starting transfers between devices: 51.6 us -> 47.7 us
  local copies, waits for them, and re-layouts: 42.8 us -> 39.2 us
  other arithmetic: 21.3 us -> 18.4 us
    ppermute x12, starting transfers between devices: 28.2 us -> 23.8 us  [seq_swap(): return lax.ppermute(value, 'seq', [(i, i ^ distance) for i in range(count)])]
    unnamed x146 -> x116, local copies, waits for them, and re-layouts: 39.8 us -> 36.2 us
  transfers between devices with their start and end apart: 37 -> 37, of which waited for: 14 -> 14; matrix products, arithmetic and copies ran while one was open for 8% -> 7% of each run, Pallas kernels for 35% -> 36%
where the time goes in v3:
time: 280 us; the launch traced here: 279 us
  Pallas kernels  111 us (40%)
  waiting for transfers between devices  61.7 us (22%)
  starting transfers between devices  47.7 us (17%)
  local copies, waits for them, and re-layouts  39.2 us (14%)
  other arithmetic  18.4 us (7%)
    pallas_call x16, Pallas kernels, call(): return run(*arrays) if ids is None else run(ids, *arrays)  111 us
    ppermute x12, waiting for transfers between devices, seq_swap(): return lax.ppermute(value, 'seq', [(i, i ^ distance) for i in range(count)])  42.1 us
    unnamed x116, local copies, waits for them, and re-layouts  36.2 us
    ppermute x12, starting transfers between devices, seq_swap(): return lax.ppermute(value, 'seq', [(i, i ^ distance) for i in range(count)])  23.8 us
    ppermute x19, waiting for transfers between devices, wa_swap(): return lax.ppermute(value, 'wa', [(i, i ^ distance) for i in range(count)])  18.4 us
    ppermute x6, starting transfers between devices, seq_shift(): return lax.ppermute(value, 'seq', pairs)  15.4 us
    ppermute x19, starting transfers between devices, wa_swap(): return lax.ppermute(value, 'wa', [(i, i ^ distance) for i in range(count)])  8.5 us
  transfers between devices with their start and end apart: 37, of which 14 were waited for; matrix products, arithmetic and copies ran while one was open for 7% of the time, Pallas kernels for 36%

profile of v3, /device:TPU:0, one launch (start us, length us, event | category | flops | bytes accessed | tf_op | source)
XLA Modules:
  0.0 279.3 jit_solution(13164271062871662262)
XLA Ops:
  11.8 7.0 %shard_map.289 = (bf16[1536,1024]{1,0:T(8,128)(2,1)S(1)}, bf16[1536,1024]{1,0:T(8,128)(2,1)S(1)}, f32[1536,128]{1,0:T(8,128)S(1)}, f32[1536,128]{1,0:T(8,128)S(1...) custom-call(f32[1536,1024]{1,0:T(8,128)S(1)} %copy-done, f32[1,1024]{1,0:T(1,128)S(1)} %bitcast.45, ...), custom_call_target="tpu_custom_call" | custom-call | flops 350000000 | bytes 700000 | tf_op jit(solution)/shard_map/pallas_call | solution.py:486
  23.2 3.5 %collective-permute-start.1 = (f32[8,128]{1,0:T(8,128)S(1)}, f32[8,128]{1,0:T(8,128)S(1)}, u32[]{:S(2)}, u32[]{:S(2)}) collective-permute-start(f32[8,128]{1,0:T(8,128)S(1)} %get-tuple-element.93), channel_id=1, source_target_pairs={{0,8},{4,12},{8,16},{12,20},{16,24},{20,28},{1,9},{5,13},{9,17},{1... | collective-permute-start | bytes 12296 | tf_op jit(solution)/shard_map/ppermute | solution.py:506
  26.7 4.5 %collective-permute-start.2 = (f32[8,128]{1,0:T(8,128)S(1)}, f32[8,128]{1,0:T(8,128)S(1)}, u32[]{:S(2)}, u32[]{:S(2)}) collective-permute-start(f32[8,128]{1,0:T(8,128)S(1)} %get-tuple-element.93), channel_id=1, source_target_pairs={{0,12},{4,16},{8,20},{12,24},{16,28},{1,13},{5,17},{9,21},{13,25},... | collective-permute-start | bytes 12296 | tf_op jit(solution)/shard_map/ppermute | solution.py:506
  34.6 11.7 %shard_map.291 = (f32[1536,768]{1,0:T(8,128)S(1)}, f32[1536,768]{1,0:T(8,128)S(1)}) custom-call(bf16[1536,1024]{1,0:T(8,128)(2,1)S(1)} %get-tuple-element.95.refs_0_.refs_1_, bf16[1536,1024]{1,0:T(8,128)(2,1)S(1)} %get-tuple-element.96.refs_1_.refs_2_, f32[1024,768]{1,0:T(8,128)S(1)} %copy-done.4, f32[1,768]{1,0:T(1,128)S(1)} %broadcast_in_dim.40.refs_3_, ...), custom_call_target="tpu_custom_call" | custom-call | flops 600000000 | bytes 1200000 | tf_op jit(solution)/shard_map/pallas_call | solution.py:486
  60.3 15.9 %shard_map.292 = (bf16[1536,1024]{1,0:T(8,128)(2,1)S(1)}, bf16[1536,1024]{1,0:T(8,128)(2,1)S(1)}, f32[1536,768]{1,0:T(8,128)S(1)}, bf16[1536,768]{1,0:T(8,128)(2...) custom-call(s32[10]{0:T(128)S(1)} %pad_add_fusion.refs_0_, ...), custom_call_target="tpu_custom_call" | custom-call | flops 850000000 | bytes 1700000 | tf_op jit(solution)/shard_map/pallas_call | solution.py:486
  78.0 4.3 %shard_map.293 = (f32[1536,256]{1,0:T(8,128)S(1)}, f32[8,768]{1,0:T(8,128)S(1)}) custom-call(s32[10]{0:T(128)S(1)} %pad_add_fusion.refs_0_, bf16[1536,768]{1,0:T(8,128)(2,1)S(1)} %get-tuple-element.99.refs_1_.refs_3_, bf16[1536,768]{1,0:T(8,128)(2,1)S(1)} %get-tuple-element.100.refs_2_.refs_4_, f32[512,768]{1,0:T(8,128)S(1)} %copy-done.12, ...), custom_call_target="tpu_custom_call" | custom-call | flops 20000000000 | bytes 40000000 | tf_op jit(solution)/shard_map/pallas_call | solution.py:486
  90.5 6.8 %shard_map.294 = (bf16[1536,512]{1,0:T(8,128)(2,1)S(1)}, bf16[1536,512]{1,0:T(8,128)(2,1)S(1)}, bf16[1536,768]{1,0:T(8,128)(2,1)S(1)}, bf16[1536,768]{1,0:T(8,12...) custom-call(s32[10]{0:T(128)S(1)} %pad_add_fusion.refs_0_, ...), custom_call_target="tpu_custom_call" | custom-call | flops 450000000 | bytes 900000 | tf_op jit(solution)/shard_map/pallas_call | solution.py:486
  101.0 9.1 %shard_map.295 = (f32[4,128,768]{2,1,0:T(8,128)S(1)}, f32[4,128,768]{2,1,0:T(8,128)S(1)}) custom-call(s32[10]{0:T(128)S(1)} %pad_add_fusion.refs_0_, bf16[1536,1024]{1,0:T(8,128)(2,1)S(1)} %copy-done.20, bf16[1536,1024]{1,0:T(8,128)(2,1)S(1)} %copy-done.22, bf16[1536,768]{1,0:T(8,128)(2,1)S(1)} %get-tuple-element.106.refs_3_.refs_1_, ...), custom_call_target="tpu_custom_call" | custom-call | flops 500000000 | bytes 1000000 | tf_op jit(solution)/shard_map/pallas_call | solution.py:486
  115.9 9.8 %shard_map.297 = (f32[1536,256]{1,0:T(8,128)S(1)}, f32[1536,256]{1,0:T(8,128)S(1)}, f32[1536,256]{1,0:T(8,128)S(1)}, f32[1536,256]{1,0:T(8,128)S(1)}) custom-call(s32[10]{0:T(128)S(1)} %pad_add_fusion.refs_0_, bf16[1536,768]{1,0:T(8,128)(2,1)S(1)} %get-tuple-element.106.refs_3_.refs_1_, bf16[1536,768]{1,0:T(8,128)(2,1)S(1)} %get-tuple-element.107.refs_4_.refs_2_, ...), custom_call_target="tpu_custom_call" | custom-call | flops 450000000 | bytes 900000 | tf_op jit(solution)/shard_map/pallas_call | solution.py:486
  125.8 7.9 %shard_map.298 = (bf16[1536,128]{1,0:T(8,128)(2,1)S(1)}, bf16[1536,128]{1,0:T(8,128)(2,1)S(1)}, f32[1536,256]{1,0:T(8,128)S(1)}, f32[1536,256]{1,0:T(8,128)S(1)}...) custom-call(s32[10]{0:T(128)S(1)} %pad_add_fusion.refs_0_, ...), custom_call_target="tpu_custom_call" | custom-call | flops 400000000 | bytes 800000 | tf_op jit(solution)/shard_map/pallas_call | solution.py:486
  133.9 7.2 %shard_map.299 = (f32[1536,256]{1,0:T(8,128)S(1)}, f32[1536,256]{1,0:T(8,128)S(1)}, f32[8,1024]{1,0:T(8,128)S(1)}) custom-call(s32[10]{0:T(128)S(1)} %pad_add_fusion.refs_0_, bf16[1536,128]{1,0:T(8,128)(2,1)S(1)} %get-tuple-element.122.refs_1_.refs_3_, bf16[1536,128]{1,0:T(8,128)(2,1)S(1)} %get-tuple-element.123.refs_2_.refs_4_, ...), custom_call_target="tpu_custom_call" | custom-call | flops 350000000 | bytes 700000 | tf_op jit(solution)/shard_map/pallas_call | solution.py:486
  147.2 9.1 %shard_map.300 = (f32[4,128,768]{2,1,0:T(8,128)S(1)}, f32[4,128,768]{2,1,0:T(8,128)S(1)}) custom-call(s32[10]{0:T(128)S(1)} %pad_add_fusion.2.refs_0_, bf16[1536,1024]{1,0:T(8,128)(2,1)S(1)} %copy-done.7, bf16[1536,1024]{1,0:T(8,128)(2,1)S(1)} %copy-done.9, bf16[1536,768]{1,0:T(8,128)(2,1)S(1)} %get-tuple-element.120.refs_5_.refs_3_, ...), custom_call_target="tpu_custom_call" | custom-call | flops 500000000 | bytes 1000000 | tf_op jit(solution)/shard_map/pallas_call | solution.py:486
  159.7 5.1 %shard_map.301 = (f32[4,64,768]{2,1,0:T(8,128)S(1)}, f32[4,64,768]{2,1,0:T(8,128)S(1)}) custom-call(s32[10]{0:T(128)S(1)} %pad_add_fusion.refs_0_, bf16[1536,512]{1,0:T(8,128)(2,1)S(1)} %get-tuple-element.139.refs_1_, bf16[1536,512]{1,0:T(8,128)(2,1)S(1)} %get-tuple-element.140.refs_2_, bf16[1536,768]{1,0:T(8,128)(2,1)S(1)} %copy-done.24, ...), custom_call_target="tpu_custom_call" | custom-call | flops 500000000 | bytes 1000000 | tf_op jit(solution)/shard_map/pallas_call | solution.py:486
  164.9 4.9 %shard_map.303 = (f32[4,136,128]{2,1,0:T(8,128)S(1)}, f32[4,136,128]{2,1,0:T(8,128)S(1)}) custom-call(s32[10]{0:T(128)S(1)} %pad_add_fusion.refs_0_, bf16[1536,1024]{1,0:T(8,128)(2,1)S(1)} %copy-done.7, bf16[1536,1024]{1,0:T(8,128)(2,1)S(1)} %copy-done.9, bf16[1536,128]{1,0:T(8,128)(2,1)S(1)} %get-tuple-element.122.refs_1_.refs_3_, ...), custom_call_target="tpu_custom_call" | custom-call | flops 250000000 | bytes 500000 | tf_op jit(solution)/shard_map/pallas_call | solution.py:486
  169.8 9.0 %collective-permute-done.16 = f32[4,128,768]{2,1,0:T(8,128)S(1)} collective-permute-done((f32[4,128,768]{2,1,0:T(8,128)S(1)}, f32[4,128,768]{2,1,0:T(8,128)S(1)}, u32[]{:S(2)}, u32[]{:S(2)}) %collective-permute-start.16) | collective-permute-done | bytes 1572896 | tf_op jit(solution)/shard_map/ppermute | solution.py:500
  185.0 9.9 %collective-permute-done.22 = f32[4,128,768]{2,1,0:T(8,128)S(1)} collective-permute-done((f32[4,128,768]{2,1,0:T(8,128)S(1)}, f32[4,128,768]{2,1,0:T(8,128)S(1)}, u32[]{:S(2)}, u32[]{:S(2)}) %collective-permute-start.22) | collective-permute-done | bytes 1572896 | tf_op jit(solution)/shard_map/ppermute | solution.py:500
  196.5 5.3 %collective-permute-done.21 = f32[4,64,768]{2,1,0:T(8,128)S(1)} collective-permute-done((f32[4,64,768]{2,1,0:T(8,128)S(1)}, f32[4,64,768]{2,1,0:T(8,128)S(1)}, u32[]{:S(2)}, u32[]{:S(2)}) %collective-permute-start.21) | collective-permute-done | bytes 786464 | tf_op jit(solution)/shard_map/ppermute | solution.py:500
  204.1 6.7 %collective-permute-done.20 = f32[2,128,768]{2,1,0:T(8,128)S(1)} collective-permute-done((f32[2,128,768]{2,1,0:T(8,128)S(1)}, f32[2,128,768]{2,1,0:T(8,128)S(1)}, u32[]{:S(2)}, u32[]{:S(2)}) %collective-permute-start.20) | collective-permute-done | bytes 786464 | tf_op jit(solution)/shard_map/ppermute | solution.py:500
  211.8 6.0 %collective-permute-done.25.refs_5_ = f32[1536,256]{1,0:T(8,128)} collective-permute-done((f32[1536,256]{1,0:T(8,128)S(1)}, f32[1536,256]{1,0:T(8,128)}, u32[]{:S(2)}, u32[]{:S(2)}) %collective-permute-start.25) | collective-permute-done | bytes 1572896 | tf_op jit(solution)/shard_map/ppermute | solution.py:495
  224.1 4.7 %collective-permute-start.36 = (f32[1,128,768]{2,1,0:T(8,128)S(1)}, f32[1,128,768]{2,1,0:T(8,128)S(1)}, u32[]{:S(2)}, u32[]{:S(2)}) collective-permute-start(f32[1,128,768]{2,1,0:T(8,128)S(1)} %copy-done.49), channel_id=1, source_target_pairs={{0,16},{4,20},{8,24},{12,28},{16,0},{20,4},{24,8},{28,12},{1,17},{... | collective-permute-start | bytes 1179656 | tf_op jit(solution)/shard_map/ppermute | solution.py:500
  233.8 10.3 %shard_map.304 = f32[1536,1024]{1,0:T(8,128)} custom-call(s32[10]{0:T(128)S(1)} %pad_add_fusion.refs_0_, f32[1536,1024]{1,0:T(8,128)S(1)} %copy-done.1, f32[1,1024]{1,0:T(1,128)S(1)} %bitcast.46, f32[1536,256]{1,0:T(8,128)S(1)} %add.95.refs_3_, f32[1536,256]{1,0:T(8,128)} %collective-permute-done.24.refs_4_, f32[1536,256]{1,0:T(8,128)} %collective-permute-done.25.refs_5_, ...), custom_call_target="tpu_custom_call" | custom-call | flops 450000000 | bytes 900000 | tf_op jit(solution)/shard_map/pallas_call | solution.py:486
  250.6 4.3 %collective-permute-done.27 = f32[1536,256]{1,0:T(8,128)} collective-permute-done((f32[1536,256]{1,0:T(8,128)}, f32[1536,256]{1,0:T(8,128)}, u32[]{:S(2)}, u32[]{:S(2)}) %collective-permute-start.27) | collective-permute-done | bytes 1572896 | tf_op jit(solution)/shard_map/ppermute | solution.py:495
  257.7 7.6 %collective-permute-done.31 = f32[1,136,128]{2,1,0:T(8,128)S(1)} collective-permute-done((f32[1,136,128]{2,1,0:T(8,128)S(1)}, f32[1,136,128]{2,1,0:T(8,128)S(1)}, u32[]{:S(2)}, u32[]{:S(2)}) %collective-permute-start.31) | collective-permute-done | bytes 69664 | tf_op jit(solution)/shard_map/ppermute | solution.py:500
  273.9 3.6 %collective-permute-done.34 = f32[1,128,768]{2,1,0:T(8,128)S(1)} collective-permute-done((f32[1,128,768]{2,1,0:T(8,128)S(1)}, f32[1,128,768]{2,1,0:T(8,128)S(1)}, u32[]{:S(2)}, u32[]{:S(2)}) %collective-permute-start.34) | collective-permute-done | bytes 393248 | tf_op jit(solution)/shard_map/ppermute | solution.py:500
  (221 shorter events, 104.1 us)
Async XLA Ops:
  0.6 51.7 %collective-permute-start.6 = (f32[1536,256]{1,0:T(8,128)}, f32[1536,256]{1,0:T(8,128)}, u32[]{:S(2)}, u32[]{:S(2)}) collective-permute-start(f32[1536,256]{1,0:T(8,128)} %refs_7_.7), channel_id=1, source_target_pairs={{0,2},{1,3},{2,0},{3,1},{4,6},{5,7},{6,4},{7,5},{8,10},{9,11},{10,... | collective-permute-start | bytes 4718600 | tf_op jit(solution)/shard_map/ppermute | solution.py:495
  31.1 22.0 %collective-permute-start.5 = (f32[1536,256]{1,0:T(8,128)}, f32[1536,256]{1,0:T(8,128)}, u32[]{:S(2)}, u32[]{:S(2)}) collective-permute-start(f32[1536,256]{1,0:T(8,128)} %refs_7_.7), channel_id=1, source_target_pairs={{0,1},{1,0},{2,3},{3,2},{4,5},{5,4},{6,7},{7,6},{8,9},{9,8},{10,11... | collective-permute-start | bytes 4718600 | tf_op jit(solution)/shard_map/ppermute | solution.py:495
  52.4 31.1 %collective-permute-start.4 = (f32[1536,128]{1,0:T(8,128)S(1)}, f32[1536,128]{1,0:T(8,128)S(1)}, u32[]{:S(2)}, u32[]{:S(2)}) collective-permute-start(f32[1536,128]{1,0:T(8,128)S(1)} %get-tuple-element.94.refs_4_.refs_1_), channel_id=1, source_target_pairs={{0,2},{1,3},{2,0},{3,1},{4,6},{5,7},{6,4},{7,5},{8,10},{9,11},{10,... | collective-permute-start | bytes 2359304 | tf_op jit(solution)/shard_map/ppermute | solution.py:495
  52.9 31.4 %collective-permute-start.3 = (f32[1536,128]{1,0:T(8,128)S(1)}, f32[1536,128]{1,0:T(8,128)S(1)}, u32[]{:S(2)}, u32[]{:S(2)}) collective-permute-start(f32[1536,128]{1,0:T(8,128)S(1)} %get-tuple-element.94.refs_4_.refs_1_), channel_id=1, source_target_pairs={{0,1},{1,0},{2,3},{3,2},{4,5},{5,4},{6,7},{7,6},{8,9},{9,8},{10,11... | collective-permute-start | bytes 2359304 | tf_op jit(solution)/shard_map/ppermute | solution.py:495
  83.7 26.4 %collective-permute-start.10 = (f32[1536,128]{1,0:T(8,128)S(1)}, f32[1536,128]{1,0:T(8,128)S(1)}, u32[]{:S(2)}, u32[]{:S(2)}) collective-permute-start(f32[1536,128]{1,0:T(8,128)S(1)} %slice_add_fusion.refs_10_), channel_id=1, source_target_pairs={{0,2},{1,3},{2,0},{3,1},{4,6},{5,7},{6,4},{7,5},{8,10},{9,11},{10,... | collective-permute-start | bytes 2359304 | tf_op jit(solution)/shard_map/ppermute | solution.py:495
  111.7 14.0 %collective-permute-start.11 = (f32[8,128]{1,0:T(8,128)S(1)}, f32[8,128]{1,0:T(8,128)S(1)}, u32[]{:S(2)}, u32[]{:S(2)}) collective-permute-start(f32[8,128]{1,0:T(8,128)S(1)} %get-tuple-element.113.refs_6_), channel_id=1, source_target_pairs={{4,0},{8,4},{12,8},{16,12},{20,16},{24,20},{28,24},{5,1},{9,5},{13... | collective-permute-start | bytes 12296 | tf_op jit(solution)/shard_map/ppermute | solution.py:506
  113.0 12.7 %collective-permute-start.12 = (f32[8,128]{1,0:T(8,128)S(1)}, f32[8,128]{1,0:T(8,128)S(1)}, u32[]{:S(2)}, u32[]{:S(2)}) collective-permute-start(f32[8,128]{1,0:T(8,128)S(1)} %get-tuple-element.113.refs_6_), channel_id=1, source_target_pairs={{8,0},{12,4},{16,8},{20,12},{24,16},{28,20},{9,1},{13,5},{17,9},{2... | collective-permute-start | bytes 12296 | tf_op jit(solution)/shard_map/ppermute | solution.py:506
  141.5 37.3 %collective-permute-start.16 = (f32[4,128,768]{2,1,0:T(8,128)S(1)}, f32[4,128,768]{2,1,0:T(8,128)S(1)}, u32[]{:S(2)}, u32[]{:S(2)}) collective-permute-start(f32[4,128,768]{2,1,0:T(8,128)S(1)} %get-tuple-element.132), channel_id=1, source_target_pairs={{0,4},{4,0},{8,12},{12,8},{16,20},{20,16},{24,28},{28,24},{1,5},{5... | collective-permute-start | bytes 4718600 | tf_op jit(solution)/shard_map/ppermute | solution.py:500
  144.4 36.2 %collective-permute-start.17 = (f32[1536,256]{1,0:T(8,128)S(1)}, f32[1536,256]{1,0:T(8,128)S(1)}, u32[]{:S(2)}, u32[]{:S(2)}) collective-permute-start(f32[1536,256]{1,0:T(8,128)S(1)} %add.92), channel_id=1, source_target_pairs={{0,2},{1,3},{2,0},{3,1},{4,6},{5,7},{6,4},{7,5},{8,10},{9,11},{10,... | collective-permute-start | bytes 4718600 | tf_op jit(solution)/shard_map/ppermute | solution.py:495
  156.3 38.6 %collective-permute-start.22 = (f32[4,128,768]{2,1,0:T(8,128)S(1)}, f32[4,128,768]{2,1,0:T(8,128)S(1)}, u32[]{:S(2)}, u32[]{:S(2)}) collective-permute-start(f32[4,128,768]{2,1,0:T(8,128)S(1)} %get-tuple-element.150), channel_id=1, source_target_pairs={{0,8},{4,12},{8,0},{12,4},{16,24},{20,28},{24,16},{28,20},{1,9},{5... | collective-permute-start | bytes 4718600 | tf_op jit(solution)/shard_map/ppermute | solution.py:500
  180.7 22.0 %collective-permute-start.23 = (f32[1536,256]{1,0:T(8,128)S(1)}, f32[1536,256]{1,0:T(8,128)S(1)}, u32[]{:S(2)}, u32[]{:S(2)}) collective-permute-start(f32[1536,256]{1,0:T(8,128)S(1)} %get-tuple-element.155), channel_id=1, source_target_pairs={{0,1},{1,0},{2,3},{3,2},{4,5},{5,4},{6,7},{7,6},{8,9},{9,8},{10,11... | collective-permute-start | bytes 4718600 | tf_op jit(solution)/shard_map/ppermute | solution.py:495
  180.8 36.9 %collective-permute-start.25 = (f32[1536,256]{1,0:T(8,128)S(1)}, f32[1536,256]{1,0:T(8,128)}, u32[]{:S(2)}, u32[]{:S(2)}) collective-permute-start(f32[1536,256]{1,0:T(8,128)S(1)} %add.95.refs_3_), channel_id=1, source_target_pairs={{0,2},{1,3},{2,0},{3,1},{4,6},{5,7},{6,4},{7,5},{8,10},{9,11},{10,... | collective-permute-start | bytes 4718600 | tf_op jit(solution)/shard_map/ppermute | solution.py:495
  181.4 20.4 %collective-permute-start.21 = (f32[4,64,768]{2,1,0:T(8,128)S(1)}, f32[4,64,768]{2,1,0:T(8,128)S(1)}, u32[]{:S(2)}, u32[]{:S(2)}) collective-permute-start(f32[4,64,768]{2,1,0:T(8,128)S(1)} %get-tuple-element.149), channel_id=1, source_target_pairs={{0,4},{4,0},{8,12},{12,8},{16,20},{20,16},{24,28},{28,24},{1,5},{5... | collective-permute-start | bytes 2359304 | tf_op jit(solution)/shard_map/ppermute | solution.py:500
  181.7 29.1 %collective-permute-start.20 = (f32[2,128,768]{2,1,0:T(8,128)S(1)}, f32[2,128,768]{2,1,0:T(8,128)S(1)}, u32[]{:S(2)}, u32[]{:S(2)}) collective-permute-start(f32[2,128,768]{2,1,0:T(8,128)S(1)} %get-tuple-element.170), channel_id=1, source_target_pairs={{0,8},{4,12},{8,0},{12,4},{16,24},{20,28},{24,16},{28,20},{1,9},{5... | collective-permute-start | bytes 2359304 | tf_op jit(solution)/shard_map/ppermute | solution.py:500
  194.9 16.8 %collective-permute-start.19 = (f32[4,136,128]{2,1,0:T(8,128)S(1)}, f32[4,136,128]{2,1,0:T(8,128)S(1)}, u32[]{:S(2)}, u32[]{:S(2)}) collective-permute-start(f32[4,136,128]{2,1,0:T(8,128)S(1)} %get-tuple-element.147), channel_id=1, source_target_pairs={{0,4},{4,0},{8,12},{12,8},{16,20},{20,16},{24,28},{28,24},{1,5},{5... | collective-permute-start | bytes 835592 | tf_op jit(solution)/shard_map/ppermute | solution.py:500
  202.8 16.3 %collective-permute-start.18 = (f32[1536,256]{1,0:T(8,128)S(1)}, f32[1536,256]{1,0:T(8,128)}, u32[]{:S(2)}, u32[]{:S(2)}) collective-permute-start(f32[1536,256]{1,0:T(8,128)S(1)} %get-tuple-element.146), channel_id=1, source_target_pairs={{0,1},{1,0},{2,3},{3,2},{4,5},{5,4},{6,7},{7,6},{8,9},{9,8},{10,11... | collective-permute-start | bytes 4718600 | tf_op jit(solution)/shard_map/ppermute | solution.py:495
  218.2 25.9 %collective-permute-start.30 = (f32[2,128,768]{2,1,0:T(8,128)}, f32[2,128,768]{2,1,0:T(8,128)}, u32[]{:S(2)}, u32[]{:S(2)}) collective-permute-start(f32[2,128,768]{2,1,0:T(8,128)} %get-tuple-element.168), channel_id=1, source_target_pairs={{0,4},{4,0},{8,12},{12,8},{16,20},{20,16},{24,28},{28,24},{1,5},{5... | collective-permute-start | bytes 2359304 | tf_op jit(solution)/shard_map/ppermute | solution.py:500
  218.6 36.3 %collective-permute-start.27 = (f32[1536,256]{1,0:T(8,128)}, f32[1536,256]{1,0:T(8,128)}, u32[]{:S(2)}, u32[]{:S(2)}) collective-permute-start(f32[1536,256]{1,0:T(8,128)} %add.100), channel_id=1, source_target_pairs={{0,2},{1,3},{2,0},{3,1},{4,6},{5,7},{6,4},{7,5},{8,10},{9,11},{10,... | collective-permute-start | bytes 4718600 | tf_op jit(solution)/shard_map/ppermute | solution.py:495
  219.1 26.2 %collective-permute-start.29 = (f32[2,64,768]{2,1,0:T(8,128)}, f32[2,64,768]{2,1,0:T(8,128)}, u32[]{:S(2)}, u32[]{:S(2)}) collective-permute-start(f32[2,64,768]{2,1,0:T(8,128)} %get-tuple-element.172), channel_id=1, source_target_pairs={{0,8},{4,12},{8,0},{12,4},{16,24},{20,28},{24,16},{28,20},{1,9},{5... | collective-permute-start | bytes 1179656 | tf_op jit(solution)/shard_map/ppermute | solution.py:500
  224.1 22.8 %collective-permute-start.36 = (f32[1,128,768]{2,1,0:T(8,128)S(1)}, f32[1,128,768]{2,1,0:T(8,128)S(1)}, u32[]{:S(2)}, u32[]{:S(2)}) collective-permute-start(f32[1,128,768]{2,1,0:T(8,128)S(1)} %copy-done.49), channel_id=1, source_target_pairs={{0,16},{4,20},{8,24},{12,28},{16,0},{20,4},{24,8},{28,12},{1,17},{... | collective-permute-start | bytes 1179656 | tf_op jit(solution)/shard_map/ppermute | solution.py:500
  228.8 17.5 %collective-permute-start.28 = (f32[2,136,128]{2,1,0:T(8,128)S(1)}, f32[2,136,128]{2,1,0:T(8,128)S(1)}, u32[]{:S(2)}, u32[]{:S(2)}) collective-permute-start(f32[2,136,128]{2,1,0:T(8,128)S(1)} %get-tuple-element.174.refs_11_), channel_id=1, source_target_pairs={{0,8},{4,12},{8,0},{12,4},{16,24},{20,28},{24,16},{28,20},{1,9},{5... | collective-permute-start | bytes 417800 | tf_op jit(solution)/shard_map/ppermute | solution.py:500
  246.3 18.9 %collective-permute-start.31 = (f32[1,136,128]{2,1,0:T(8,128)S(1)}, f32[1,136,128]{2,1,0:T(8,128)S(1)}, u32[]{:S(2)}, u32[]{:S(2)}) collective-permute-start(f32[1,136,128]{2,1,0:T(8,128)S(1)} %slice_add_fusion.15), channel_id=1, source_target_pairs={{0,16},{4,20},{8,24},{12,28},{16,0},{20,4},{24,8},{28,12},{1,17},{... | collective-permute-start | bytes 208904 | tf_op jit(solution)/shard_map/ppermute | solution.py:500
  247.7 24.5 %collective-permute-start.35 = (f32[1,64,768]{2,1,0:T(8,128)S(1)}, f32[1,64,768]{2,1,0:T(8,128)S(1)}, u32[]{:S(2)}, u32[]{:S(2)}) collective-permute-start(f32[1,64,768]{2,1,0:T(8,128)S(1)} %slice_add_fusion.12), channel_id=1, source_target_pairs={{0,16},{4,20},{8,24},{12,28},{16,0},{20,4},{24,8},{28,12},{1,17},{... | collective-permute-start | bytes 589832 | tf_op jit(solution)/shard_map/ppermute | solution.py:500
  250.2 27.3 %collective-permute-start.34 = (f32[1,128,768]{2,1,0:T(8,128)S(1)}, f32[1,128,768]{2,1,0:T(8,128)S(1)}, u32[]{:S(2)}, u32[]{:S(2)}) collective-permute-start(f32[1,128,768]{2,1,0:T(8,128)S(1)} %slice_add_fusion.7), channel_id=1, source_target_pairs={{0,16},{4,20},{8,24},{12,28},{16,0},{20,4},{24,8},{28,12},{1,17},{... | collective-permute-start | bytes 1179656 | tf_op jit(solution)/shard_map/ppermute | solution.py:500
  (71 other events, 522.1 us)

commit v4 on v3

--- a/solution.py
+++ b/solution.py
@@ -705,18 +705,8 @@
     )
     back_gots = [seq_shift(back_end, -hop) for hop in range(1, hops + 1)]
 
-    out_send, out_keep, near_send, near_keep = call(
-        9,
-        output_kernel,
-        steps,
-        ids,
-        tiled(p_high, p_low)
-        + whole(w_down)
-        + [(inputs, tiles(inputs, column=part)), (b_down_row, pl.BlockSpec((1, part), lambda i, ids: (0, ids[0])))],
-        tiled(t(part), t(part), t(part), t(part)),
-        [((width, units), BF16)] * 2,
-        [back_end],
-    )
+    w_gate_keep, w_gate_send = weight((n_high, n_low), (gg_high, gg_low), ids_z, False, [back_end])
+    gate_total = ScatterSum(w_gate_keep, after(w_gate_send, *back_gots), (2, 1, 4))
     down_sum = ScatterSum(w_down_keep, after(w_down_send, *back_gots), (1, 2, 4))
     r_high, r_low, far_send, far_keep, turn_sum, red_sum, far_norm = call(
         8,
@@ -729,7 +719,7 @@
         tiled(t(own, dtype=BF16), t(own, dtype=BF16), t(part), t(part))
         + whole(shape(8, own), shape(8, own), shape(16, width)),
         [((2 * part, units), BF16)] * 2 + [((2 * part, own), BF16)] * 2 + [((TILE, width), F32)],
-        [near_keep],
+        [w_gate_keep],
     )
     far_recv = wa_swap(far_send, 1)
     next_send, next_keep, norm = call(
@@ -749,10 +739,20 @@
     next_recv = wa_swap(next_send, 1)
     near_sum = after(next_keep, far_sum) + next_recv
 
-    w_gate_keep, w_gate_send = weight((n_high, n_low), (gg_high, gg_low), ids_z, False, [near_sum])
-    gate_total = ScatterSum(w_gate_keep, w_gate_send, (2, 1, 4))
-    w_expand_keep, w_expand_send = weight((m_high, m_low), (ge_high, ge_low), ids, True, [w_gate_keep])
+    w_expand_keep, w_expand_send = weight((m_high, m_low), (ge_high, ge_low), ids, True, [near_sum])
     expand_total = ScatterSum(w_expand_keep, w_expand_send, (1, 2, 4))
+    out_send, out_keep, near_send, near_keep = call(
+        9,
+        output_kernel,
+        steps,
+        ids,
+        tiled(p_high, p_low)
+        + whole(w_down)
+        + [(inputs, tiles(inputs, column=part)), (b_down_row, pl.BlockSpec((1, part), lambda i, ids: (0, ids[0])))],
+        tiled(t(part), t(part), t(part), t(part)),
+        [((width, units), BF16)] * 2,
+        [w_expand_keep],
+    )
     [vector] = call(
         1.5,
         pack_kernel,
@@ -761,7 +761,7 @@
         whole(norm, c_sum, gg_sum, ge_sum, red_sum, turn_sum, out_sum),
         whole(shape(8 * seqs, 128)),
         [((8, max(width, units)), F32), ((8, width), F32)],
-        [w_expand_keep],
+        [near_keep],
     )
     half = shape(seqs // 2, width // seqs + 8, own)
     w_red_keep, w_red_send = call(

time: 280 us -> 279 us (level)
  waiting for transfers between devices: 61.7 us -> 49.3 us
  starting transfers between devices: 47.7 us -> 59.1 us
  local copies, waits for them, and re-layouts: 39.2 us -> 34.9 us
  Pallas kernels: 111 us -> 114 us
    ppermute x12, waiting for transfers between devices: 42.1 us -> 30.2 us  [seq_swap(): return lax.ppermute(value, 'seq', [(i, i ^ distance) for i in range(count)])]
    ppermute x19, starting transfers between devices: 8.5 us -> 18 us  [wa_swap(): return lax.ppermute(value, 'wa', [(i, i ^ distance) for i in range(count)])]
    unnamed x116 -> x148, local copies, waits for them, and re-layouts: 36.2 us -> 31.9 us
    pallas_call x16, Pallas kernels: 111 us -> 114 us  [call(): return run(*arrays) if ids is None else run(ids, *arrays)]
  transfers between devices with their start and end apart: 37 -> 37, of which waited for: 14 -> 11; matrix products, arithmetic and copies ran while one was open for 7% -> 7% of each run, Pallas kernels for 36% -> 38%
where the time goes in v4:
time: 279 us; the launch traced here: 278 us
  Pallas kernels  114 us (41%)
  starting transfers between devices  59.1 us (21%)
  waiting for transfers between devices  49.3 us (18%)
  local copies, waits for them, and re-layouts  34.9 us (13%)
  other arithmetic  18.6 us (7%)
    pallas_call x16, Pallas kernels, call(): return run(*arrays) if ids is None else run(ids, *arrays)  114 us
    unnamed x148, local copies, waits for them, and re-layouts  31.9 us
    ppermute x12, waiting for transfers between devices, seq_swap(): return lax.ppermute(value, 'seq', [(i, i ^ distance) for i in range(count)])  30.2 us
    ppermute x12, starting transfers between devices, seq_swap(): return lax.ppermute(value, 'seq', [(i, i ^ distance) for i in range(count)])  25.3 us
    ppermute x19, starting transfers between devices, wa_swap(): return lax.ppermute(value, 'wa', [(i, i ^ distance) for i in range(count)])  18 us
    ppermute x19, waiting for transfers between devices, wa_swap(): return lax.ppermute(value, 'wa', [(i, i ^ distance) for i in range(count)])  17.9 us
    ppermute x6, starting transfers between devices, seq_shift(): return lax.ppermute(value, 'seq', pairs)  15.8 us
  transfers between devices with their start and end apart: 37, of which 11 were waited for; matrix products, arithmetic and copies ran while one was open for 7% of the time, Pallas kernels for 38%

profile of v4, /device:TPU:0, one launch (start us, length us, event | category | flops | bytes accessed | tf_op | source)
XLA Modules:
  0.0 277.6 jit_solution(3178748458944936133)
XLA Ops:
  12.1 7.0 %shard_map.289 = (bf16[1536,1024]{1,0:T(8,128)(2,1)S(1)}, bf16[1536,1024]{1,0:T(8,128)(2,1)S(1)}, f32[1536,128]{1,0:T(8,128)S(1)}, f32[1536,128]{1,0:T(8,128)S(1...) custom-call(f32[1536,1024]{1,0:T(8,128)S(1)} %copy-done, f32[1,1024]{1,0:T(1,128)S(1)} %bitcast.47, ...), custom_call_target="tpu_custom_call" | custom-call | flops 350000000 | bytes 700000 | tf_op jit(solution)/shard_map/pallas_call | solution.py:486
  20.1 3.4 %collective-permute-start = (f32[8,128]{1,0:T(8,128)S(1)}, f32[8,128]{1,0:T(8,128)S(1)}, u32[]{:S(2)}, u32[]{:S(2)}) collective-permute-start(f32[8,128]{1,0:T(8,128)S(1)} %get-tuple-element.94), channel_id=1, source_target_pairs={{0,4},{4,8},{8,12},{12,16},{16,20},{20,24},{24,28},{1,5},{5,9},{9,... | collective-permute-start | bytes 12296 | tf_op jit(solution)/shard_map/ppermute | solution.py:506
  23.4 3.5 %collective-permute-start.1 = (f32[8,128]{1,0:T(8,128)S(1)}, f32[8,128]{1,0:T(8,128)S(1)}, u32[]{:S(2)}, u32[]{:S(2)}) collective-permute-start(f32[8,128]{1,0:T(8,128)S(1)} %get-tuple-element.94), channel_id=1, source_target_pairs={{0,8},{4,12},{8,16},{12,20},{16,24},{20,28},{1,9},{5,13},{9,17},{1... | collective-permute-start | bytes 12296 | tf_op jit(solution)/shard_map/ppermute | solution.py:506
  26.9 4.5 %collective-permute-start.2 = (f32[8,128]{1,0:T(8,128)S(1)}, f32[8,128]{1,0:T(8,128)S(1)}, u32[]{:S(2)}, u32[]{:S(2)}) collective-permute-start(f32[8,128]{1,0:T(8,128)S(1)} %get-tuple-element.94), channel_id=1, source_target_pairs={{0,12},{4,16},{8,20},{12,24},{16,28},{1,13},{5,17},{9,21},{13,25},... | collective-permute-start | bytes 12296 | tf_op jit(solution)/shard_map/ppermute | solution.py:506
  34.9 11.7 %shard_map.291 = (f32[1536,768]{1,0:T(8,128)S(1)}, f32[1536,768]{1,0:T(8,128)S(1)}) custom-call(bf16[1536,1024]{1,0:T(8,128)(2,1)S(1)} %get-tuple-element.96.refs_0_.refs_1_, bf16[1536,1024]{1,0:T(8,128)(2,1)S(1)} %get-tuple-element.97.refs_1_.refs_2_, f32[1024,768]{1,0:T(8,128)S(1)} %copy-done.4, f32[1,768]{1,0:T(1,128)S(1)} %broadcast_in_dim.40.refs_3_, ...), custom_call_target="tpu_custom_call" | custom-call | flops 600000000 | bytes 1200000 | tf_op jit(solution)/shard_map/pallas_call | solution.py:486
  62.0 16.8 %shard_map.292 = (bf16[1536,1024]{1,0:T(8,128)(2,1)S(1)}, bf16[1536,1024]{1,0:T(8,128)(2,1)S(1)}, f32[1536,768]{1,0:T(8,128)S(1)}, bf16[1536,768]{1,0:T(8,128)(2...) custom-call(s32[10]{0:T(128)S(1)} %pad_add_fusion.refs_0_, ...), custom_call_target="tpu_custom_call" | custom-call | flops 850000000 | bytes 1700000 | tf_op jit(solution)/shard_map/pallas_call | solution.py:486
  79.0 4.3 %shard_map.293 = (f32[1536,256]{1,0:T(8,128)S(1)}, f32[8,768]{1,0:T(8,128)S(1)}) custom-call(s32[10]{0:T(128)S(1)} %pad_add_fusion.refs_0_, bf16[1536,768]{1,0:T(8,128)(2,1)S(1)} %get-tuple-element.100.refs_1_.refs_3_, bf16[1536,768]{1,0:T(8,128)(2,1)S(1)} %get-tuple-element.101.refs_2_.refs_4_, f32[512,768]{1,0:T(8,128)S(1)} %copy-done.17, ...), custom_call_target="tpu_custom_call" | custom-call | flops 20000000000 | bytes 40000000 | tf_op jit(solution)/shard_map/pallas_call | solution.py:486
  90.6 7.0 %shard_map.294 = (bf16[1536,512]{1,0:T(8,128)(2,1)S(1)}, bf16[1536,512]{1,0:T(8,128)(2,1)S(1)}, bf16[1536,768]{1,0:T(8,128)(2,1)S(1)}, bf16[1536,768]{1,0:T(8,12...) custom-call(s32[10]{0:T(128)S(1)} %pad_add_fusion.refs_0_, ...), custom_call_target="tpu_custom_call" | custom-call | flops 450000000 | bytes 900000 | tf_op jit(solution)/shard_map/pallas_call | solution.py:486
  97.7 10.5 %shard_map.295 = (f32[4,128,768]{2,1,0:T(8,128)S(1)}, f32[4,128,768]{2,1,0:T(8,128)}) custom-call(s32[10]{0:T(128)S(1)} %pad_add_fusion.refs_0_, bf16[1536,1024]{1,0:T(8,128)(2,1)S(1)} %get-tuple-element.112.refs_1_, bf16[1536,1024]{1,0:T(8,128)(2,1)S(1)} %get-tuple-element.113.refs_2_, bf16[1536,768]{1,0:T(8,128)(2,1)S(1)} %get-tuple-element.107.refs_3_.refs_1_, ...), custom_call_target="tpu_custom_call" | custom-call | flops 500000000 | bytes 1000000 | tf_op jit(solution)/shard_map/pallas_call | solution.py:486
  114.4 9.2 %shard_map.297 = (f32[4,128,768]{2,1,0:T(8,128)S(1)}, f32[4,128,768]{2,1,0:T(8,128)S(1)}) custom-call(s32[10]{0:T(128)S(1)} %pad_add_fusion.2.refs_0_, bf16[1536,1024]{1,0:T(8,128)(2,1)S(1)} %copy-done.6, bf16[1536,1024]{1,0:T(8,128)(2,1)S(1)} %copy-done.8, bf16[1536,768]{1,0:T(8,128)(2,1)S(1)} %get-tuple-element.120.refs_3_.refs_5_, ...), custom_call_target="tpu_custom_call" | custom-call | flops 500000000 | bytes 1000000 | tf_op jit(solution)/shard_map/pallas_call | solution.py:486
  123.7 8.1 %shard_map.298 = (bf16[1536,128]{1,0:T(8,128)(2,1)S(1)}, bf16[1536,128]{1,0:T(8,128)(2,1)S(1)}, f32[1536,256]{1,0:T(8,128)S(1)}, f32[1536,256]{1,0:T(8,128)S(1)}...) custom-call(s32[10]{0:T(128)S(1)} %pad_add_fusion.refs_0_, ...), custom_call_target="tpu_custom_call" | custom-call | flops 400000000 | bytes 800000 | tf_op jit(solution)/shard_map/pallas_call | solution.py:486
  132.1 7.4 %shard_map.299 = (f32[1536,256]{1,0:T(8,128)S(1)}, f32[1536,256]{1,0:T(8,128)S(1)}, f32[8,1024]{1,0:T(8,128)S(1)}) custom-call(s32[10]{0:T(128)S(1)} %pad_add_fusion.refs_0_, bf16[1536,128]{1,0:T(8,128)(2,1)S(1)} %get-tuple-element.124.refs_1_.refs_3_, bf16[1536,128]{1,0:T(8,128)(2,1)S(1)} %get-tuple-element.125.refs_2_.refs_4_, ...), custom_call_target="tpu_custom_call" | custom-call | flops 350000000 | bytes 700000 | tf_op jit(solution)/shard_map/pallas_call | solution.py:486
  143.8 3.3 %collective-permute-start.22 = (f32[4,128,768]{2,1,0:T(8,128)S(1)}, f32[4,128,768]{2,1,0:T(8,128)S(1)}, u32[]{:S(2)}, u32[]{:S(2)}) collective-permute-start(f32[4,128,768]{2,1,0:T(8,128)S(1)} %get-tuple-element.152), channel_id=1, source_target_pairs={{0,8},{4,12},{8,0},{12,4},{16,24},{20,28},{24,16},{28,20},{1,9},{5... | collective-permute-start | bytes 4718600 | tf_op jit(solution)/shard_map/ppermute | solution.py:500
  147.3 5.2 %shard_map.300 = (f32[4,64,768]{2,1,0:T(8,128)S(1)}, f32[4,64,768]{2,1,0:T(8,128)S(1)}) custom-call(s32[10]{0:T(128)S(1)} %pad_add_fusion.refs_0_, bf16[1536,512]{1,0:T(8,128)(2,1)S(1)} %copy-done.37, bf16[1536,512]{1,0:T(8,128)(2,1)S(1)} %get-tuple-element.110.refs_2_, bf16[1536,768]{1,0:T(8,128)(2,1)S(1)} %get-tuple-element.100.refs_1_.refs_3_, ...), custom_call_target="tpu_custom_call" | custom-call | flops 500000000 | bytes 1000000 | tf_op jit(solution)/shard_map/pallas_call | solution.py:486
  152.6 9.8 %shard_map.301 = (f32[1536,256]{1,0:T(8,128)S(1)}, f32[1536,256]{1,0:T(8,128)S(1)}, f32[1536,256]{1,0:T(8,128)S(1)}, f32[1536,256]{1,0:T(8,128)S(1)}) custom-call(s32[10]{0:T(128)S(1)} %pad_add_fusion.refs_0_, bf16[1536,768]{1,0:T(8,128)(2,1)S(1)} %copy-done.14, bf16[1536,768]{1,0:T(8,128)(2,1)S(1)} %copy-done.16, f32[1024,768]{1,0:T(8,128)S(1)} %copy-done.10, ...), custom_call_target="tpu_custom_call" | custom-call | flops 450000000 | bytes 900000 | tf_op jit(solution)/shard_map/pallas_call | solution.py:486
  162.5 4.9 %shard_map.303 = (f32[4,136,128]{2,1,0:T(8,128)S(1)}, f32[4,136,128]{2,1,0:T(8,128)S(1)}) custom-call(s32[10]{0:T(128)S(1)} %pad_add_fusion.refs_0_, bf16[1536,1024]{1,0:T(8,128)(2,1)S(1)} %copy-done.6, bf16[1536,1024]{1,0:T(8,128)(2,1)S(1)} %copy-done.8, bf16[1536,128]{1,0:T(8,128)(2,1)S(1)} %get-tuple-element.124.refs_1_.refs_3_, ...), custom_call_target="tpu_custom_call" | custom-call | flops 250000000 | bytes 500000 | tf_op jit(solution)/shard_map/pallas_call | solution.py:486
  167.4 9.9 %collective-permute-done.16 = f32[4,128,768]{2,1,0:T(8,128)S(1)} collective-permute-done((f32[4,128,768]{2,1,0:T(8,128)}, f32[4,128,768]{2,1,0:T(8,128)S(1)}, u32[]{:S(2)}, u32[]{:S(2)}) %collective-permute-start.16) | collective-permute-done | bytes 1572896 | tf_op jit(solution)/shard_map/ppermute | solution.py:500
  180.8 3.3 %collective-permute-start.20 = (f32[2,128,768]{2,1,0:T(8,128)S(1)}, f32[2,128,768]{2,1,0:T(8,128)S(1)}, u32[]{:S(2)}, u32[]{:S(2)}) collective-permute-start(f32[2,128,768]{2,1,0:T(8,128)S(1)} %get-tuple-element.172), channel_id=1, source_target_pairs={{0,8},{4,12},{8,0},{12,4},{16,24},{20,28},{24,16},{28,20},{1,9},{5... | collective-permute-start | bytes 2359304 | tf_op jit(solution)/shard_map/ppermute | solution.py:500
  186.9 13.7 %collective-permute-done.21 = f32[4,64,768]{2,1,0:T(8,128)S(1)} collective-permute-done((f32[4,64,768]{2,1,0:T(8,128)S(1)}, f32[4,64,768]{2,1,0:T(8,128)S(1)}, u32[]{:S(2)}, u32[]{:S(2)}) %collective-permute-start.21) | collective-permute-done | bytes 786464 | tf_op jit(solution)/shard_map/ppermute | solution.py:500
  205.8 10.2 %collective-permute-done.25.refs_5_ = f32[1536,256]{1,0:T(8,128)} collective-permute-done((f32[1536,256]{1,0:T(8,128)S(1)}, f32[1536,256]{1,0:T(8,128)}, u32[]{:S(2)}, u32[]{:S(2)}) %collective-permute-start.25) | collective-permute-done | bytes 1572896 | tf_op jit(solution)/shard_map/ppermute | solution.py:495
  224.3 4.1 %collective-permute-start.36 = (f32[1,128,768]{2,1,0:T(8,128)S(1)}, f32[1,128,768]{2,1,0:T(8,128)S(1)}, u32[]{:S(2)}, u32[]{:S(2)}) collective-permute-start(f32[1,128,768]{2,1,0:T(8,128)S(1)} %copy-done.63), channel_id=1, source_target_pairs={{0,16},{4,20},{8,24},{12,28},{16,0},{20,4},{24,8},{28,12},{1,17},{... | collective-permute-start | bytes 1179656 | tf_op jit(solution)/shard_map/ppermute | solution.py:500
  232.0 10.3 %shard_map.304 = f32[1536,1024]{1,0:T(8,128)} custom-call(s32[10]{0:T(128)S(1)} %pad_add_fusion.refs_0_, f32[1536,1024]{1,0:T(8,128)S(1)} %copy-done.1, f32[1,1024]{1,0:T(1,128)S(1)} %bitcast.48, f32[1536,256]{1,0:T(8,128)S(1)} %add.95.refs_3_, f32[1536,256]{1,0:T(8,128)} %collective-permute-done.24.refs_4_, f32[1536,256]{1,0:T(8,128)} %collective-permute-done.25.refs_5_, ...), custom_call_target="tpu_custom_call" | custom-call | flops 450000000 | bytes 900000 | tf_op jit(solution)/shard_map/pallas_call | solution.py:486
  259.0 8.4 %collective-permute-start.33 = (f32[8,128]{1,0:T(8,128)S(1)}, f32[8,128]{1,0:T(8,128)S(1)}, u32[]{:S(2)}, u32[]{:S(2)}) collective-permute-start(f32[8,128]{1,0:T(8,128)S(1)} %fusion.9), channel_id=1, source_target_pairs={{0,2},{1,3},{2,0},{3,1},{4,6},{5,7},{6,4},{7,5},{8,10},{9,11},{10,... | collective-permute-start | bytes 12296 | tf_op jit(solution)/shard_map/ppermute | solution.py:495
  271.2 4.7 %collective-permute-done.34 = f32[1,128,768]{2,1,0:T(8,128)S(1)} collective-permute-done((f32[1,128,768]{2,1,0:T(8,128)S(1)}, f32[1,128,768]{2,1,0:T(8,128)S(1)}, u32[]{:S(2)}, u32[]{:S(2)}) %collective-permute-start.34) | collective-permute-done | bytes 393248 | tf_op jit(solution)/shard_map/ppermute | solution.py:500
  (254 shorter events, 95.2 us)
Async XLA Ops:
  0.6 52.0 %collective-permute-start.6 = (f32[1536,256]{1,0:T(8,128)}, f32[1536,256]{1,0:T(8,128)}, u32[]{:S(2)}, u32[]{:S(2)}) collective-permute-start(f32[1536,256]{1,0:T(8,128)} %refs_7_.7), channel_id=1, source_target_pairs={{0,2},{1,3},{2,0},{3,1},{4,6},{5,7},{6,4},{7,5},{8,10},{9,11},{10,... | collective-permute-start | bytes 4718600 | tf_op jit(solution)/shard_map/ppermute | solution.py:495
  31.4 22.0 %collective-permute-start.5 = (f32[1536,256]{1,0:T(8,128)}, f32[1536,256]{1,0:T(8,128)}, u32[]{:S(2)}, u32[]{:S(2)}) collective-permute-start(f32[1536,256]{1,0:T(8,128)} %refs_7_.7), channel_id=1, source_target_pairs={{0,1},{1,0},{2,3},{3,2},{4,5},{5,4},{6,7},{7,6},{8,9},{9,8},{10,11... | collective-permute-start | bytes 4718600 | tf_op jit(solution)/shard_map/ppermute | solution.py:495
  52.7 30.6 %collective-permute-start.4 = (f32[1536,128]{1,0:T(8,128)}, f32[1536,128]{1,0:T(8,128)S(1)}, u32[]{:S(2)}, u32[]{:S(2)}) collective-permute-start(f32[1536,128]{1,0:T(8,128)} %copy-done.32), channel_id=1, source_target_pairs={{0,2},{1,3},{2,0},{3,1},{4,6},{5,7},{6,4},{7,5},{8,10},{9,11},{10,... | collective-permute-start | bytes 2359304 | tf_op jit(solution)/shard_map/ppermute | solution.py:495
  53.2 32.6 %collective-permute-start.3 = (f32[1536,128]{1,0:T(8,128)}, f32[1536,128]{1,0:T(8,128)S(1)}, u32[]{:S(2)}, u32[]{:S(2)}) collective-permute-start(f32[1536,128]{1,0:T(8,128)} %copy-done.32), channel_id=1, source_target_pairs={{0,1},{1,0},{2,3},{3,2},{4,5},{5,4},{6,7},{7,6},{8,9},{9,8},{10,11... | collective-permute-start | bytes 2359304 | tf_op jit(solution)/shard_map/ppermute | solution.py:495
  85.2 23.0 %collective-permute-start.10 = (f32[1536,128]{1,0:T(8,128)S(1)}, f32[1536,128]{1,0:T(8,128)S(1)}, u32[]{:S(2)}, u32[]{:S(2)}) collective-permute-start(f32[1536,128]{1,0:T(8,128)S(1)} %slice_add_fusion.refs_10_), channel_id=1, source_target_pairs={{0,2},{1,3},{2,0},{3,1},{4,6},{5,7},{6,4},{7,5},{8,10},{9,11},{10,... | collective-permute-start | bytes 2359304 | tf_op jit(solution)/shard_map/ppermute | solution.py:495
  109.9 13.7 %collective-permute-start.11 = (f32[8,128]{1,0:T(8,128)S(1)}, f32[8,128]{1,0:T(8,128)S(1)}, u32[]{:S(2)}, u32[]{:S(2)}) collective-permute-start(f32[8,128]{1,0:T(8,128)S(1)} %get-tuple-element.122.refs_5_), channel_id=1, source_target_pairs={{4,0},{8,4},{12,8},{16,12},{20,16},{24,20},{28,24},{5,1},{9,5},{13... | collective-permute-start | bytes 12296 | tf_op jit(solution)/shard_map/ppermute | solution.py:506
  111.5 12.2 %collective-permute-start.12 = (f32[8,128]{1,0:T(8,128)S(1)}, f32[8,128]{1,0:T(8,128)S(1)}, u32[]{:S(2)}, u32[]{:S(2)}) collective-permute-start(f32[8,128]{1,0:T(8,128)S(1)} %get-tuple-element.122.refs_5_), channel_id=1, source_target_pairs={{8,0},{12,4},{16,8},{20,12},{24,16},{28,20},{9,1},{13,5},{17,9},{2... | collective-permute-start | bytes 12296 | tf_op jit(solution)/shard_map/ppermute | solution.py:506
  139.8 37.4 %collective-permute-start.16 = (f32[4,128,768]{2,1,0:T(8,128)}, f32[4,128,768]{2,1,0:T(8,128)S(1)}, u32[]{:S(2)}, u32[]{:S(2)}) collective-permute-start(f32[4,128,768]{2,1,0:T(8,128)} %get-tuple-element.137), channel_id=1, source_target_pairs={{0,4},{4,0},{8,12},{12,8},{16,20},{20,16},{24,28},{28,24},{1,5},{5... | collective-permute-start | bytes 4718600 | tf_op jit(solution)/shard_map/ppermute | solution.py:500
  142.6 36.2 %collective-permute-start.17 = (f32[1536,256]{1,0:T(8,128)S(1)}, f32[1536,256]{1,0:T(8,128)S(1)}, u32[]{:S(2)}, u32[]{:S(2)}) collective-permute-start(f32[1536,256]{1,0:T(8,128)S(1)} %add.92), channel_id=1, source_target_pairs={{0,2},{1,3},{2,0},{3,1},{4,6},{5,7},{6,4},{7,5},{8,10},{9,11},{10,... | collective-permute-start | bytes 4718600 | tf_op jit(solution)/shard_map/ppermute | solution.py:495
  143.8 40.3 %collective-permute-start.22 = (f32[4,128,768]{2,1,0:T(8,128)S(1)}, f32[4,128,768]{2,1,0:T(8,128)S(1)}, u32[]{:S(2)}, u32[]{:S(2)}) collective-permute-start(f32[4,128,768]{2,1,0:T(8,128)S(1)} %get-tuple-element.152), channel_id=1, source_target_pairs={{0,8},{4,12},{8,0},{12,4},{16,24},{20,28},{24,16},{28,20},{1,9},{5... | collective-permute-start | bytes 4718600 | tf_op jit(solution)/shard_map/ppermute | solution.py:500
  179.0 22.6 %collective-permute-start.23 = (f32[1536,256]{1,0:T(8,128)S(1)}, f32[1536,256]{1,0:T(8,128)S(1)}, u32[]{:S(2)}, u32[]{:S(2)}) collective-permute-start(f32[1536,256]{1,0:T(8,128)S(1)} %get-tuple-element.157), channel_id=1, source_target_pairs={{0,1},{1,0},{2,3},{3,2},{4,5},{5,4},{6,7},{7,6},{8,9},{9,8},{10,11... | collective-permute-start | bytes 4718600 | tf_op jit(solution)/shard_map/ppermute | solution.py:495
  179.1 36.9 %collective-permute-start.25 = (f32[1536,256]{1,0:T(8,128)S(1)}, f32[1536,256]{1,0:T(8,128)}, u32[]{:S(2)}, u32[]{:S(2)}) collective-permute-start(f32[1536,256]{1,0:T(8,128)S(1)} %add.95.refs_3_), channel_id=1, source_target_pairs={{0,2},{1,3},{2,0},{3,1},{4,6},{5,7},{6,4},{7,5},{8,10},{9,11},{10,... | collective-permute-start | bytes 4718600 | tf_op jit(solution)/shard_map/ppermute | solution.py:495
  180.2 20.4 %collective-permute-start.21 = (f32[4,64,768]{2,1,0:T(8,128)S(1)}, f32[4,64,768]{2,1,0:T(8,128)S(1)}, u32[]{:S(2)}, u32[]{:S(2)}) collective-permute-start(f32[4,64,768]{2,1,0:T(8,128)S(1)} %get-tuple-element.150), channel_id=1, source_target_pairs={{0,4},{4,0},{8,12},{12,8},{16,20},{20,16},{24,28},{28,24},{1,5},{5... | collective-permute-start | bytes 2359304 | tf_op jit(solution)/shard_map/ppermute | solution.py:500
  180.8 22.1 %collective-permute-start.20 = (f32[2,128,768]{2,1,0:T(8,128)S(1)}, f32[2,128,768]{2,1,0:T(8,128)S(1)}, u32[]{:S(2)}, u32[]{:S(2)}) collective-permute-start(f32[2,128,768]{2,1,0:T(8,128)S(1)} %get-tuple-element.172), channel_id=1, source_target_pairs={{0,8},{4,12},{8,0},{12,4},{16,24},{20,28},{24,16},{28,20},{1,9},{5... | collective-permute-start | bytes 2359304 | tf_op jit(solution)/shard_map/ppermute | solution.py:500
  184.1 21.7 %collective-permute-start.19 = (f32[4,136,128]{2,1,0:T(8,128)S(1)}, f32[4,136,128]{2,1,0:T(8,128)S(1)}, u32[]{:S(2)}, u32[]{:S(2)}) collective-permute-start(f32[4,136,128]{2,1,0:T(8,128)S(1)} %get-tuple-element.148), channel_id=1, source_target_pairs={{0,4},{4,0},{8,12},{12,8},{16,20},{20,16},{24,28},{28,24},{1,5},{5... | collective-permute-start | bytes 835592 | tf_op jit(solution)/shard_map/ppermute | solution.py:500
  201.6 16.6 %collective-permute-start.18 = (f32[1536,256]{1,0:T(8,128)S(1)}, f32[1536,256]{1,0:T(8,128)S(1)}, u32[]{:S(2)}, u32[]{:S(2)}) collective-permute-start(f32[1536,256]{1,0:T(8,128)S(1)} %get-tuple-element.147), channel_id=1, source_target_pairs={{0,1},{1,0},{2,3},{3,2},{4,5},{5,4},{6,7},{7,6},{8,9},{9,8},{10,11... | collective-permute-start | bytes 4718600 | tf_op jit(solution)/shard_map/ppermute | solution.py:495
  216.0 12.5 %collective-permute-start.24 = (f32[1536,256]{1,0:T(8,128)S(1)}, f32[1536,256]{1,0:T(8,128)}, u32[]{:S(2)}, u32[]{:S(2)}) collective-permute-start(f32[1536,256]{1,0:T(8,128)S(1)} %add.95.refs_3_), channel_id=1, source_target_pairs={{0,1},{1,0},{2,3},{3,2},{4,5},{5,4},{6,7},{7,6},{8,9},{9,8},{10,11... | collective-permute-start | bytes 4718600 | tf_op jit(solution)/shard_map/ppermute | solution.py:495
  216.5 25.8 %collective-permute-start.30 = (f32[2,128,768]{2,1,0:T(8,128)}, f32[2,128,768]{2,1,0:T(8,128)}, u32[]{:S(2)}, u32[]{:S(2)}) collective-permute-start(f32[2,128,768]{2,1,0:T(8,128)} %get-tuple-element.170), channel_id=1, source_target_pairs={{0,4},{4,0},{8,12},{12,8},{16,20},{20,16},{24,28},{28,24},{1,5},{5... | collective-permute-start | bytes 2359304 | tf_op jit(solution)/shard_map/ppermute | solution.py:500
  217.1 36.3 %collective-permute-start.27 = (f32[1536,256]{1,0:T(8,128)}, f32[1536,256]{1,0:T(8,128)}, u32[]{:S(2)}, u32[]{:S(2)}) collective-permute-start(f32[1536,256]{1,0:T(8,128)} %add.100), channel_id=1, source_target_pairs={{0,2},{1,3},{2,0},{3,1},{4,6},{5,7},{6,4},{7,5},{8,10},{9,11},{10,... | collective-permute-start | bytes 4718600 | tf_op jit(solution)/shard_map/ppermute | solution.py:495
  219.3 24.2 %collective-permute-start.29 = (f32[2,64,768]{2,1,0:T(8,128)}, f32[2,64,768]{2,1,0:T(8,128)}, u32[]{:S(2)}, u32[]{:S(2)}) collective-permute-start(f32[2,64,768]{2,1,0:T(8,128)} %get-tuple-element.174), channel_id=1, source_target_pairs={{0,8},{4,12},{8,0},{12,4},{16,24},{20,28},{24,16},{28,20},{1,9},{5... | collective-permute-start | bytes 1179656 | tf_op jit(solution)/shard_map/ppermute | solution.py:500
  224.3 22.8 %collective-permute-start.36 = (f32[1,128,768]{2,1,0:T(8,128)S(1)}, f32[1,128,768]{2,1,0:T(8,128)S(1)}, u32[]{:S(2)}, u32[]{:S(2)}) collective-permute-start(f32[1,128,768]{2,1,0:T(8,128)S(1)} %copy-done.63), channel_id=1, source_target_pairs={{0,16},{4,20},{8,24},{12,28},{16,0},{20,4},{24,8},{28,12},{1,17},{... | collective-permute-start | bytes 1179656 | tf_op jit(solution)/shard_map/ppermute | solution.py:500
  228.5 16.0 %collective-permute-start.28 = (f32[2,136,128]{2,1,0:T(8,128)S(1)}, f32[2,136,128]{2,1,0:T(8,128)S(1)}, u32[]{:S(2)}, u32[]{:S(2)}) collective-permute-start(f32[2,136,128]{2,1,0:T(8,128)S(1)} %get-tuple-element.176.refs_11_), channel_id=1, source_target_pairs={{0,8},{4,12},{8,0},{12,4},{16,24},{20,28},{24,16},{28,20},{1,9},{5... | collective-permute-start | bytes 417800 | tf_op jit(solution)/shard_map/ppermute | solution.py:500
  247.9 21.6 %collective-permute-start.35 = (f32[1,64,768]{2,1,0:T(8,128)S(1)}, f32[1,64,768]{2,1,0:T(8,128)S(1)}, u32[]{:S(2)}, u32[]{:S(2)}) collective-permute-start(f32[1,64,768]{2,1,0:T(8,128)S(1)} %slice_add_fusion.12), channel_id=1, source_target_pairs={{0,16},{4,20},{8,24},{12,28},{16,0},{20,4},{24,8},{28,12},{1,17},{... | collective-permute-start | bytes 589832 | tf_op jit(solution)/shard_map/ppermute | solution.py:500
  248.4 27.5 %collective-permute-start.34 = (f32[1,128,768]{2,1,0:T(8,128)S(1)}, f32[1,128,768]{2,1,0:T(8,128)S(1)}, u32[]{:S(2)}, u32[]{:S(2)}) collective-permute-start(f32[1,128,768]{2,1,0:T(8,128)S(1)} %slice_add_fusion.7), channel_id=1, source_target_pairs={{0,16},{4,20},{8,24},{12,28},{16,0},{20,4},{24,8},{28,12},{1,17},{... | collective-permute-start | bytes 1179656 | tf_op jit(solution)/shard_map/ppermute | solution.py:500
  (87 other events, 622.3 us)
